TPU v7x, 32 devices: a whole 2x2x4 slice. The times are simulated.
32 devices in a mesh: frames: 8 (over z, y), rep: 4 (over x, core).
Axes of the slice: x: 2, y: 2, z: 4, core: 2. Of those that a mesh axis runs over, the one named last changes fastest.
Arguments:
- frames_in: bfloat16 [192, 7, 7, 512], P(('frames', 'rep'))
- cotangent: bfloat16 [192, 7, 7, 512], P(('frames', 'rep')), may hold values from -6 to 6
- lengths: int32 [33], replicated, may hold values from 1 to 10, as said below
- spatial_weights: float32 [2, 4608, 1152], P(None, 'frames', 'rep'), may hold values from -0.09375 to 0.09375
- spatial_first: float32 [2, 4608, 1152], P(None, 'frames', 'rep')
- spatial_second: float32 [2, 4608, 1152], P(None, 'frames', 'rep'), may hold values from 2352 to 9408
- temporal_weights: float32 [2, 3456, 512], P(None, 'frames', 'rep'), may hold values from -0.109375 to 0.109375
- temporal_first: float32 [2, 3456, 512], P(None, 'frames', 'rep')
- temporal_second: float32 [2, 3456, 512], P(None, 'frames', 'rep'), may hold values from 2352 to 9408
- mid_norm: float32 [2, 2, 1152], replicated
- mid_first: float32 [2, 2, 1152], replicated
- mid_second: float32 [2, 2, 1152], replicated, may hold values from 4704 to 18816
- out_norm: float32 [2, 2, 512], replicated
- out_first: float32 [2, 2, 512], replicated
- out_second: float32 [2, 2, 512], replicated, may hold values from 4704 to 18816
Outputs:
- block_out: bfloat16 [192, 7, 7, 512], P(('frames', 'rep'))
- input_grad: float32 [192, 7, 7, 512], P(('frames', 'rep'))
- spatial_new: float32 [2, 4608, 1152], P(None, 'frames', 'rep')
- spatial_first_new: float32 [2, 4608, 1152], P(None, 'frames', 'rep')
- spatial_second_new: float32 [2, 4608, 1152], P(None, 'frames', 'rep')
- spatial_low: bfloat16 [2, 4608, 1152], P(None, 'frames', 'rep')
- temporal_new: float32 [2, 3456, 512], P(None, 'frames', 'rep')
- temporal_first_new: float32 [2, 3456, 512], P(None, 'frames', 'rep')
- temporal_second_new: float32 [2, 3456, 512], P(None, 'frames', 'rep')
- temporal_low: bfloat16 [2, 3456, 512], P(None, 'frames', 'rep')
- mid_norm_new: float32 [2, 2, 1152], replicated
- mid_first_new: float32 [2, 2, 1152], replicated
- mid_second_new: float32 [2, 2, 1152], replicated
- out_norm_new: float32 [2, 2, 512], replicated
- out_first_new: float32 [2, 2, 512], replicated
- out_second_new: float32 [2, 2, 512], replicated
Inputs may be any that keep to these rules, and one draw needn't show every extreme that they name: `lengths`: the clips cover all 192 frames in order; every device's block of 6 frames holds exactly one clip start besides frame 0, never at the block's first frame.
All inputs are finite; a program needn't handle non-finite values.
Results may differ from a plain program's by a relative error of at most 0.018.
Values may be sent and summed in bfloat16 or wider, within the bound.
No kernel may reach another device: no remote copies, remote signals or barrier semaphores. Data moves between devices by JAX's collectives and lax.ppermute only.
A program may use at most 320 MiB of HBM per device.

v0:
```python
import jax
import jax.numpy as jnp
from jax import lax
from jax.sharding import PartitionSpec as P

HH = 7
WW = 7
STEP = 5


NORM_EPS = 1e-05
ADAM_EPS = 1e-08
BETA_ONE = 0.5
BETA_TWO = 0.5
RATE_WEIGHT = 0.015
RATE_NORM = 0.2
DECAY = 0.05


def extended_2(cells, sides, width):
    for axis, dim in sides:
        count = lax.axis_size(axis)
        ends = count - 1
        head = lax.slice_in_dim(cells, 0, width, axis=dim)
        tail = lax.slice_in_dim(cells, cells.shape[dim] - width, cells.shape[dim], axis=dim)
        cells = jnp.concatenate(
            [
                lax.ppermute(tail, axis, [(i, (i + 1) % count) for i in range(ends)]),
                cells,
                lax.ppermute(head, axis, [((i + 1) % count, i) for i in range(ends)]),
            ],
            axis=dim,
        )
    return cells


def silu_slope(values):
    sigmoid = jax.nn.sigmoid(values)
    return sigmoid * (1.0 + values * (1.0 - sigmoid))


def spatial_patches(act_low):
    padded = jnp.pad(act_low, ((0, 0), (1, 1), (1, 1), (0, 0)))
    pieces = [
        padded[:, row_tap : row_tap + HH, col_tap : col_tap + WW, :]
        for row_tap in range(3)
        for col_tap in range(3)
    ]
    stacked = jnp.concatenate(pieces, axis=-1)
    return stacked.reshape(-1, stacked.shape[-1])


def spatial_adjoint(patch_grad, frame_count, channels):
    grid = patch_grad.reshape(frame_count, HH, WW, 9, channels)
    padded = jnp.zeros((frame_count, HH + 2, WW + 2, channels), jnp.float32)
    for row_tap in range(3):
        for col_tap in range(3):
            padded = padded + jnp.pad(
                grid[:, :, :, 3 * row_tap + col_tap, :],
                ((0, 0), (row_tap, 2 - row_tap), (col_tap, 2 - col_tap), (0, 0)),
            )
    return padded[:, 1 : HH + 1, 1 : WW + 1, :].reshape(-1, channels)


def normalize(values, params, pixel_total):
    center = lax.psum(jnp.sum(values, axis=0), ("frames", "rep")) / pixel_total
    shifted = values - center
    spread = lax.psum(jnp.sum(shifted * shifted, axis=0), ("frames", "rep")) / pixel_total
    inverse = lax.rsqrt(spread + NORM_EPS)
    normed = shifted * inverse
    return (normed * params[0] + params[1], normed, inverse)


def normalize_back(upstream, normed, inverse, params, pixel_total):
    bias_grad, gain_grad = lax.psum(
        (jnp.sum(upstream, axis=0), jnp.sum(upstream * normed, axis=0)), ("frames", "rep")
    )
    values_grad = (
        params[0]
        * inverse
        * (upstream - bias_grad / pixel_total - normed * (gain_grad / pixel_total))
    )
    return (values_grad, jnp.stack([gain_grad, bias_grad]))


def unit_forward(
    act, spatial_w, temporal_w, mid_params, out_params, keep_prev, keep_next, pixel_total
):
    frame_count = keep_prev.shape[0]
    act_low = act.astype(jnp.bfloat16)
    patches = spatial_patches(act_low.reshape(frame_count, HH, WW, -1))
    spatial_out = jnp.dot(patches, spatial_w, preferred_element_type=jnp.float32)
    mid_values, mid_normed, mid_inverse = normalize(spatial_out, mid_params, pixel_total)
    mid_low = jax.nn.silu(mid_values).astype(jnp.bfloat16)
    frames_mid = mid_low.reshape(frame_count, HH * WW, -1)
    extended = extended_2(frames_mid, ((("frames", "rep"), 0),), 1)
    prev_frames = extended[:-2] * keep_prev
    next_frames = extended[2:] * keep_next
    window = jnp.concatenate([prev_frames, frames_mid, next_frames], axis=-1)
    window = window.reshape(-1, window.shape[-1])
    temporal_out = jnp.dot(window, temporal_w, preferred_element_type=jnp.float32)
    out_values, out_normed, out_inverse = normalize(temporal_out, out_params, pixel_total)
    saved = (act_low, mid_values, mid_normed, mid_inverse, window, out_normed, out_inverse)
    return (out_values, saved)


def unit_backward(
    upstream,
    saved,
    spatial_w,
    temporal_w,
    mid_params,
    out_params,
    keep_prev,
    keep_next,
    pixel_total,
):
    act_low, mid_values, mid_normed, mid_inverse, window, out_normed, out_inverse = saved
    frame_count = keep_prev.shape[0]
    channels = act_low.shape[-1]
    middle_width = mid_values.shape[-1]
    temporal_grad, out_param_grad = normalize_back(
        upstream, out_normed, out_inverse, out_params, pixel_total
    )
    temporal_low = temporal_grad.astype(jnp.bfloat16)
    temporal_term = lax.dot_general(
        window, temporal_low, (((0,), (0,)), ((), ())), preferred_element_type=jnp.float32
    )
    frames_grad = temporal_low.reshape(frame_count, HH * WW, -1)
    extended = extended_2(frames_grad, ((("frames", "rep"), 0),), 1)
    later_frames = extended[2:] * keep_next
    earlier_frames = extended[:-2] * keep_prev
    stacked = jnp.stack([later_frames, frames_grad, earlier_frames]).reshape(
        3, -1, frames_grad.shape[-1]
    )
    taps = temporal_w.reshape(3, middle_width, -1)
    middle_grad = jnp.einsum("krd,kmd->rm", stacked, taps, preferred_element_type=jnp.float32)
    middle_grad = middle_grad * silu_slope(mid_values)
    spatial_grad, mid_param_grad = normalize_back(
        middle_grad, mid_normed, mid_inverse, mid_params, pixel_total
    )
    spatial_grad_low = spatial_grad.astype(jnp.bfloat16)
    patches = spatial_patches(act_low.reshape(frame_count, HH, WW, -1))
    spatial_term = lax.dot_general(
        patches, spatial_grad_low, (((0,), (0,)), ((), ())), preferred_element_type=jnp.float32
    )
    patch_grad = lax.dot_general(
        spatial_grad_low, spatial_w, (((1,), (1,)), ((), ())), preferred_element_type=jnp.float32
    )
    act_grad = spatial_adjoint(patch_grad, frame_count, channels)
    return (act_grad, spatial_term, temporal_term, mid_param_grad, out_param_grad)


def block_layout(terms, row_groups, col_groups):
    units, rows, cols = terms.shape
    arranged = terms.reshape(units, row_groups, rows // row_groups, col_groups, cols // col_groups)
    arranged = arranged.transpose(0, 1, 3, 2, 4)
    return arranged.reshape(
        units, row_groups * col_groups * (rows // row_groups), cols // col_groups
    )


def reduce_terms(spatial_terms, temporal_terms):
    row_groups = lax.axis_size("frames")
    col_groups = lax.axis_size("rep")
    spatial_flat = block_layout(spatial_terms, row_groups, col_groups)
    temporal_flat = block_layout(temporal_terms, row_groups, col_groups)
    spatial_part, temporal_part = (
        lax.psum_scatter(spatial_flat, ("frames", "rep"), scatter_dimension=1, tiled=True),
        lax.psum_scatter(temporal_flat, ("frames", "rep"), scatter_dimension=1, tiled=True),
    )
    return (spatial_part, temporal_part)


def adam_step(param, gradient, moment_one, moment_two, rate, decay):
    first_new = BETA_ONE * moment_one + (1.0 - BETA_ONE) * gradient
    second_new = BETA_TWO * moment_two + (1.0 - BETA_TWO) * gradient * gradient
    fix_one = 1.0 - BETA_ONE**STEP
    fix_two = 1.0 - BETA_TWO**STEP
    update = first_new / fix_one / (jnp.sqrt(second_new / fix_two) + ADAM_EPS)
    return (param - rate * (update + decay * param), first_new, second_new)


def on_device(
    frames_in,
    cotangent,
    lengths,
    spatial_weights,
    spatial_first,
    spatial_second,
    temporal_weights,
    temporal_first,
    temporal_second,
    mid_norm,
    mid_first,
    mid_second,
    out_norm,
    out_first,
    out_second,
):
    frame_count = frames_in.shape[0]
    channels = frames_in.shape[-1]
    devices = lax.axis_size(("frames", "rep"))
    pixel_total = frame_count * HH * WW * devices
    unit_count = spatial_weights.shape[0]
    block_count = unit_count // 2
    spatial_local, temporal_local = (
        lax.all_gather(spatial_weights.astype(jnp.bfloat16), "rep", axis=2, tiled=True),
        lax.all_gather(temporal_weights.astype(jnp.bfloat16), "rep", axis=2, tiled=True),
    )
    spatial_all, temporal_all = (
        lax.all_gather(spatial_local, "frames", axis=1, tiled=True),
        lax.all_gather(temporal_local, "frames", axis=1, tiled=True),
    )
    device = lax.axis_index(("frames", "rep"))
    frame_ids = device * frame_count + jnp.arange(frame_count, dtype=jnp.int32)
    clip_ends = jnp.cumsum(lengths)
    starts = jnp.concatenate([jnp.zeros((1,), jnp.int32), clip_ends[:-1]])
    opening = jnp.any(frame_ids[:, None] == starts[None, :], axis=1)
    opening_next = jnp.any((frame_ids + 1)[:, None] == starts[None, :], axis=1)
    keep_prev = jnp.where(opening, 0.0, 1.0).astype(jnp.bfloat16)[:, None, None]
    keep_next = jnp.where(opening_next, 0.0, 1.0).astype(jnp.bfloat16)[:, None, None]
    state = frames_in.astype(jnp.float32).reshape(-1, channels)
    block_id = 0
    first_unit = 2 * block_id
    second_unit = first_unit + 1
    first_out, first_saved = unit_forward(
        state,
        spatial_all[first_unit],
        temporal_all[first_unit],
        mid_norm[first_unit],
        out_norm[first_unit],
        keep_prev,
        keep_next,
        pixel_total,
    )
    second_out, second_saved = unit_forward(
        jax.nn.silu(first_out),
        spatial_all[second_unit],
        temporal_all[second_unit],
        mid_norm[second_unit],
        out_norm[second_unit],
        keep_prev,
        keep_next,
        pixel_total,
    )
    summed = second_out + state
    saved_blocks = [(first_out, summed, first_saved, second_saved)]
    state = jax.nn.silu(summed)
    block_out = state.astype(jnp.bfloat16).reshape(frames_in.shape)
    upstream = cotangent.astype(jnp.float32).reshape(-1, channels)
    block_grads = {}
    for block_id in reversed(range(block_count)):
        first_unit = 2 * block_id
        second_unit = first_unit + 1
        first_out, summed, first_saved, second_saved = saved_blocks[block_id]
        summed_grad = upstream * silu_slope(summed)
        middle_grad, spatial_two, temporal_two, mid_two, out_two = unit_backward(
            summed_grad,
            second_saved,
            spatial_all[second_unit],
            temporal_all[second_unit],
            mid_norm[second_unit],
            out_norm[second_unit],
            keep_prev,
            keep_next,
            pixel_total,
        )
        first_grad = middle_grad * silu_slope(first_out)
        input_part, spatial_one, temporal_one, mid_one, out_one = unit_backward(
            first_grad,
            first_saved,
            spatial_all[first_unit],
            temporal_all[first_unit],
            mid_norm[first_unit],
            out_norm[first_unit],
            keep_prev,
            keep_next,
            pixel_total,
        )
        upstream = input_part + summed_grad
        spatial_part, temporal_part = reduce_terms(
            jnp.stack([spatial_one, spatial_two]), jnp.stack([temporal_one, temporal_two])
        )
        block_grads[block_id] = (
            spatial_part,
            temporal_part,
            jnp.stack([mid_one, mid_two]),
            jnp.stack([out_one, out_two]),
        )
    input_grad = upstream.reshape(frames_in.shape)
    spatial_grad = block_grads[0][0]
    temporal_grad = block_grads[0][1]
    mid_grad = block_grads[0][2]
    out_grad = block_grads[0][3]
    spatial_new, spatial_first_new, spatial_second_new = adam_step(
        spatial_weights, spatial_grad, spatial_first, spatial_second, RATE_WEIGHT, DECAY
    )
    temporal_new, temporal_first_new, temporal_second_new = adam_step(
        temporal_weights, temporal_grad, temporal_first, temporal_second, RATE_WEIGHT, DECAY
    )
    mid_new, mid_first_new, mid_second_new = adam_step(
        mid_norm, mid_grad, mid_first, mid_second, RATE_NORM, 0.0
    )
    out_new, out_first_new, out_second_new = adam_step(
        out_norm, out_grad, out_first, out_second, RATE_NORM, 0.0
    )
    return (
        block_out,
        input_grad,
        spatial_new,
        spatial_first_new,
        spatial_second_new,
        spatial_new.astype(jnp.bfloat16),
        temporal_new,
        temporal_first_new,
        temporal_second_new,
        temporal_new.astype(jnp.bfloat16),
        mid_new,
        mid_first_new,
        mid_second_new,
        out_new,
        out_first_new,
        out_second_new,
    )


def solution(mesh):
    placed = (
        P(("frames", "rep"), None, None, None),
        P(("frames", "rep"), None, None, None),
        P(),
        P(None, "frames", "rep"),
        P(None, "frames", "rep"),
        P(None, "frames", "rep"),
        P(None, "frames", "rep"),
        P(None, "frames", "rep"),
        P(None, "frames", "rep"),
        P(),
        P(),
        P(),
        P(),
        P(),
        P(),
    )
    return jax.shard_map(
        on_device,
        mesh=mesh,
        in_specs=placed,
        out_specs=(
            P(("frames", "rep"), None, None, None),
            P(("frames", "rep"), None, None, None),
            P(None, "frames", "rep"),
            P(None, "frames", "rep"),
            P(None, "frames", "rep"),
            P(None, "frames", "rep"),
            P(None, "frames", "rep"),
            P(None, "frames", "rep"),
            P(None, "frames", "rep"),
            P(None, "frames", "rep"),
            P(),
            P(),
            P(),
            P(),
            P(),
            P(),
        ),
        check_vma=False,
    )
```

profile of v0, /device:TPU:0, one launch (start us, length us, event | category | flops | bytes accessed | tf_op | source)
XLA Modules:
  0.0 1829.4 jit_solution(9534217539355760508)
XLA Ops:
  10.7 30.2 %all-gather.4.cloned.1.call-done = bf16[2,576,1152]{1,0,2:T(2,128)(2,1)} async-done(((bf16[2,576,288]{1,0,2:T(2,128)(2,1)}), bf16[2,576,1152]{1,0,2:T(2,128)(2,1)}) %all-gather.4.cloned.1.call-update) | async-done | bytes 2654224 | tf_op jit(solution)/shard_map/all_gather | solution.py:208
  40.9 10.5 copy.169
  52.4 9.6 all_gather.14
  75.4 382.9 %all-gather.6.cloned.1.call-done = bf16[2,4608,1152]{2,0,1:T(2,128)(2,1)} async-done(((bf16[2,576,1152]{2,0,1:T(2,128)(2,1)}), bf16[2,4608,1152]{2,0,1:T(2,128)(2,1)}) %all-gather.6.cloned.1.call-update) | async-done | bytes 21233680 | tf_op jit(solution)/shard_map/all_gather | solution.py:212
  458.3 40.7 %fusion.60 = (bf16[1,4608,1152]{2,0,1:T(2,128)(2,1)}, bf16[1,4608,1152]{2,0,1:T(2,128)(2,1)}) fusion(bf16[2,4608,1152]{2,0,1:T(2,128)(2,1)} %all-gather.6.cloned.1.call-done), kind=kLoop, calls=%fused_computation.221 | loop fusion | bytes 42467328 | tf_op jit(solution)/shard_map/slice | solution.py:239
  498.9 11.6 copy.203
  518.2 42.8 %psum.112 = f32[1152]{0:T(1024)S(1)} all-reduce(f32[1152]{0:T(1024)S(1)} %get-tuple-element.121), channel_id=1, replica_groups=mesh['frames'=8,'rep'=4] {'frames','rep'}, use_global_device_ids=true, to_apply=%region_1.2 | all-reduce | flops 1152 | bytes 9216 | tf_op jit(solution)/shard_map/psum | solution.py:66
  561.1 40.4 %psum.113 = f32[1152]{0:T(1024)S(1)} all-reduce(f32[1152]{0:T(1024)S(1)} %multiply_reduce_fusion.3), channel_id=1, replica_groups=mesh['frames'=8,'rep'=4] {'frames','rep'}, use_global_device_ids=true, to_apply=%region_3.4 | all-reduce | flops 1152 | bytes 9216 | tf_op jit(solution)/shard_map/psum | solution.py:68
  605.8 15.5 copy.204
  627.7 43.2 %psum.114 = f32[512]{0:T(512)S(1)} all-reduce(f32[512]{0:T(512)S(1)} %get-tuple-element.123), channel_id=1, replica_groups=mesh['frames'=8,'rep'=4] {'frames','rep'}, use_global_device_ids=true, to_apply=%region_8.9 | all-reduce | flops 512 | bytes 4096 | tf_op jit(solution)/shard_map/psum | solution.py:66
  671.0 40.7 %psum.115 = f32[512]{0:T(512)S(1)} all-reduce(f32[512]{0:T(512)S(1)} %multiply_reduce_fusion.7), channel_id=1, replica_groups=mesh['frames'=8,'rep'=4] {'frames','rep'}, use_global_device_ids=true, to_apply=%region_10.11 | all-reduce | flops 512 | bytes 4096 | tf_op jit(solution)/shard_map/psum | solution.py:68
  725.2 39.4 %psum.116 = f32[1152]{0:T(1024)S(1)} all-reduce(f32[1152]{0:T(1024)S(1)} %get-tuple-element.125), channel_id=1, replica_groups=mesh['frames'=8,'rep'=4] {'frames','rep'}, use_global_device_ids=true, to_apply=%region_12.13 | all-reduce | flops 1152 | bytes 9216 | tf_op jit(solution)/shard_map/psum | solution.py:66
  764.8 40.8 %psum.117 = f32[1152]{0:T(1024)S(1)} all-reduce(f32[1152]{0:T(1024)S(1)} %multiply_reduce_fusion.2), channel_id=1, replica_groups=mesh['frames'=8,'rep'=4] {'frames','rep'}, use_global_device_ids=true, to_apply=%region_14.15 | all-reduce | flops 1152 | bytes 9216 | tf_op jit(solution)/shard_map/psum | solution.py:68
  828.0 42.6 %psum.118 = f32[512]{0:T(512)S(1)} all-reduce(f32[512]{0:T(512)S(1)} %get-tuple-element.127), channel_id=1, replica_groups=mesh['frames'=8,'rep'=4] {'frames','rep'}, use_global_device_ids=true, to_apply=%region_16.17 | all-reduce | flops 512 | bytes 4096 | tf_op jit(solution)/shard_map/psum | solution.py:66
  870.7 40.7 %psum.119 = f32[512]{0:T(512)S(1)} all-reduce(f32[512]{0:T(512)S(1)} %multiply_reduce_fusion.6), channel_id=1, replica_groups=mesh['frames'=8,'rep'=4] {'frames','rep'}, use_global_device_ids=true, to_apply=%region_18.19 | all-reduce | flops 512 | bytes 4096 | tf_op jit(solution)/shard_map/psum | solution.py:68
  914.8 39.6 %all-reduce.23 = (f32[512]{0:T(512)S(1)}, f32[512]{0:T(512)S(1)}) all-reduce(f32[512]{0:T(512)} %get-tuple-element.23, f32[512]{0:T(512)} %get-tuple-element.22), channel_id=1, replica_groups=mesh['frames'=8,'rep'=4] {'frames','rep'}, use_global_device_ids=true, to_apply=%region_22.23 | all-reduce | flops 1024 | bytes 8192 | tf_op jit(solution)/shard_map/psum | solution.py:75
  966.8 9.1 stack.106
  982.7 41.0 %all-reduce.22 = (f32[1152]{0:T(1024)S(1)}, f32[1152]{0:T(1024)S(1)}) all-reduce(f32[1152]{0:T(1024)S(1)} %get-tuple-element.19, f32[1152]{0:T(1024)S(1)} %get-tuple-element.18), channel_id=1, replica_groups=mesh['frames'=8,'rep'=4] {'frames','rep'}, use_global_device_ids=true, to_apply=%region_26.27 | all-reduce | flops 2304 | bytes 18432 | tf_op jit(solution)/shard_map/psum | solution.py:75
  1037.0 39.9 %all-reduce.21 = (f32[512]{0:T(512)S(1)}, f32[512]{0:T(512)S(1)}) all-reduce(f32[512]{0:T(512)S(1)} %get-tuple-element.21, f32[512]{0:T(512)S(1)} %get-tuple-element.20), channel_id=1, replica_groups=mesh['frames'=8,'rep'=4] {'frames','rep'}, use_global_device_ids=true, to_apply=%region_30.31 | all-reduce | flops 1024 | bytes 8192 | tf_op jit(solution)/shard_map/psum | solution.py:75
  1083.4 9.2 stack.105
  1092.6 13.8 maximum_bitcast_fusion.1
  1106.4 11.1 copy.192
  1122.2 12.2 fusion.68
  1134.4 26.6 %stack.103 = f32[1,8,576,4,288]{2,1,4,3,0:T(8,128)} reshape(f32[4608,1152]{0,1:T(8,128)} %fusion.68) | data formatting | bytes 42467328 | tf_op jit(solution)/shard_map/stack | solution.py:283
  1166.5 44.5 %all-reduce.20 = (f32[1152]{0:T(1024)S(1)}, f32[1152]{0:T(1024)S(1)}) all-reduce(f32[1152]{0:T(1024)S(1)} %get-tuple-element.17, f32[1152]{0:T(1024)S(1)} %get-tuple-element.16), channel_id=1, replica_groups=mesh['frames'=8,'rep'=4] {'frames','rep'}, use_global_device_ids=true, to_apply=%region_34.35 | all-reduce | flops 2304 | bytes 18432 | tf_op jit(solution)/shard_map/psum | solution.py:75
  1211.3 11.7 fusion.67
  1223.0 25.4 %stack.102 = f32[1,8,576,4,288]{2,1,4,3,0:T(8,128)} reshape(f32[4608,1152]{0,1:T(8,128)} %fusion.67) | data formatting | bytes 42467328 | tf_op jit(solution)/shard_map/stack | solution.py:283
  1248.5 32.7 %maximum_bitcast_fusion = f32[2,8,4,576,288]{3,1,4,2,0:T(8,128)} fusion(f32[1,8,576,4,288]{2,1,4,3,0:T(8,128)} %stack.103, f32[1,8,576,4,288]{2,1,4,3,0:T(8,128)} %stack.102), kind=kLoop, calls=%fused_computation | loop fusion | flops 10616832 | bytes 84934656 | tf_op jit(solution)/shard_map/transpose | solution.py:157
  1281.2 58.5 %copy.201 = f32[2,8,4,576,288]{4,0,3,2,1:T(2,128)} copy(f32[2,8,4,576,288]{3,1,4,2,0:T(8,128)} %maximum_bitcast_fusion) | data formatting | bytes 84934656
  1339.6 63.3 %reshape.237 = f32[18432,576]{1,0:T(8,128)} reshape(f32[18432,2,288]{2,1,0:T(2,128)} %bitcast.175) | data formatting | bytes 84934656
  1405.7 8.6 fusion.27
  1421.0 390.8 %reduce-scatter.7.cloned.1.call-done = f32[576,576]{1,0:T(8,128)} async-done(((f32[18432,576]{1,0:T(8,128)}), f32[576,576]{1,0:T(8,128)}) %reduce-scatter.7.cloned.1.call-update) | async-done | bytes 1327120
  (285 shorter events, 144.5 us)
Async XLA Ops:
  7.2 33.7 %all-gather.4.cloned.1.call-start = ((), (), s32[]{:S(2)}) async-start(), calls=%async_computation.2 | async-start | bytes 3686400 | tf_op jit(solution)/shard_map/all_gather | solution.py:208
  10.6 447.6 %all-gather.6.cloned.1.call-start = ((), (), s32[]{:S(2)}) async-start(), calls=%async_computation.3 | async-start | bytes 23887872 | tf_op jit(solution)/shard_map/all_gather | solution.py:212
  51.4 10.8 copy-start.14
  51.4 572.7 %all-gather.8.cloned.1.call-start = ((), (), s32[]{:S(2)}) async-start(), calls=%async_computation.4 | async-start | bytes 7962624 | tf_op jit(solution)/shard_map/all_gather | solution.py:213
  62.1 1356.5 %reduce-scatter.5.cloned.1.call-start = ((), (), s32[]{:S(2)}) async-start(), calls=%async_computation.5 | async-start | bytes 14598144 | tf_op jit(solution)/shard_map/reduce_scatter | solution.py:170
  65.6 536.5 %copy-start.24 = (f32[1152]{0:T(1024)}, f32[1152]{0:T(1024)S(1)}, u32[]{:S(2)}) copy-start(f32[1152]{0:T(1024)S(1)} %get-tuple-element.26) | copy-start | bytes 13828
  510.6 91.6 %copy-start.30 = (f32[1152]{0:T(1024)S(1)}, f32[1152]{0:T(1024)}, u32[]{:S(2)}) copy-start(f32[1152]{0:T(1024)} %get-tuple-element.25) | copy-start | bytes 13828
  518.2 87.6 %copy-start = (f32[294,1152]{1,0:T(8,128)}, f32[294,1152]{1,0:T(8,128)S(1)}, u32[]{:S(2)}) copy-start(f32[294,1152]{1,0:T(8,128)S(1)} %get-tuple-element.122) | copy-start | bytes 4064260
  518.2 87.3 %copy-start.58 = (pred[6]{0:T(512)(128)(4,1)S(1)}, pred[6]{0:T(512)(128)(4,1)}, u32[]{:S(2)}) copy-start(pred[6]{0:T(512)(128)(4,1)} %get-tuple-element.29) | copy-start | bytes 22
  561.0 44.5 %copy-start.20 = (f32[1152]{0:T(1024)}, f32[1152]{0:T(1024)S(1)}, u32[]{:S(2)}) copy-start(f32[1152]{0:T(1024)S(1)} %broadcast_multiply_fusion.5) | copy-start | bytes 13828
  602.6 21.5 %copy-start.7 = (bf16[294,1152]{1,0:T(8,128)(2,1)}, bf16[294,1152]{1,0:T(8,128)(2,1)S(1)}, u32[]{:S(2)}) copy-start(bf16[294,1152]{1,0:T(8,128)(2,1)S(1)} %multiply_convert_fusion.3) | copy-start | bytes 2032132
  602.7 18.6 %collective-permute-start = (bf16[1,49,1152]{2,1,0:T(8,128)(2,1)S(1)}, bf16[1,49,1152]{2,1,0:T(8,128)(2,1)S(1)}, u32[]{:S(2)}, u32[]{:S(2)}) collective-permute-start(bf16[1,49,1152]{2,1,0:T(8,128)(2,1)S(1)} %get-tuple-element.83), channel_id=1, source_target_pairs={{0,1},{1,2},{2,3},{3,4},{4,5},{5,6},{6,7},{7,8},{8,9},{9,10},{10,1... | collective-permute-start | bytes 338696 | tf_op jit(solution)/shard_map/ppermute | solution.py:28
  604.0 17.3 collective-permute-start.1
  605.5 211.8 %copy-start.45 = (bf16[6]{0:T(256)(128)(2,1)}, bf16[6]{0:T(256)(128)(2,1)S(1)}, u32[]{:S(2)}) copy-start(bf16[6]{0:T(256)(128)(2,1)S(1)} %select_convert_fusion) | copy-start | bytes 40
  605.8 15.6 copy-start.43
  624.1 87.6 %copy-start.28 = (f32[1,1,512]{2,1,0:T(1,128)S(1)}, f32[1,1,512]{2,1,0:T(1,128)}, u32[]{:S(2)}) copy-start(f32[1,1,512]{2,1,0:T(1,128)} %get-tuple-element.113) | copy-start | bytes 6148
  624.1 88.2 %copy-start.29 = (f32[1,1,512]{2,1,0:T(1,128)S(1)}, f32[1,1,512]{2,1,0:T(1,128)}, u32[]{:S(2)}) copy-start(f32[1,1,512]{2,1,0:T(1,128)} %get-tuple-element.115) | copy-start | bytes 6148
  717.7 87.9 %copy-start.32 = (f32[1152]{0:T(1024)S(1)}, f32[1152]{0:T(1024)}, u32[]{:S(2)}) copy-start(f32[1152]{0:T(1024)} %get-tuple-element.27) | copy-start | bytes 13828
  806.0 11.1 copy-start.9
  806.8 10.5 collective-permute-start.2
  808.7 8.5 collective-permute-start.3
  824.0 87.3 %copy-start.40 = (f32[1,1,512]{2,1,0:T(1,128)S(1)}, f32[1,1,512]{2,1,0:T(1,128)}, u32[]{:S(2)}) copy-start(f32[1,1,512]{2,1,0:T(1,128)} %get-tuple-element.114) | copy-start | bytes 6148
  824.0 87.9 %copy-start.11 = (bf16[294,512]{1,0:T(8,128)(2,1)S(1)}, bf16[294,512]{1,0:T(8,128)(2,1)}, u32[]{:S(2)}) copy-start(bf16[294,512]{1,0:T(8,128)(2,1)} %copy-done.10) | copy-start | bytes 903172
  914.8 51.9 %copy-start.5 = (f32[294,512]{1,0:T(8,128)}, f32[294,512]{1,0:T(8,128)S(1)}, u32[]{:S(2)}) copy-start(f32[294,512]{1,0:T(8,128)S(1)} %get-tuple-element.53) | copy-start | bytes 1806340
  955.8 20.1 %collective-permute-start.4 = (bf16[1,49,512]{2,1,0:T(8,128)(2,1)S(1)}, bf16[1,49,512]{2,1,0:T(8,128)(2,1)S(1)}, u32[]{:S(2)}, u32[]{:S(2)}) collective-permute-start(bf16[1,49,512]{2,1,0:T(8,128)(2,1)S(1)} %get-tuple-element.107), channel_id=1, source_target_pairs={{1,0},{2,1},{3,2},{4,3},{5,4},{6,5},{7,6},{8,7},{9,8},{10,9},{11,1... | collective-permute-start | bytes 150536 | tf_op jit(solution)/shard_map/ppermute | solution.py:30
  957.1 18.8 %collective-permute-start.5 = (bf16[1,49,512]{2,1,0:T(8,128)(2,1)S(1)}, bf16[1,49,512]{2,1,0:T(8,128)(2,1)S(1)}, u32[]{:S(2)}, u32[]{:S(2)}) collective-permute-start(bf16[1,49,512]{2,1,0:T(8,128)(2,1)S(1)} %get-tuple-element.108), channel_id=1, source_target_pairs={{0,1},{1,2},{2,3},{3,4},{4,5},{5,6},{6,7},{7,8},{8,9},{9,10},{10,1... | collective-permute-start | bytes 150536 | tf_op jit(solution)/shard_map/ppermute | solution.py:28
  1036.5 40.4 %copy-start.47 = (f32[512]{0:T(512)S(1)}, f32[512]{0:T(512)}, u32[]{:S(2)}) copy-start(f32[512]{0:T(512)} %get-tuple-element.117) | copy-start | bytes 6148
  1036.5 40.6 %copy-start.8 = (bf16[294,1152]{1,0:T(8,128)(2,1)S(1)}, bf16[294,1152]{1,0:T(8,128)(2,1)}, u32[]{:S(2)}) copy-start(bf16[294,1152]{1,0:T(8,128)(2,1)} %copy-done.7) | copy-start | bytes 2032132
  1117.5 694.3 %reduce-scatter.7.cloned.1.call-start = ((), (), s32[]{:S(2)}) async-start(), calls=%async_computation.6 | async-start | bytes 48660480
  1117.6 43.5 %collective-permute-start.6 = (bf16[1,49,512]{2,1,0:T(8,128)(2,1)S(1)}, bf16[1,49,512]{2,1,0:T(8,128)(2,1)S(1)}, u32[]{:S(2)}, u32[]{:S(2)}) collective-permute-start(bf16[1,49,512]{2,1,0:T(8,128)(2,1)S(1)} %get-tuple-element.105), channel_id=1, source_target_pairs={{1,0},{2,1},{3,2},{4,3},{5,4},{6,5},{7,6},{8,7},{9,8},{10,9},{11,1... | collective-permute-start | bytes 150536 | tf_op jit(solution)/shard_map/ppermute | solution.py:30
  1118.9 42.2 %collective-permute-start.7 = (bf16[1,49,512]{2,1,0:T(8,128)(2,1)S(1)}, bf16[1,49,512]{2,1,0:T(8,128)(2,1)S(1)}, u32[]{:S(2)}, u32[]{:S(2)}) collective-permute-start(bf16[1,49,512]{2,1,0:T(8,128)(2,1)S(1)} %get-tuple-element.106), channel_id=1, source_target_pairs={{0,1},{1,2},{2,3},{3,4},{4,5},{5,6},{6,7},{7,8},{8,9},{9,10},{10,1... | collective-permute-start | bytes 150536 | tf_op jit(solution)/shard_map/ppermute | solution.py:28
  1162.6 48.4 %copy-start.33 = (f32[1152]{0:T(1024)S(1)}, f32[1152]{0:T(1024)}, u32[]{:S(2)}) copy-start(f32[1152]{0:T(1024)} %get-tuple-element.109) | copy-start | bytes 13828
  (41 other events, 117.8 us)
Sparse Core Ops, SparseCore 0:
  10.7 30.1 all-gather.3
  51.5 406.6 all-gather.5
  460.5 109.5 all-gather.7
  1117.6 164.7 reduce-scatter.4
  1403.1 408.6 reduce-scatter.6
where the time goes:
time: 1840 us; the launch traced here: 1830 us
  waiting for transfers between devices  804 us (44%)
  blocking collectives  505 us (27%)
  local copies, waits for them, and re-layouts  331 us (18%)
  matrix products  84.9 us (5%)
  other arithmetic  73.3 us (4%)
    unnamed x6, waiting for transfers between devices  391 us
    all_gather x1, waiting for transfers between devices, on_device(): lax.all_gather(spatial_local, 'frames', axis=1, tiled=True)  383 us
    unnamed x142, local copies, waits for them, and re-layouts  169 us
    psum x4, blocking collectives, normalize(): center = lax.psum(jnp.sum(values, axis=0), ('frames', 'rep')) / pixel_total  168 us
    psum x4, blocking collectives, normalize_back(): lax.psum((jnp.sum(upstream, axis=0), jnp.sum(upstream * normed, axis=0)),...  165 us
    psum x4, blocking collectives, normalize(): lax.psum(jnp.sum(shifted * shifted, axis=0), ('frames', 'rep'))  163 us
    another operation x2, local copies, waits for them, and re-layouts, on_device(): jnp.stack([spatial_one, spatial_two])  52.1 us
    transpose x2, other arithmetic, block_layout(): arranged = arranged.transpose(0, 1, 3, 2, 4)  46.5 us
  transfers between devices with their start and end apart: 13, of which 3 were waited for; matrix products, arithmetic and copies ran while one was open for 20% of the time, Pallas kernels for 0%

commit v1 on v0

v1 whole, which is shorter than its diff:
```python
import jax
import jax.numpy as jnp
from jax import lax
from jax.sharding import PartitionSpec as P

STEP = 5
NORM_EPS = 1e-05
ADAM_EPS = 1e-08
BETA_ONE = 0.5
BETA_TWO = 0.5
RATE_WEIGHT = 0.015
RATE_NORM = 0.2
DECAY = 0.05
BF = jnp.bfloat16
F32 = jnp.float32


def silu_slope(values):
    sigmoid = jax.nn.sigmoid(values)
    return sigmoid * (1.0 + values * (1.0 - sigmoid))


def swap(parts, axis):
    return lax.all_to_all(parts, axis, 0, 0, tiled=True)


def from_all(value, axis):
    count = lax.axis_size(axis)
    return swap(jnp.broadcast_to(value[None], (count,) + value.shape), axis)


def neighbours(first, last, axis):
    count = lax.axis_size(axis)
    before = lax.ppermute(last, axis, [(i, i + 1) for i in range(count - 1)])
    after = lax.ppermute(first, axis, [(i + 1, i) for i in range(count - 1)])
    return before, after


def moments(values, axis):
    rows = values.shape[0]
    center = jnp.mean(values, axis=0)
    spread = jnp.sum(jnp.square(values - center), axis=0)
    both = from_all(jnp.stack([center, spread]), axis)
    count = both.shape[0]
    mean = jnp.mean(both[:, 0], axis=0)
    total = jnp.sum(both[:, 1], axis=0) + rows * jnp.sum(jnp.square(both[:, 0] - mean), axis=0)
    return mean, lax.rsqrt(total / (rows * count) + NORM_EPS)


def gradient_sums(upstream, normed, axis):
    both = from_all(jnp.stack([jnp.sum(upstream * normed, axis=0), jnp.sum(upstream, axis=0)]), axis)
    return jnp.sum(both, axis=0)


def patches_of(act):
    height, width, frames, channels = act.shape
    padded = jnp.pad(act, ((1, 1), (1, 1), (0, 0), (0, 0)))
    pieces = [
        padded[i : i + height, j : j + width] for i in range(3) for j in range(3)
    ]
    return jnp.concatenate(pieces, axis=-1).reshape(height * width * frames, 9 * channels)


def adjoint(patch_grad, shape):
    height, width, frames, channels = shape
    grid = patch_grad.reshape(height, width, frames, 9, channels)
    total = jnp.zeros((height + 2, width + 2, frames, channels), F32)
    for i in range(3):
        for j in range(3):
            total = total.at[i : i + height, j : j + width].add(grid[:, :, :, 3 * i + j])
    return total[1 : height + 1, 1 : width + 1]


def split_columns(values, count):
    rows, cols = values.shape
    return values.reshape(rows, count, cols // count).transpose(1, 0, 2)


def sum_over(parts, axis):
    return jnp.sum(swap(parts, axis).astype(F32), axis=0)


def adam_step(param, gradient, moment_one, moment_two, rate, decay):
    first_new = BETA_ONE * moment_one + (1.0 - BETA_ONE) * gradient
    second_new = BETA_TWO * moment_two + (1.0 - BETA_TWO) * gradient * gradient
    fix_one = 1.0 - BETA_ONE**STEP
    fix_two = 1.0 - BETA_TWO**STEP
    update = first_new / fix_one / (jnp.sqrt(second_new / fix_two) + ADAM_EPS)
    return (param - rate * (update + decay * param), first_new, second_new)


def window_of(middle, before, after, keep_prev, keep_next):
    earlier = jnp.concatenate([before[:, None], middle[:, :-1]], axis=1) * keep_prev
    later = jnp.concatenate([middle[:, 1:], after[:, None]], axis=1) * keep_next
    return earlier, later


def mm(a, b, dims):
    return lax.dot_general(a, b, (dims, ((), ())), preferred_element_type=F32)


def on_device(
    frames_in, cotangent, lengths,
    spatial_weights, spatial_first, spatial_second,
    temporal_weights, temporal_first, temporal_second,
    mid_norm, mid_first, mid_second,
    out_norm, out_first, out_second,
):
    own_frames, height, width, depth = frames_in.shape
    n_f, n_r = lax.axis_size("frames"), lax.axis_size("rep")
    me_r = lax.axis_index("rep")
    frames = own_frames * n_r
    pixels = height * width
    rows = pixels * frames
    total = rows * n_f
    mid = spatial_weights.shape[2]
    cols = depth // n_r
    units = spatial_weights.shape[0]

    spatial_low = spatial_weights.astype(BF)
    temporal_low = temporal_weights.astype(BF)
    spatial_w = [lax.all_gather(spatial_low[u], "frames", axis=0, tiled=True) for u in range(units)]
    temporal_w = []
    for u in range(units):
        shard = lax.all_gather(temporal_low[u], "frames", axis=0, tiled=True)
        shard = shard.reshape(3, n_r, mid, cols).transpose(1, 0, 2, 3)
        shard = swap(shard, "rep")
        temporal_w.append(shard.transpose(1, 2, 0, 3).reshape(3, mid, depth))

    frame_ids = lax.axis_index("frames") * frames + jnp.arange(frames, dtype=jnp.int32)
    clip_ends = jnp.cumsum(lengths)
    starts = jnp.concatenate([jnp.zeros((1,), jnp.int32), clip_ends[:-1]])
    opening = jnp.any(frame_ids[:, None] == starts[None, :], axis=1)
    closing = jnp.any((frame_ids + 1)[:, None] == clip_ends[None, :], axis=1)
    keep_prev = jnp.where(opening, 0.0, 1.0).astype(BF)[None, :, None]
    keep_next = jnp.where(closing, 0.0, 1.0).astype(BF)[None, :, None]

    act = lax.all_gather(frames_in, "rep", axis=0, tiled=True).transpose(1, 2, 0, 3)
    state_cols = lax.dynamic_slice_in_dim(act.reshape(rows, depth), me_r * cols, cols, axis=1)
    state_cols = state_cols.astype(F32)
    cot = cotangent.reshape(own_frames, pixels, n_r, cols).transpose(2, 0, 1, 3)
    cot = swap(cot, "rep").reshape(frames, pixels, cols).transpose(1, 0, 2)
    cot = cot.reshape(rows, cols).astype(F32)

    mid_own = lax.dynamic_slice_in_dim(mid_norm, me_r * mid, mid, axis=2)
    out_own = lax.dynamic_slice_in_dim(out_norm, me_r * cols, cols, axis=2)

    saved = []
    out_cols = None
    for u in range(units):
        patches = patches_of(act)
        spatial = mm(patches, spatial_w[u], ((1,), (0,)))
        grid = spatial.reshape(pixels, frames, mid)
        before, after = neighbours(grid[:, 0], grid[:, -1], "frames")
        mean, inverse = moments(spatial, "frames")
        gain, bias = mid_own[u, 0], mid_own[u, 1]

        def activate(v):
            return jax.nn.silu((v - mean) * inverse * gain + bias).astype(BF)

        middle = activate(grid)
        earlier, later = window_of(middle, activate(before), activate(after), keep_prev, keep_next)
        window = jnp.stack([earlier, middle, later]).reshape(3, rows, mid)
        part = sum(mm(window[k], temporal_w[u][k], ((1,), (0,))) for k in range(3))
        temporal = sum_over(split_columns(part.astype(BF), n_r), "rep")
        out_mean, out_inverse = moments(temporal, "frames")
        out_normed = (temporal - out_mean) * out_inverse
        out_cols = out_normed * out_own[u, 0] + out_own[u, 1]
        saved.append((act, spatial, mean, inverse, window, out_normed, out_inverse, out_cols))
        if u + 1 < units:
            low = jax.nn.silu(out_cols).astype(BF)
            low = lax.all_gather(low, "rep", axis=1, tiled=True)
            act = low.reshape(height, width, frames, depth)

    summed = out_cols + state_cols
    block = jax.nn.silu(summed).astype(BF)
    block = block.reshape(pixels, n_r, own_frames, cols).transpose(1, 2, 0, 3)
    block = swap(block, "rep")
    block_out = block.transpose(1, 2, 0, 3).reshape(frames_in.shape)

    summed_grad = cot * silu_slope(summed)
    upstream = summed_grad
    spatial_grads, temporal_grads = [None] * units, [None] * units
    norm_grads = [None] * units
    input_grad = None
    for u in reversed(range(units)):
        act, spatial, mean, inverse, window, out_normed, out_inverse, out_cols = saved[u]
        out_sums = gradient_sums(upstream, out_normed, "frames")
        dt = (
            out_own[u, 0] * out_inverse
            * (upstream - out_sums[1] / total - out_normed * (out_sums[0] / total))
        ).astype(BF)
        dt = lax.all_gather(dt, "rep", axis=1, tiled=True)
        grid = dt.reshape(pixels, frames, depth)
        before, after = neighbours(grid[:, 0], grid[:, -1], "frames")
        earlier, later = window_of(grid, before, after, keep_prev, keep_next)
        d_mid = (
            mm(later.reshape(rows, depth), temporal_w[u][0], ((1,), (1,)))
            + mm(dt, temporal_w[u][1], ((1,), (1,)))
            + mm(earlier.reshape(rows, depth), temporal_w[u][2], ((1,), (1,)))
        )
        t_term = mm(window, dt, ((1,), (0,))).astype(BF)
        t_term = t_term.reshape(3, mid, n_r, cols).transpose(2, 0, 1, 3)
        t_term = swap(t_term, "rep").transpose(1, 0, 2, 3).reshape(n_f, -1, cols)
        temporal_grads[u] = sum_over(t_term, "frames")

        normed = (spatial - mean) * inverse
        gain, bias = mid_own[u, 0], mid_own[u, 1]
        d_mid = d_mid * silu_slope(normed * gain + bias)
        mid_sums = gradient_sums(d_mid, normed, "frames")
        d_spatial = (
            gain * inverse * (d_mid - mid_sums[1] / total - normed * (mid_sums[0] / total))
        ).astype(BF)
        patch_grad = mm(d_spatial, spatial_w[u], ((1,), (1,)))
        d_act = adjoint(patch_grad, act.shape).reshape(rows, depth)
        s_term = mm(patches_of(act), d_spatial, ((0,), (0,))).astype(BF)
        spatial_grads[u] = sum_over(s_term.reshape(n_f, -1, mid), "frames")
        norm_grads[u] = (mid_sums, out_sums)
        if u > 0:
            upstream = sum_over(split_columns(d_act.astype(BF), n_r), "rep")
            upstream = upstream * silu_slope(saved[u - 1][7])
        else:
            mine = jnp.arange(n_r)[:, None, None] == me_r
            parts = split_columns(d_act, n_r) + jnp.where(mine, summed_grad[None], 0.0)
            parts = parts.astype(BF).reshape(n_r, pixels, n_r, own_frames, cols)
            parts = parts.transpose(2, 3, 1, 0, 4).reshape(n_r, own_frames * pixels, depth)
            input_grad = sum_over(parts, "rep").reshape(frames_in.shape)

    flat = jnp.concatenate(
        [jnp.concatenate([m.reshape(-1), o.reshape(-1)]) for m, o in norm_grads]
    )
    flat = from_all(flat, "rep").reshape(n_r, units, -1)
    mid_grad = flat[:, :, : 2 * mid].reshape(n_r, units, 2, mid).transpose(1, 2, 0, 3)
    mid_grad = mid_grad.reshape(units, 2, n_r * mid)
    out_grad = flat[:, :, 2 * mid :].reshape(n_r, units, 2, cols).transpose(1, 2, 0, 3)
    out_grad = out_grad.reshape(units, 2, depth)

    spatial_new, spatial_first_new, spatial_second_new = adam_step(
        spatial_weights, jnp.stack(spatial_grads), spatial_first, spatial_second, RATE_WEIGHT, DECAY
    )
    temporal_new, temporal_first_new, temporal_second_new = adam_step(
        temporal_weights, jnp.stack(temporal_grads), temporal_first, temporal_second, RATE_WEIGHT, DECAY
    )
    mid_new, mid_first_new, mid_second_new = adam_step(
        mid_norm, mid_grad, mid_first, mid_second, RATE_NORM, 0.0
    )
    out_new, out_first_new, out_second_new = adam_step(
        out_norm, out_grad, out_first, out_second, RATE_NORM, 0.0
    )
    return (
        block_out, input_grad,
        spatial_new, spatial_first_new, spatial_second_new, spatial_new.astype(BF),
        temporal_new, temporal_first_new, temporal_second_new, temporal_new.astype(BF),
        mid_new, mid_first_new, mid_second_new,
        out_new, out_first_new, out_second_new,
    )


def solution(mesh):
    by_frame = P(("frames", "rep"), None, None, None)
    by_block = P(None, "frames", "rep")
    placed = (by_frame, by_frame, P()) + (by_block,) * 6 + (P(),) * 6
    return jax.shard_map(
        on_device,
        mesh=mesh,
        in_specs=placed,
        out_specs=(by_frame, by_frame) + (by_block,) * 8 + (P(),) * 6,
        check_vma=False,
    )
```

time: 1840 us -> 1080 us (0.59)
  waiting for transfers between devices: 804 us -> 283 us
  blocking collectives: 505 us -> 98.4 us
  starting transfers between devices: 15.5 us -> 116 us
  other arithmetic: 73.3 us -> 122 us
  local copies, waits for them, and re-layouts: 331 us -> 359 us
    psum x12 -> x0, blocking collectives: 496 us -> none  [the longest x4 168 us: normalize(): center = lax.psum(jnp.sum(values, axis=0), ('frames', 'rep')) / pixel_total]
    unnamed x6, waiting for transfers between devices: 391 us -> 1.43 us
    all_gather x3 -> x6, waiting for transfers between devices: 413 us -> 73.7 us  [the longest x2 61.3 us: on_device(): lax.all_gather(spatial_low[u], 'frames', axis=0, tiled=True)]
    all_to_all x0 -> x21, waiting for transfers between devices: none -> 207 us  [swap(): return lax.all_to_all(parts, axis, 0, 0, tiled=True)]
    unnamed x142 -> x233, local copies, waits for them, and re-layouts: 169 us -> 35.3 us
    slice x10 -> x26, local copies, waits for them, and re-layouts: 50.8 us -> 153 us  [the longest x2 124 us: adjoint(): total = total.at[i:i + height, j:j + width].add(grid[:, :, :, 3 * i + j])]
    all_to_all x0 -> x21, starting transfers between devices: none -> 92.5 us  [swap(): return lax.all_to_all(parts, axis, 0, 0, tiled=True)]
    reshape x11 -> x22, local copies, waits for them, and re-layouts: 4.64 us -> 85.2 us  [the longest x2 53.9 us: adjoint(): grid = patch_grad.reshape(height, width, frames, 9, channels)]
  transfers between devices with their start and end apart: 13 -> 35, of which waited for: 3 -> 19; matrix products, arithmetic and copies ran while one was open for 20% -> 33% of each run, Pallas kernels for 0% -> 0%
where the time goes in v1:
time: 1080 us; the launch traced here: 1070 us
  local copies, waits for them, and re-layouts  359 us (33%)
  waiting for transfers between devices  283 us (26%)
  other arithmetic  122 us (11%)
  starting transfers between devices  116 us (11%)
  blocking collectives  98.4 us (9%)
  matrix products  74 us (7%)
  between operations  16.3 us (2%)
    all_to_all x21, waiting for transfers between devices, swap(): return lax.all_to_all(parts, axis, 0, 0, tiled=True)  207 us
    slice x2, local copies, waits for them, and re-layouts, adjoint(): total = total.at[i:i + height, j:j + width].add(grid[:, :, :, 3 * i + j])  124 us
    all_to_all x21, starting transfers between devices, swap(): return lax.all_to_all(parts, axis, 0, 0, tiled=True)  92.5 us
    dot_general x20, matrix products, mm(): return lax.dot_general(a, b, (dims, ((), ())), preferred_element_type=F32)  74 us
    all_gather x2, blocking collectives, on_device(): shard = lax.all_gather(temporal_low[u], 'frames', axis=0, tiled=True)  69.8 us
    all_gather x2, waiting for transfers between devices, on_device(): lax.all_gather(spatial_low[u], 'frames', axis=0, tiled=True)  61.3 us
    reshape x2, local copies, waits for them, and re-layouts, adjoint(): grid = patch_grad.reshape(height, width, frames, 9, channels)  53.9 us
    scatter-add x16, other arithmetic, adjoint(): total = total.at[i:i + height, j:j + width].add(grid[:, :, :, 3 * i + j])  44.1 us
  transfers between devices with their start and end apart: 35, of which 19 were waited for; matrix products, arithmetic and copies ran while one was open for 33% of the time, Pallas kernels for 0%

profile of v1, /device:TPU:0, one launch (start us, length us, event | category | flops | bytes accessed | tf_op | source)
XLA Modules:
  0.0 1068.9 jit_solution(16798491612497316000)
XLA Ops:
  14.0 34.5 %all-gather.1 = bf16[1,3456,128]{2,1,0:T(8,128)(2,1)S(1)} all-gather(bf16[1,432,128]{2,1,0:T(8,128)(2,1)S(1)} %get-tuple-element.342), channel_id=3, replica_groups=mesh['frames'=8,'rep'=4] {'frames'}, dimensions={1}, use_global_device_ids=true | all-gather | bytes 995328 | tf_op jit(solution)/shard_map/all_gather | solution.py:125
  56.1 9.6 all-to-all-done.1
  81.9 61.3 %all-gather.19.cloned.1.call-done = bf16[1,4608,288]{2,0,1:T(2,128)(2,1)} async-done(((bf16[1,576,288]{2,0,1:T(2,128)(2,1)}), bf16[1,4608,288]{2,0,1:T(2,128)(2,1)}) %all-gather.19.cloned.1.call-update) | async-done | bytes 2654224 | tf_op jit(solution)/shard_map/all_gather | solution.py:122
  143.2 15.8 %copy.358 = bf16[1,4608,288]{1,2,0:T(8,128)(2,1)} copy(bf16[1,4608,288]{2,0,1:T(2,128)(2,1)} %all-gather.19.cloned.1.call-done) | data formatting | bytes 5308416 | tf_op jit(solution)/shard_map/all_gather | solution.py:122
  158.9 8.6 fusion.149
  194.7 16.1 %all-to-all-done.2 = bf16[4,1176,128]{2,1,0:T(8,128)(2,1)S(1)} async-done(((bf16[4,1176,128]{2,1,0:T(8,128)(2,1)}), bf16[4,1176,128]{2,1,0:T(8,128)(2,1)S(1)}, u32[]{:S(2)}, u32[]{:S(2)}) %all-to-all-start.2) | async-done | bytes 1204256 | tf_op jit(solution)/shard_map/all_to_all | solution.py:24
  212.4 7.0 all-to-all-start.3
  228.3 35.3 %all-gather.3 = bf16[1,3456,128]{2,1,0:T(8,128)(2,1)S(1)} all-gather(bf16[1,432,128]{2,1,0:T(8,128)(2,1)S(1)} %copy-done.46), channel_id=5, replica_groups=mesh['frames'=8,'rep'=4] {'frames'}, dimensions={1}, use_global_device_ids=true | all-gather | bytes 995328 | tf_op jit(solution)/shard_map/all_gather | solution.py:125
  263.7 19.2 %all_to_all.116 = bf16[4,3,288,128]{3,2,1,0:T(8,128)(2,1)S(1)} all-to-all(bf16[4,3,288,128]{3,2,1,0:T(8,128)(2,1)S(1)} %copy.379), channel_id=1, replica_groups=mesh['frames'=8,'rep'=4] {'rep'}, dimensions={0} | all-to-all | bytes 1769472 | tf_op jit(solution)/shard_map/all_to_all | solution.py:24
  285.6 15.7 %copy.373 = bf16[1,4608,288]{1,2,0:T(8,128)(2,1)} copy(bf16[1,4608,288]{2,0,1:T(2,128)(2,1)} %all-gather.21.cloned.1.call-done) | data formatting | bytes 5308416 | tf_op jit(solution)/shard_map/all_gather | solution.py:122
  352.8 12.6 %all-to-all-done.6 = bf16[4,1176,128]{2,1,0:T(8,128)(2,1)} async-done(((bf16[4,1176,128]{2,1,0:T(8,128)(2,1)}), bf16[4,1176,128]{2,1,0:T(8,128)(2,1)}, u32[]{:S(2)}, u32[]{:S(2)}) %all-to-all-start.6) | async-done | bytes 1204256 | tf_op jit(solution)/shard_map/all_to_all | solution.py:24
  377.7 6.7 all-to-all-start.7
  400.1 9.4 all_to_all.117
  415.7 12.4 %all-gather.15.cloned.1.call-done = bf16[1176,512]{1,0:T(8,128)(2,1)} async-done(((bf16[1176,128]{1,0:T(8,128)(2,1)}), bf16[1176,512]{1,0:T(8,128)(2,1)}) %all-gather.15.cloned.1.call-update) | async-done | bytes 1204240 | tf_op jit(solution)/shard_map/all_gather | solution.py:193
  444.4 6.3 all-to-all-start.11
  451.3 6.1 all-to-all-done.11
  460.2 12.7 %fusion.4 = f32[1176,4608]{1,0:T(8,128)} fusion(bf16[1,4608,288]{1,2,0:T(8,128)(2,1)} %copy.373, f32[1176,288]{0,1:T(8,128)} %get-tuple-element.375, f32[1176,288]{0,1:T(8,128)S(1)} %get-tuple-element.374, f32[288]{0:T(512)S(1)} %get-tuple-element.255, f32[288]{0:T(512)S(1)} %get-tuple-element.254, f32[288]{0:T(512)} %get-tuple-element.276, ...), kind=kOutput, calls=%fused_computation.38 | convolution fusion | flops 3123719424 | bytes 27045504 | tf_op jit(solution)/shard_map/dot_general | solution.py:99
  472.8 27.0 %reshape.1642 = f32[7,7,24,9,512]{4,3,2,1,0:T(8,128)} reshape(f32[1176,4608]{1,0:T(8,128)} %fusion.4) | data formatting | bytes 43352064 | tf_op jit(solution)/shard_map/reshape | solution.py:66
  499.8 62.2 %fusion.134 = (f32[7,7,24,1,512]{4,3,2,1,0:T(1,128)}, f32[7,7,24,1,512]{4,3,2,1,0:T(1,128)}, f32[7,7,24,1,512]{4,3,2,1,0:T(1,128)}, f32[7,7,24,1,512]{4,3,2,1,0:...) fusion(f32[7,7,24,9,512]{4,3,2,1,0:T(8,128)} %reshape.1642), kind=kLoop, calls=%fused_computation.339 | loop fusion | bytes 43352064 | tf_op jit(solution)/shard_map/slice | solution.py:70
  600.3 6.6 all-to-all-done.12
  643.7 8.7 all-to-all-done.20
  685.7 12.6 %fusion.8 = f32[1176,4608]{1,0:T(8,128)} fusion(bf16[1,4608,288]{1,2,0:T(8,128)(2,1)} %copy.358, f32[1176,288]{0,1:T(8,128)} %get-tuple-element.376, f32[1176,288]{0,1:T(8,128)S(1)} %get-tuple-element.372, f32[288]{0:T(512)S(1)} %get-tuple-element.253, f32[288]{0:T(512)S(1)} %get-tuple-element.252, f32[288]{0:T(512)S(1)} %copy-done.59, ...), kind=kOutput, calls=%fused_computation.42 | convolution fusion | flops 3123719424 | bytes 27045504 | tf_op jit(solution)/shard_map/dot_general | solution.py:99
  698.3 27.0 %reshape.1656 = f32[7,7,24,9,512]{4,3,2,1,0:T(8,128)} reshape(f32[1176,4608]{1,0:T(8,128)} %fusion.8) | data formatting | bytes 43352064 | tf_op jit(solution)/shard_map/reshape | solution.py:66
  725.3 62.2 %fusion.133 = (f32[7,7,24,1,512]{4,3,2,1,0:T(1,128)}, f32[7,7,24,1,512]{4,3,2,1,0:T(1,128)}, f32[7,7,24,1,512]{4,3,2,1,0:T(1,128)}, f32[7,7,24,1,512]{4,3,2,1,0:...) fusion(f32[7,7,24,9,512]{4,3,2,1,0:T(8,128)} %reshape.1656), kind=kLoop, calls=%fused_computation.338 | loop fusion | bytes 43352064 | tf_op jit(solution)/shard_map/slice | solution.py:70
  796.7 6.2 fusion.13
  822.9 7.4 all-to-all-done.21
  866.6 9.8 convolution_convert_fusion
  876.4 5.9 reshape.1669
  892.9 65.1 %all-to-all-done.17 = bf16[8,576,288]{1,2,0:T(8,128)(2,1)} async-done(((bf16[8,576,288]{1,2,0:T(8,128)(2,1)}), bf16[8,576,288]{1,2,0:T(8,128)(2,1)}, u32[]{:S(2)}, u32[]{:S(2)}) %all-to-all-start.17) | async-done | bytes 2654240 | tf_op jit(solution)/shard_map/all_to_all | solution.py:24
  962.5 9.3 convolution_convert_fusion.1
  978.5 6.3 all-to-all-done.19
  1003.5 51.5 %all-to-all-done.16 = bf16[8,576,288]{1,2,0:T(8,128)(2,1)S(1)} async-done(((bf16[8,576,288]{1,2,0:T(8,128)(2,1)}), bf16[8,576,288]{1,2,0:T(8,128)(2,1)S(1)}, u32[]{:S(2)}, u32[]{:S(2)}) %all-to-all-start.16) | async-done | bytes 2654240 | tf_op jit(solution)/shard_map/all_to_all | solution.py:24
  (519 shorter events, 395.8 us)
Async XLA Ops:
  7.2 61.2 %all-gather.11.cloned.1.call-start = ((), (), s32[]{:S(2)}) async-start(), calls=%async_computation.23 | async-start | bytes 1720320 | tf_op jit(solution)/shard_map/all_gather | solution.py:138
  7.9 135.2 %all-gather.19.cloned.1.call-start = ((), (), s32[]{:S(2)}) async-start(), calls=%async_computation.27 | async-start | bytes 7962624 | tf_op jit(solution)/shard_map/all_gather | solution.py:122
  49.5 16.2 %all-to-all-start.1 = ((bf16[4,3,288,128]{3,2,1,0:T(8,128)(2,1)}), bf16[4,3,288,128]{3,2,1,0:T(8,128)(2,1)S(1)}, u32[]{:S(2)}, u32[]{:S(2)}) async-start(bf16[4,3,288,128]{3,2,1,0:T(8,128)(2,1)} %copy.365), calls=%async_computation.1 | async-start | bytes 1769472 | tf_op jit(solution)/shard_map/all_to_all | solution.py:24
  53.0 232.6 %all-gather.21.cloned.1.call-start = ((), (), s32[]{:S(2)}) async-start(), calls=%async_computation.28 | async-start | bytes 7962624 | tf_op jit(solution)/shard_map/all_gather | solution.py:122
  169.5 10.3 all-to-all-start
  173.7 9.0 collective-permute-start
  191.1 19.7 %all-to-all-start.2 = ((bf16[4,1176,128]{2,1,0:T(8,128)(2,1)}), bf16[4,1176,128]{2,1,0:T(8,128)(2,1)S(1)}, u32[]{:S(2)}, u32[]{:S(2)}) async-start(bf16[4,1176,128]{2,1,0:T(8,128)(2,1)} %bitcast.398), calls=%async_computation.2 | async-start | bytes 2408448 | tf_op jit(solution)/shard_map/all_to_all | solution.py:24
  212.4 13.6 %all-to-all-start.3 = ((f32[8,2,128]{2,1,0:T(2,128)}), f32[8,2,128]{2,1,0:T(2,128)S(1)}, u32[]{:S(2)}, u32[]{:S(2)}) async-start(f32[8,2,128]{2,1,0:T(2,128)} %broadcast_in_dim.52), calls=%async_computation.3 | async-start | bytes 16384 | tf_op jit(solution)/shard_map/all_to_all | solution.py:24
  219.4 82.0 %all-gather.13.cloned.1.call-start = ((), (), s32[]{:S(2)}) async-start(), calls=%async_computation.24 | async-start | bytes 1505280 | tf_op jit(solution)/shard_map/all_gather | solution.py:172
  318.2 12.7 %all-to-all-start.4 = ((f32[8,2,288]{2,1,0:T(2,128)}), f32[8,2,288]{2,1,0:T(2,128)}, u32[]{:S(2)}, u32[]{:S(2)}) async-start(f32[8,2,288]{2,1,0:T(2,128)} %broadcast_in_dim.53), calls=%async_computation.4 | async-start | bytes 49152 | tf_op jit(solution)/shard_map/all_to_all | solution.py:24
  324.8 12.7 %collective-permute-start.2 = (f32[49,288]{1,0:T(8,128)}, f32[49,288]{1,0:T(8,128)}, u32[]{:S(2)}, u32[]{:S(2)}) collective-permute-start(f32[49,288]{1,0:T(8,128)} %bitcast.370), channel_id=1, source_target_pairs={{0,4},{4,8},{8,12},{12,16},{16,20},{20,24},{24,28},{1,5},{5,9},{9,... | collective-permute-start | bytes 169352 | tf_op jit(solution)/shard_map/ppermute | solution.py:34
  329.7 7.9 collective-permute-start.3
  344.9 20.5 %all-to-all-start.6 = ((bf16[4,1176,128]{2,1,0:T(8,128)(2,1)}), bf16[4,1176,128]{2,1,0:T(8,128)(2,1)}, u32[]{:S(2)}, u32[]{:S(2)}) async-start(bf16[4,1176,128]{2,1,0:T(8,128)(2,1)} %bitcast.399), calls=%async_computation.6 | async-start | bytes 2408448 | tf_op jit(solution)/shard_map/all_to_all | solution.py:24
  365.4 11.1 %all-to-all-start.9 = ((bf16[4,6,49,128]{3,2,1,0:T(8,128)(2,1)}), bf16[4,6,49,128]{3,2,1,0:T(8,128)(2,1)}, u32[]{:S(2)}, u32[]{:S(2)}) async-start(bf16[4,6,49,128]{3,2,1,0:T(8,128)(2,1)} %bitcast.435), calls=%async_computation.9 | async-start | bytes 688128 | tf_op jit(solution)/shard_map/all_to_all | solution.py:24
  377.7 13.3 %all-to-all-start.7 = ((f32[8,2,128]{2,1,0:T(2,128)}), f32[8,2,128]{2,1,0:T(2,128)}, u32[]{:S(2)}, u32[]{:S(2)}) async-start(f32[8,2,128]{2,1,0:T(2,128)} %broadcast_in_dim.54), calls=%async_computation.7 | async-start | bytes 16384 | tf_op jit(solution)/shard_map/all_to_all | solution.py:24
  384.4 43.7 %all-gather.15.cloned.1.call-start = ((), (), s32[]{:S(2)}) async-start(), calls=%async_computation.25 | async-start | bytes 1505280 | tf_op jit(solution)/shard_map/all_gather | solution.py:193
  429.4 8.3 collective-permute-start.4
  444.4 13.1 %all-to-all-start.11 = ((f32[8,2,288]{2,1,0:T(2,128)}), f32[8,2,288]{2,1,0:T(2,128)}, u32[]{:S(2)}, u32[]{:S(2)}) async-start(f32[8,2,288]{2,1,0:T(2,128)} %broadcast_in_dim.58), calls=%async_computation.11 | async-start | bytes 49152 | tf_op jit(solution)/shard_map/all_to_all | solution.py:24
  586.4 20.5 %all-to-all-start.12 = ((bf16[4,1176,128]{2,1,0:T(8,128)(2,1)}), bf16[4,1176,128]{2,1,0:T(8,128)(2,1)}, u32[]{:S(2)}, u32[]{:S(2)}) async-start(bf16[4,1176,128]{2,1,0:T(8,128)(2,1)} %bitcast.397), calls=%async_computation.12 | async-start | bytes 2408448 | tf_op jit(solution)/shard_map/all_to_all | solution.py:24
  610.9 10.4 all-to-all-start.13
  614.8 39.8 %all-gather.17.cloned.1.call-start = ((), (), s32[]{:S(2)}) async-start(), calls=%async_computation.26 | async-start | bytes 1505280 | tf_op jit(solution)/shard_map/all_gather | solution.py:193
  635.0 17.4 %all-to-all-start.20 = ((bf16[4,3,288,128]{3,2,1,0:T(8,128)(2,1)}), bf16[4,3,288,128]{3,2,1,0:T(8,128)(2,1)}, u32[]{:S(2)}, u32[]{:S(2)}) async-start(bf16[4,3,288,128]{3,2,1,0:T(8,128)(2,1)} %bitcast.422), calls=%async_computation.20 | async-start | bytes 1769472 | tf_op jit(solution)/shard_map/all_to_all | solution.py:24
  655.9 8.2 collective-permute-start.6
  670.7 11.2 %all-to-all-start.14 = ((f32[8,2,288]{2,1,0:T(2,128)}), f32[8,2,288]{2,1,0:T(2,128)S(1)}, u32[]{:S(2)}, u32[]{:S(2)}) async-start(f32[8,2,288]{2,1,0:T(2,128)} %broadcast_in_dim.62), calls=%async_computation.14 | async-start | bytes 49152 | tf_op jit(solution)/shard_map/all_to_all | solution.py:24
  681.9 121.0 %all-to-all-start.8 = ((bf16[4,6,49,128]{3,2,1,0:T(8,128)(2,1)}), bf16[4,6,49,128]{3,2,1,0:T(8,128)(2,1)S(1)}, u32[]{:S(2)}, u32[]{:S(2)}) async-start(bf16[4,6,49,128]{3,2,1,0:T(8,128)(2,1)} %copy.388), calls=%async_computation.8 | async-start | bytes 688128 | tf_op jit(solution)/shard_map/all_to_all | solution.py:24
  802.9 27.4 %all-to-all-start.21 = ((bf16[8,432,128]{2,1,0:T(8,128)(2,1)}), bf16[8,432,128]{2,1,0:T(8,128)(2,1)}, u32[]{:S(2)}, u32[]{:S(2)}) async-start(bf16[8,432,128]{2,1,0:T(8,128)(2,1)} %bitcast.419), calls=%async_computation.21 | async-start | bytes 1769472 | tf_op jit(solution)/shard_map/all_to_all | solution.py:24
  830.9 7.9 all-to-all-start.22
  838.8 23.5 %all-to-all-start.18 = ((bf16[4,3,288,128]{3,2,1,0:T(8,128)(2,1)}), bf16[4,3,288,128]{3,2,1,0:T(8,128)(2,1)}, u32[]{:S(2)}, u32[]{:S(2)}) async-start(bf16[4,3,288,128]{3,2,1,0:T(8,128)(2,1)} %bitcast.420), calls=%async_computation.18 | async-start | bytes 1769472 | tf_op jit(solution)/shard_map/all_to_all | solution.py:24
  862.2 23.9 %all-to-all-start.15 = ((bf16[4,294,512]{2,1,0:T(8,128)(2,1)}), bf16[4,294,512]{2,1,0:T(8,128)(2,1)}, u32[]{:S(2)}, u32[]{:S(2)}) async-start(bf16[4,294,512]{2,1,0:T(8,128)(2,1)} %reshape.1666), calls=%async_computation.15 | async-start | bytes 2424832 | tf_op jit(solution)/shard_map/all_to_all | solution.py:24
  886.1 71.8 %all-to-all-start.17 = ((bf16[8,576,288]{1,2,0:T(8,128)(2,1)}), bf16[8,576,288]{1,2,0:T(8,128)(2,1)}, u32[]{:S(2)}, u32[]{:S(2)}) async-start(bf16[8,576,288]{1,2,0:T(8,128)(2,1)} %copy.424), calls=%async_computation.17 | async-start | bytes 5898240 | tf_op jit(solution)/shard_map/all_to_all | solution.py:24
  958.0 26.8 %all-to-all-start.19 = ((bf16[8,432,128]{2,1,0:T(8,128)(2,1)}), bf16[8,432,128]{2,1,0:T(8,128)(2,1)}, u32[]{:S(2)}, u32[]{:S(2)}) async-start(bf16[8,432,128]{2,1,0:T(8,128)(2,1)} %bitcast.115), calls=%async_computation.19 | async-start | bytes 1769472 | tf_op jit(solution)/shard_map/all_to_all | solution.py:24
  984.8 70.3 %all-to-all-start.16 = ((bf16[8,576,288]{1,2,0:T(8,128)(2,1)}), bf16[8,576,288]{1,2,0:T(8,128)(2,1)S(1)}, u32[]{:S(2)}, u32[]{:S(2)}) async-start(bf16[8,576,288]{1,2,0:T(8,128)(2,1)} %copy.423), calls=%async_computation.16 | async-start | bytes 5898240 | tf_op jit(solution)/shard_map/all_to_all | solution.py:24
  (106 other events, 1389.9 us)
Sparse Core Ops, SparseCore 0:
  9.6 21.2 all-gather.10
  33.6 109.4 all-gather.18
  145.9 118.1 all-gather.20
  266.1 20.7 all-gather.12
  413.8 14.2 all-gather.14
  625.4 15.9 all-gather.16

commit v2 on v1

v2 whole, which is shorter than its diff:
```python
import functools

import jax
import jax.numpy as jnp
from jax import lax
from jax.experimental import pallas as pl
from jax.experimental.pallas import tpu as pltpu
from jax.sharding import PartitionSpec as P

STEP = 5
NORM_EPS = 1e-05
ADAM_EPS = 1e-08
BETA_ONE = 0.5
BETA_TWO = 0.5
RATE_WEIGHT = 0.015
RATE_NORM = 0.2
DECAY = 0.05
BF = jnp.bfloat16
F32 = jnp.float32
MIB = 1 << 20
VMEM = pl.BlockSpec(memory_space=pltpu.VMEM)
SMEM = pl.BlockSpec(memory_space=pltpu.SMEM)
LANES = 128


def shape(dims, dtype):
    return jax.ShapeDtypeStruct(tuple(dims), dtype)


def run(body, outs, args, name, scratch=(), limit=40, scalars=0, flops=0, moved=0):
    return pl.pallas_call(
        body,
        out_shape=tuple(outs),
        in_specs=[SMEM] * scalars + [VMEM] * (len(args) - scalars),
        out_specs=tuple(VMEM for _ in outs),
        scratch_shapes=list(scratch),
        compiler_params=pltpu.CompilerParams(vmem_limit_bytes=limit * MIB),
        cost_estimate=pl.CostEstimate(flops=flops, bytes_accessed=moved, transcendentals=0),
        name=name,
    )(*args)


def sigmoid(v):
    return 1.0 / (1.0 + jnp.exp(-v))


def silu(v):
    return v / (1.0 + jnp.exp(-v))


def silu_slope(v):
    s = sigmoid(v)
    return s * (1.0 + v * (1.0 - s))


def mm(a, b, dims):
    return lax.dot_general(a, b, (dims, ((), ())), preferred_element_type=F32)


def put_moments(values, out_ref):
    rows = values.shape[0]
    mean = jnp.sum(values, axis=0, keepdims=True) * (1.0 / rows)
    off = values - mean
    out_ref[0:1, :] = mean
    out_ref[1:2, :] = jnp.sum(off * off, axis=0, keepdims=True)


def joined_moments(both, rows):
    count = both.shape[0]
    mean = jnp.sum(both[:, 0:1], axis=0) * (1.0 / count)
    off = both[:, 0:1] - mean[None]
    total = jnp.sum(both[:, 1:2] + rows * (off * off), axis=0)
    return mean, lax.rsqrt(total * (1.0 / (rows * count)) + NORM_EPS)


def put_sums(upstream, normed, out_ref):
    out_ref[0:1, :] = jnp.sum(upstream * normed, axis=0, keepdims=True)
    out_ref[1:2, :] = jnp.sum(upstream, axis=0, keepdims=True)


def convolve(pad, w_ref, acc_ref, dims):
    height, width, frames, depth = dims
    rows = height * width * frames

    def tap(k, carry):
        piece = pad[pl.ds(k // 3, height), pl.ds(k % 3, width)]
        piece = piece.reshape(rows, depth).astype(BF)
        w = w_ref[:, pl.ds(pl.multiple_of(k * depth, LANES), depth)]
        part = mm(piece, w, ((1,), (1,)))

        @pl.when(k == 0)
        def _():
            acc_ref[...] = part

        @pl.when(k > 0)
        def _():
            acc_ref[...] += part

        return carry

    lax.fori_loop(0, 9, tap, 0)


def widened(scr, values, before, after):
    frames = values.shape[1]
    scr[:, 8 : 8 + frames, :] = values
    scr[:, 7:8, :] = before
    scr[:, 8 + frames : 9 + frames, :] = after


def dense_wire(mid, k, count):
    return mid % 32 == 0 and (2 * k) % LANES == 0 and k % LANES == LANES // 2 and count % 2 == 0


def low_half(shape_):
    return lax.broadcasted_iota(jnp.int32, shape_, 1) < LANES // 2


def fold(top, bottom, out_ref, k):
    edge = k - LANES // 2
    out_ref[:, 0:edge] = top[:, 0:edge].astype(out_ref.dtype)
    mixed = jnp.where(low_half((top.shape[0], LANES)), top[:, edge : edge + LANES], bottom[:, 0:LANES])
    out_ref[:, edge : edge + LANES] = mixed.astype(out_ref.dtype)
    out_ref[:, edge + LANES : 2 * k] = bottom[:, LANES : k + LANES // 2].astype(out_ref.dtype)


def pack_body(w_ref, out_ref, scr):
    units, mid, k = w_ref.shape
    half, wide = mid // 2, k + LANES // 2
    for u in range(units):
        scr[:, 0:k] = w_ref[u]
        fold(scr[0:half, :], pltpu.roll(scr[half:mid, :], LANES // 2, 1), out_ref.at[u], k)


def unpack_body(wire_ref, out_ref):
    count, half, double = wire_ref.shape
    k = double // 2
    wide, back = k + LANES // 2, k
    edge = k - LANES // 2
    for i in range(count // 2):
        even, odd = wire_ref[2 * i].astype(F32), wire_ref[2 * i + 1].astype(F32)
        pairs = (
            (0, even[:, 0:wide], pltpu.roll(odd[:, 0:wide], LANES // 2, 1)),
            (half, pltpu.roll(even[:, edge:double], back, 1), odd[:, edge:double]),
        )
        for start, top, bottom in pairs:
            fold(top, bottom, out_ref.at[start : start + half, double * i : double * (i + 1)], k)


def spatial_body(act_ref, w_ref, s_ref, first_ref, last_ref, mom_ref, pad, *, dims):
    height, width, frames, depth = dims
    pad[...] = jnp.zeros(pad.shape, F32)
    pad[1 : height + 1, 1 : width + 1] = act_ref[...].astype(F32).reshape(dims)
    convolve(pad, w_ref, s_ref, dims)
    put_spatial(s_ref, first_ref, last_ref, mom_ref, dims)


def put_spatial(s_ref, first_ref, last_ref, mom_ref, dims):
    height, width, frames, depth = dims
    values = s_ref[...]
    put_moments(values, mom_ref)
    grid = values.reshape(height * width, frames, values.shape[-1])
    first_ref[...] = grid[:, 0:1, :]
    last_ref[...] = grid[:, frames - 1 : frames, :]


def next_body(
    ids_ref, t0, t1, t2, t3, both_ref, norm_ref, w_ref,
    s_ref, first_ref, last_ref, mom_ref, act_ref, pad, *, dims
):
    height, width, frames, depth = dims
    rows = height * width * frames
    pad[...] = jnp.zeros(pad.shape, F32)
    for j, t_ref in enumerate((t0, t1, t2, t3)):
        b = ids_ref[j]
        mean, inverse = joined_moments(both_ref[:, b], rows)
        norm = norm_ref[b]
        y = (t_ref[...].astype(F32) - mean) * (inverse * norm[0:1]) + norm[1:2]
        a = silu(y)
        at = pl.ds(pl.multiple_of(b * LANES, LANES), LANES)
        act_ref[:, at] = a.astype(BF)
        pad[1 : height + 1, 1 : width + 1, :, at] = a.reshape(height, width, frames, LANES)
    convolve(pad, w_ref, s_ref, dims)
    put_spatial(s_ref, first_ref, last_ref, mom_ref, dims)


def temporal_body(
    ids_ref, s_ref, both_ref, before_ref, after_ref, norm_ref, keep_ref, w_ref,
    send_ref, kept_ref, win_ref, stat_ref, scr, part, *, dims
):
    height, width, frames, depth = dims
    pixels = height * width
    rows = pixels * frames
    mid = s_ref.shape[-1]
    mean, inverse = joined_moments(both_ref[...], rows)
    stat_ref[0:1, :] = mean
    stat_ref[1:2, :] = inverse
    scale, bias = inverse * norm_ref[0:1], norm_ref[1:2]

    def active(v):
        return silu((v - mean) * scale + bias)

    middle = active(s_ref[...])
    widened(
        scr, middle.reshape(pixels, frames, mid),
        active(before_ref[...].reshape(pixels, mid)).reshape(pixels, 1, mid),
        active(after_ref[...].reshape(pixels, mid)).reshape(pixels, 1, mid),
    )
    win_ref[0] = (scr[:, 7 : 7 + frames, :] * keep_ref[0][None]).reshape(rows, mid).astype(BF)
    win_ref[1] = middle.astype(BF)
    win_ref[2] = (scr[:, 9 : 9 + frames, :] * keep_ref[1][None]).reshape(rows, mid).astype(BF)
    part[...] = mm(win_ref[0], w_ref[0], ((1,), (0,)))
    part[...] += mm(win_ref[1], w_ref[1], ((1,), (0,)))
    part[...] += mm(win_ref[2], w_ref[2], ((1,), (0,)))
    put_halves(ids_ref, part, send_ref, kept_ref)


def put_halves(ids_ref, part, send_ref, kept_ref):
    core = ids_ref[4]
    for i in range(2):
        other = pl.multiple_of((2 * i + 1 - core) * LANES, LANES)
        own = pl.multiple_of((2 * i + core) * LANES, LANES)
        send_ref[i] = part[:, pl.ds(other, LANES)].astype(BF)
        kept_ref[i] = part[:, pl.ds(own, LANES)]


def total_body(ids_ref, got_ref, kept_ref, last_ref, t_ref, low_ref, mom_ref):
    x = ids_ref[5]
    t = got_ref[x].astype(F32) + kept_ref[x] + last_ref[...].astype(F32)
    t_ref[...] = t
    low_ref[...] = t.astype(BF)
    put_moments(t, mom_ref)


def edges_body(b0, b1, b2, b3, first_ref, last_ref, *, dims):
    height, width, frames, depth = dims
    for j, ref in enumerate((b0, b1, b2, b3)):
        grid = ref[...].astype(F32).reshape(height * width, frames, LANES)
        first_ref[j] = grid[:, 0:1, :]
        last_ref[j] = grid[:, frames - 1 : frames, :]


def top_body(ids_ref, t_ref, both_ref, norm_ref, x_ref, cot_ref, block_ref, g_ref, low_ref, sums_ref):
    rows = t_ref.shape[0]
    b = ids_ref[0]
    mean, inverse = joined_moments(both_ref[:, b], rows)
    norm = norm_ref[b]
    normed = (t_ref[...] - mean) * inverse
    summed = normed * norm[0:1] + norm[1:2] + x_ref[...].astype(F32)
    block_ref[...] = silu(summed).astype(BF)
    g = cot_ref[...].astype(F32) * silu_slope(summed)
    g_ref[...] = g
    low_ref[...] = g.astype(BF)
    put_sums(g, normed, sums_ref)


def below_body(ids_ref, got_ref, kept_ref, last_ref, t_ref, both_ref, norm_ref, low_ref, sums_ref):
    rows = t_ref.shape[0]
    b, x = ids_ref[0], ids_ref[5]
    d_act = got_ref[x].astype(F32) + kept_ref[x] + last_ref[...].astype(F32)
    mean, inverse = joined_moments(both_ref[:, b], rows)
    norm = norm_ref[b]
    normed = (t_ref[...] - mean) * inverse
    g = d_act * silu_slope(normed * norm[0:1] + norm[1:2])
    low_ref[...] = g.astype(BF)
    put_sums(g, normed, sums_ref)


def dt_body(
    ids_ref, g0, g1, g2, g3, t0, t1, t2, t3, both_ref, sums_ref, norm_ref, win_ref,
    dt_ref, coef_ref, grad_ref, sum_ref, *, total
):
    rows = g0.shape[0]
    mid = win_ref.shape[-1]
    n_r = norm_ref.shape[0]
    for j, (g_ref, t_ref) in enumerate(((g0, t0), (g1, t1), (g2, t2), (g3, t3))):
        b = ids_ref[j]
        mean, inverse = joined_moments(both_ref[:, b], rows)
        sums = jnp.sum(sums_ref[:, b], axis=0)
        if j == 0:
            sum_ref[...] = sums
        c1 = norm_ref[b][0:1] * inverse
        c2 = c1 * sums[1:2] * (1.0 / total)
        c3 = c1 * inverse * sums[0:1] * (1.0 / total)
        coef_ref[j] = jnp.concatenate([c1, c2, c3, mean], axis=0)
        d = c1 * g_ref[...].astype(F32) - c2 - c3 * (t_ref[...].astype(F32) - mean)
        dt_ref[:, pl.ds(pl.multiple_of(b * LANES, LANES), LANES)] = d.astype(BF)
    dt = dt_ref[...]
    for k in range(3):
        term = mm(win_ref[k], dt, ((0,), (0,)))
        for r in range(n_r):
            grad_ref[r, k * mid : (k + 1) * mid, :] = term[:, r * LANES : (r + 1) * LANES].astype(BF)


def middle_body(
    ids_ref, dt_ref, coef_ref, gb_ref, ga_ref, tb_ref, ta_ref, keep_ref, w_ref, s_ref, stat_ref, norm_ref,
    d_ref, sums_ref, scr, *, dims
):
    height, width, frames, depth = dims
    pixels = height * width
    rows = pixels * frames
    scr[:, 8 : 8 + frames, :] = dt_ref[...].astype(F32).reshape(pixels, frames, depth)
    for j in range(4):
        at = pl.ds(pl.multiple_of(ids_ref[j] * LANES, LANES), LANES)
        c = coef_ref[j]

        def halo(g, t):
            d = c[0:1] * g.reshape(pixels, LANES) - c[1:2] - c[2:3] * (t.reshape(pixels, LANES) - c[3:4])
            return d.astype(BF).astype(F32).reshape(pixels, 1, LANES)

        scr[:, 7:8, at] = halo(gb_ref[j], tb_ref[j])
        scr[:, 8 + frames : 9 + frames, at] = halo(ga_ref[j], ta_ref[j])
    later = (scr[:, 9 : 9 + frames, :] * keep_ref[1][None]).reshape(rows, depth).astype(BF)
    earlier = (scr[:, 7 : 7 + frames, :] * keep_ref[0][None]).reshape(rows, depth).astype(BF)
    d_ref[...] = mm(later, w_ref[0], ((1,), (1,)))
    d_ref[...] += mm(dt_ref[...], w_ref[1], ((1,), (1,)))
    d_ref[...] += mm(earlier, w_ref[2], ((1,), (1,)))
    normed = (s_ref[...] - stat_ref[0:1]) * stat_ref[1:2]
    d = d_ref[...] * silu_slope(normed * norm_ref[0:1] + norm_ref[1:2])
    d_ref[...] = d
    put_sums(d, normed, sums_ref)


def spatial_grad(d_ref, s_ref, stat_ref, norm_ref, sums_ref, ds_ref, sum_ref, total):
    sums = jnp.sum(sums_ref[...], axis=0)
    sum_ref[...] = sums
    inverse = stat_ref[1:2]
    normed = (s_ref[...] - stat_ref[0:1]) * inverse
    d = d_ref[...] - sums[1:2] * (1.0 / total) - normed * (sums[0:1] * (1.0 / total))
    ds_ref[...] = (norm_ref[0:1] * inverse * d).astype(BF)


def adjoint(ds_ref, w_ref, pad, dims):
    height, width, frames, depth = dims
    pad[...] = jnp.zeros(pad.shape, F32)

    def tap(k, carry):
        w = w_ref[:, pl.ds(pl.multiple_of(k * depth, LANES), depth)]
        part = mm(ds_ref[...], w, ((1,), (0,)))
        at = (pl.ds(k // 3, height), pl.ds(k % 3, width))
        pad[at] = pad[at] + part.reshape(dims)
        return carry

    lax.fori_loop(0, 9, tap, 0)


def input_body(
    ids_ref, d_ref, s_ref, stat_ref, norm_ref, sums_ref, w_ref,
    ds_ref, send_ref, kept_ref, sum_ref, pad, part, *, dims, total
):
    height, width, frames, depth = dims
    spatial_grad(d_ref, s_ref, stat_ref, norm_ref, sums_ref, ds_ref, sum_ref, total)
    adjoint(ds_ref, w_ref, pad, dims)
    part[...] = pad[1 : height + 1, 1 : width + 1].reshape(part.shape)
    put_halves(ids_ref, part, send_ref, kept_ref)


def last_body(
    ids_ref, d_ref, s_ref, stat_ref, norm_ref, sums_ref, w_ref, g_ref,
    ds_ref, out_ref, sum_ref, pad, *, dims, total
):
    height, width, frames, depth = dims
    spatial_grad(d_ref, s_ref, stat_ref, norm_ref, sums_ref, ds_ref, sum_ref, total)
    adjoint(ds_ref, w_ref, pad, dims)
    at = (slice(1, height + 1), slice(1, width + 1), slice(None),
          pl.ds(pl.multiple_of(ids_ref[0] * LANES, LANES), LANES))
    pad[at] = pad[at] + g_ref[...].reshape(height, width, frames, LANES)
    out_ref[...] = pad[1 : height + 1, 1 : width + 1].reshape(out_ref.shape).astype(BF)


def weight_body(act_ref, ds_ref, out_ref, pad, acc, *, dims, dense):
    height, width, frames, depth = dims
    rows = height * width * frames
    mid = ds_ref.shape[-1]
    pad[...] = jnp.zeros(pad.shape, F32)
    pad[1 : height + 1, 1 : width + 1] = act_ref[...].astype(F32).reshape(dims)
    flipped = ds_ref[...].astype(F32).T.astype(BF)

    def tap(k, carry):
        piece = pad[pl.ds(k // 3, height), pl.ds(k % 3, width)]
        piece = piece.reshape(rows, depth).astype(BF)
        acc[:, pl.ds(pl.multiple_of(k * depth, LANES), depth)] = mm(flipped, piece, ((1,), (0,)))
        return carry

    lax.fori_loop(0, 9, tap, 0)
    if not dense:
        out_ref[...] = acc[...].astype(BF)
        return
    count, half, double = out_ref.shape
    k = double // 2
    wide, edge = k + LANES // 2, k - LANES // 2
    for f in range(count):
        if f % 2 == 0:
            top = acc[0:half, k * f : k * f + wide]
            bottom = pltpu.roll(acc[half:mid, k * f : k * f + wide], LANES // 2, 1)
        else:
            start = k * f - LANES // 2
            top = pltpu.roll(acc[0:half, start : start + wide], k, 1)
            bottom = acc[half:mid, start : start + wide]
        fold(top, bottom, out_ref.at[f], k)


def adam_step(param, gradient, moment_one, moment_two, rate, decay):
    first_new = BETA_ONE * moment_one + (1.0 - BETA_ONE) * gradient
    second_new = BETA_TWO * moment_two + (1.0 - BETA_TWO) * gradient * gradient
    fix_one = 1.0 - BETA_ONE**STEP
    fix_two = 1.0 - BETA_TWO**STEP
    update = first_new / fix_one / (jnp.sqrt(second_new / fix_two) + ADAM_EPS)
    return (param - rate * (update + decay * param), first_new, second_new)


def unfold(total, k):
    top = total[:, 0:k]
    bottom = total[:, k : 2 * k]
    return jnp.concatenate([top, bottom], axis=0)


def swap(parts, axis):
    return lax.all_to_all(parts, axis, 0, 0, tiled=True)


def from_all(value, axis):
    count = lax.axis_size(axis)
    return swap(jnp.broadcast_to(value[None], (count,) + value.shape), axis)


def across(value, bit):
    count = lax.axis_size("rep")
    return lax.ppermute(value, "rep", [(i, i ^ bit) for i in range(count)])


def from_group(value):
    far = across(value, 2)
    near = across(value, 1)
    return value, far, near, across(far, 1)


def neighbours(first, last):
    count = lax.axis_size("frames")
    before = lax.ppermute(last, "frames", [(i, i + 1) for i in range(count - 1)])
    after = lax.ppermute(first, "frames", [(i + 1, i) for i in range(count - 1)])
    return before, after


def reduced(send, kept, x):
    got = across(send, 1)
    away = lax.dynamic_index_in_dim(got, 1 - x, 0, False).astype(F32)
    away = away + lax.dynamic_index_in_dim(kept, 1 - x, 0, False)
    return got, kept, across(away.astype(BF), 2)


def sum_over(parts, axis):
    return jnp.sum(swap(parts, axis).astype(F32), axis=0)


def on_device(
    frames_in, cotangent, lengths,
    spatial_weights, spatial_first, spatial_second,
    temporal_weights, temporal_first, temporal_second,
    mid_norm, mid_first, mid_second,
    out_norm, out_first, out_second,
):
    own_frames, height, width, depth = frames_in.shape
    n_f, n_r = lax.axis_size("frames"), lax.axis_size("rep")
    assert n_r == 4 and depth == n_r * LANES
    me = lax.axis_index("rep")
    frames = own_frames * n_r
    pixels = height * width
    rows = pixels * frames
    total = float(rows * n_f)
    dims = (height, width, frames, depth)
    units, k, mid = spatial_weights.shape
    cols = LANES
    everyone = ("frames", "rep")
    ids = jnp.stack([me, me ^ 2, me ^ 1, me ^ 3, me & 1, me >> 1]).astype(jnp.int32)
    dense = dense_wire(mid, k, n_f)
    spatial_flops = 2 * rows * 9 * depth * mid
    temporal_flops = 2 * rows * 3 * depth * mid
    pad = pltpu.VMEM((height + 2, width + 2, frames, depth), F32)

    turned = jnp.swapaxes(spatial_weights, 1, 2)
    if dense:
        (wire,) = run(
            pack_body, [shape((units, mid // 2, 2 * k), BF)], [turned], "pack",
            [pltpu.VMEM((mid, k + LANES // 2), F32)],
        )
    else:
        wire = turned.astype(BF)
    temporal_low = temporal_weights.astype(BF)
    spatial_w, temporal_w = [], []
    for u in range(units):
        held = lax.all_gather(wire[u], "frames", axis=0)
        if dense:
            (held,) = run(unpack_body, [shape((mid, n_f * k), BF)], [held], "unpack")
        else:
            held = held.transpose(1, 0, 2).reshape(mid, n_f * k)
        spatial_w.append(held)
        shard = lax.all_gather(temporal_low[u], "frames", axis=0, tiled=True)
        shard = shard.reshape(3, n_r, mid, cols).transpose(1, 0, 2, 3)
        shard = swap(shard, "rep")
        temporal_w.append(shard.transpose(1, 2, 0, 3).reshape(3, mid, depth))

    frame_ids = lax.axis_index("frames") * frames + jnp.arange(frames, dtype=jnp.int32)
    clip_ends = jnp.cumsum(lengths)
    starts = jnp.concatenate([jnp.zeros((1,), jnp.int32), clip_ends[:-1]])
    opening = jnp.any(frame_ids[:, None] == starts[None, :], axis=1)
    closing = jnp.any((frame_ids + 1)[:, None] == clip_ends[None, :], axis=1)
    keep = jnp.where(jnp.stack([opening, closing]), 0.0, 1.0).astype(F32)[:, :, None]

    act = lax.all_gather(frames_in, "rep", axis=0, tiled=True).transpose(1, 2, 0, 3).reshape(rows, depth)
    state_cols = lax.dynamic_slice_in_dim(act, me * cols, cols, axis=1)
    cot = cotangent.reshape(own_frames, pixels, n_r, cols).transpose(2, 0, 1, 3)
    cot = swap(cot, "rep").reshape(frames, pixels, cols).transpose(1, 0, 2).reshape(rows, cols)

    mid_own = lax.dynamic_slice_in_dim(mid_norm, me * mid, mid, axis=2)
    out_split = out_norm.reshape(units, 2, n_r, cols).transpose(0, 2, 1, 3)

    halo = shape((pixels, 1, mid), F32)
    column = shape((rows, cols), BF)
    saved = []
    for u in range(units):
        outs = [shape((rows, mid), F32), halo, halo, shape((2, mid), F32)]
        if u == 0:
            spatial, first, last, mom = run(
                functools.partial(spatial_body, dims=dims), outs, [act, spatial_w[u]],
                f"spatial_{u}", [pad], flops=spatial_flops, moved=8 * MIB,
            )
        else:
            spatial, first, last, mom, act = run(
                functools.partial(next_body, dims=dims), outs + [shape((rows, depth), BF)],
                [ids, *t_group, both, out_split[u - 1], spatial_w[u]],
                f"spatial_{u}", [pad], scalars=1, flops=spatial_flops, moved=8 * MIB,
            )
        mid_both = from_all(mom, "frames")
        before, after = neighbours(first, last)
        send, kept, window, stat = run(
            functools.partial(temporal_body, dims=dims),
            [shape((2, rows, cols), BF), shape((2, rows, cols), F32), shape((3, rows, mid), BF), shape((2, mid), F32)],
            [ids, spatial, mid_both, before, after, mid_own[u], keep, temporal_w[u]],
            f"temporal_{u}", [pltpu.VMEM((pixels, frames + 16, mid), F32), pltpu.VMEM((rows, depth), F32)],
            scalars=1, flops=temporal_flops, moved=8 * MIB,
        )
        t, low, mom = run(
            total_body, [shape((rows, cols), F32), column, shape((2, cols), F32)],
            [ids, *reduced(send, kept, me >> 1)], f"total_{u}", scalars=1, moved=3 * MIB,
        )
        both = from_all(mom, everyone).reshape(n_f, n_r, 2, cols)
        t_group = from_group(low)
        edge = [shape((n_r, pixels, 1, cols), F32)] * 2
        t_edges = neighbours(*run(functools.partial(edges_body, dims=dims), edge, t_group, f"edges_{u}"))
        saved.append((act, spatial, stat, window, t, t_group, both, t_edges))

    d_norms = [None] * units
    spatial_parts, temporal_parts = [None] * units, [None] * units
    for u in reversed(range(units)):
        act, spatial, stat, window, t, t_group, both, t_edges = saved[u]
        if u == units - 1:
            block, summed_grad, low, sums = run(
                top_body, [column, shape((rows, cols), F32), column, shape((2, cols), F32)],
                [ids, t, both, out_split[u], state_cols, cot], "top", scalars=1, moved=3 * MIB,
            )
        else:
            low, sums = run(
                below_body, [column, shape((2, cols), F32)],
                [ids, *reduced(send, kept, me >> 1), t, both, out_split[u]], f"below_{u}", scalars=1, moved=3 * MIB,
            )
        sums = from_all(sums, everyone).reshape(n_f, n_r, 2, cols)
        g_group = from_group(low)
        g_edges = neighbours(*run(functools.partial(edges_body, dims=dims), edge, g_group, f"g_edges_{u}"))
        dt, coef, t_grad, out_sums = run(
            functools.partial(dt_body, total=total),
            [shape((rows, depth), BF), shape((n_r, 4, cols), F32), shape((n_r, 3 * mid, cols), BF), shape((2, cols), F32)],
            [ids, *g_group, *t_group, both, sums, out_split[u], window],
            f"dt_{u}", scalars=1, flops=temporal_flops, moved=8 * MIB,
        )
        t_grad = swap(t_grad, "rep").reshape(n_r, 3, mid, cols).transpose(1, 0, 2, 3)
        temporal_parts[u] = swap(t_grad.reshape(n_f, -1, cols), "frames")
        d_mid, sums = run(
            functools.partial(middle_body, dims=dims), [shape((rows, mid), F32), shape((2, mid), F32)],
            [ids, dt, coef, g_edges[0], g_edges[1], t_edges[0], t_edges[1], keep, temporal_w[u], spatial, stat, mid_own[u]],
            f"middle_{u}", [pltpu.VMEM((pixels, frames + 16, depth), F32)],
            scalars=1, flops=temporal_flops, moved=8 * MIB,
        )
        sums = from_all(sums, "frames")
        ds_shape, sum_shape = shape((rows, mid), BF), shape((2, mid), F32)
        if u > 0:
            ds, send, kept, mid_sums = run(
                functools.partial(input_body, dims=dims, total=total),
                [ds_shape, shape((2, rows, cols), BF), shape((2, rows, cols), F32), sum_shape],
                [ids, d_mid, spatial, stat, mid_own[u], sums, spatial_w[u]],
                f"input_{u}", [pad, pltpu.VMEM((rows, depth), F32)], scalars=1, flops=spatial_flops, moved=8 * MIB,
            )
        else:
            ds, d_input, mid_sums = run(
                functools.partial(last_body, dims=dims, total=total),
                [ds_shape, shape((rows, depth), BF), sum_shape],
                [ids, d_mid, spatial, stat, mid_own[u], sums, spatial_w[u], summed_grad],
                f"input_{u}", [pad], scalars=1, flops=spatial_flops, moved=8 * MIB,
            )
        wire_shape = shape((n_f, mid // 2, 2 * k) if dense else (mid, n_f * k), BF)
        (s_grad,) = run(
            functools.partial(weight_body, dims=dims, dense=dense), [wire_shape], [act, ds],
            f"weight_{u}", [pad, pltpu.VMEM((mid, n_f * k), F32)], flops=spatial_flops, moved=8 * MIB,
        )
        if not dense:
            s_grad = s_grad.reshape(mid, n_f, k).transpose(1, 0, 2)
        spatial_parts[u] = swap(s_grad, "frames")
        d_norms[u] = (mid_sums, out_sums)

    parts = d_input.reshape(pixels, n_r, own_frames, depth).transpose(1, 2, 0, 3)
    input_grad = sum_over(parts, "rep").reshape(frames_in.shape)
    block = swap(block.reshape(pixels, n_r, own_frames, cols).transpose(1, 2, 0, 3), "rep")
    block_out = block.transpose(1, 2, 0, 3).reshape(frames_in.shape)

    flat = jnp.concatenate([jnp.concatenate([m.reshape(-1), o.reshape(-1)]) for m, o in d_norms])
    flat = from_all(flat, "rep").reshape(n_r, units, -1)
    mid_grad = flat[:, :, : 2 * mid].reshape(n_r, units, 2, mid).transpose(1, 2, 0, 3)
    mid_grad = mid_grad.reshape(units, 2, n_r * mid)
    out_grad = flat[:, :, 2 * mid :].reshape(n_r, units, 2, cols).transpose(1, 2, 0, 3)
    out_grad = out_grad.reshape(units, 2, depth)

    spatial_grads = []
    for part in spatial_parts:
        grad = jnp.sum(part.astype(F32), axis=0)
        spatial_grads.append(unfold(grad, k) if dense else grad)
    temporal_grads = [jnp.sum(part.astype(F32), axis=0) for part in temporal_parts]

    flip = functools.partial(jnp.swapaxes, axis1=1, axis2=2)
    s_new, s_first_new, s_second_new = adam_step(
        flip(spatial_weights), jnp.stack(spatial_grads), flip(spatial_first), flip(spatial_second), RATE_WEIGHT, DECAY
    )
    temporal_new, temporal_first_new, temporal_second_new = adam_step(
        temporal_weights, jnp.stack(temporal_grads), temporal_first, temporal_second, RATE_WEIGHT, DECAY
    )
    mid_new, mid_first_new, mid_second_new = adam_step(mid_norm, mid_grad, mid_first, mid_second, RATE_NORM, 0.0)
    out_new, out_first_new, out_second_new = adam_step(out_norm, out_grad, out_first, out_second, RATE_NORM, 0.0)
    return (
        block_out, input_grad,
        flip(s_new), flip(s_first_new), flip(s_second_new), flip(s_new).astype(BF),
        temporal_new, temporal_first_new, temporal_second_new, temporal_new.astype(BF),
        mid_new, mid_first_new, mid_second_new,
        out_new, out_first_new, out_second_new,
    )


def solution(mesh):
    by_frame = P(("frames", "rep"), None, None, None)
    by_block = P(None, "frames", "rep")
    placed = (by_frame, by_frame, P()) + (by_block,) * 6 + (P(),) * 6
    return jax.shard_map(
        on_device,
        mesh=mesh,
        in_specs=placed,
        out_specs=(by_frame, by_frame) + (by_block,) * 8 + (P(),) * 6,
        check_vma=False,
    )
```

time: 1080 us -> 668 us (0.62)
  local copies, waits for them, and re-layouts: 359 us -> 78.4 us
  other arithmetic: 122 us -> 16.3 us
  Pallas kernels: 0 us -> 89.1 us
  matrix products: 74 us -> 0 us
  waiting for transfers between devices: 283 us -> 232 us
  blocking collectives: 98.4 us -> 119 us
    slice x23 -> x3, local copies, waits for them, and re-layouts: 152 us -> 1.21 us  [the longest x1 0.89 us: on_device(): held = lax.all_gather(wire[u], 'frames', axis=0)]
    pallas_call x0 -> x23, Pallas kernels: none -> 89.1 us  [run(): pl.pallas_call(body, out_shape=tuple(outs), in_specs=[SMEM] * scalars + [...]
    reshape x13 -> x7, local copies, waits for them, and re-layouts: 79.4 us -> 4.98 us  [the longest x2 3.5 us: on_device(): swap(t_grad, 'rep').reshape(n_r, 3, mid, cols).transpose(1, 0, 2, 3)]
    dot_general x20 -> x0, matrix products: 74 us -> none  [mm(): return lax.dot_general(a, b, (dims, ((), ())), preferred_element_type=F32)]
    all_to_all x21 -> x17, waiting for transfers between devices: 207 us -> 159 us  [swap(): return lax.all_to_all(parts, axis, 0, 0, tiled=True)]
    scatter-add x16 -> x0, other arithmetic: 44.1 us -> none  [adjoint(): total = total.at[i:i + height, j:j + width].add(grid[:, :, :, 3 * i + j])]
    all_gather x5 -> x2, waiting for transfers between devices: 73.7 us -> 35 us  [on_device(): held = lax.all_gather(wire[u], 'frames', axis=0)]
    ppermute x8 -> x30, waiting for transfers between devices: 1.33 us -> 36.7 us  [the longest x18 36.7 us: across(): return lax.ppermute(value, 'rep', [(i, i ^ bit) for i in range(count)])]
  transfers between devices with their start and end apart: 35 -> 50, of which waited for: 19 -> 19; matrix products, arithmetic and copies ran while one was open for 33% -> 8% of each run, Pallas kernels for 0% -> 11%
where the time goes in v2:
time: 668 us; the launch traced here: 659 us
  waiting for transfers between devices  232 us (35%)
  blocking collectives  119 us (18%)
  starting transfers between devices  108 us (16%)
  Pallas kernels  89.1 us (13%)
  local copies, waits for them, and re-layouts  78.4 us (12%)
  other arithmetic  16.3 us (2%)
  between operations  15.1 us (2%)
    all_to_all x17, waiting for transfers between devices, swap(): return lax.all_to_all(parts, axis, 0, 0, tiled=True)  159 us
    pallas_call x23, Pallas kernels, run(): pl.pallas_call(body, out_shape=tuple(outs), in_specs=[SMEM] * scalars + [...  89.1 us
    all_gather x2, blocking collectives, on_device(): shard = lax.all_gather(temporal_low[u], 'frames', axis=0, tiled=True)  66.9 us
    all_to_all x17, starting transfers between devices, swap(): return lax.all_to_all(parts, axis, 0, 0, tiled=True)  66.3 us
    all_to_all x3, blocking collectives, swap(): return lax.all_to_all(parts, axis, 0, 0, tiled=True)  52.3 us
    unnamed x154, local copies, waits for them, and re-layouts  39.3 us
    ppermute x18, waiting for transfers between devices, across(): return lax.ppermute(value, 'rep', [(i, i ^ bit) for i in range(count)])  36.7 us
    all_gather x2, waiting for transfers between devices, on_device(): held = lax.all_gather(wire[u], 'frames', axis=0)  35 us
  transfers between devices with their start and end apart: 50, of which 19 were waited for; matrix products, arithmetic and copies ran while one was open for 8% of the time, Pallas kernels for 11%

profile of v2, /device:TPU:0, one launch (start us, length us, event | category | flops | bytes accessed | tf_op | source)
XLA Modules:
  0.0 658.5 jit_solution(2973024955212358009)
XLA Ops:
  11.3 34.2 %all-gather = bf16[1,3456,128]{2,1,0:T(8,128)(2,1)S(1)} all-gather(bf16[1,432,128]{2,1,0:T(8,128)(2,1)S(1)} %get-tuple-element.197), channel_id=2, replica_groups=mesh['frames'=8,'rep'=4] {'frames'}, dimensions={1}, use_global_device_ids=true | all-gather | bytes 995328 | tf_op jit(solution)/shard_map/all_gather | solution.py:498
  53.8 35.0 %all-gather.8.cloned.1.call-done.wire_ref = bf16[8,144,1152]{2,1,0:T(8,128)(2,1)} async-done(((bf16[1,144,1152]{2,1,0:T(8,128)(2,1)}), bf16[8,144,1152]{2,1,0:T(8,128)(2,1)}) %all-gather.8.cloned.1.call-update) | async-done | bytes 2654224 | tf_op jit(solution)/shard_map/all_gather | solution.py:492
  91.2 9.6 %spatial_0.1 = (f32[1176,288]{1,0:T(8,128)S(1)}, f32[49,1,288]{2,1,0:T(1,128)S(1)}, f32[49,1,288]{2,1,0:T(1,128)S(1)}, f32[2,288]{1,0:T(2,128)S(1)}) custom-call(bf16[1176,512]{1,0:T(8,128)(2,1)S(1)} %bitcast.112, bf16[288,4608]{1,0:T(8,128)(2,1)S(1)} %unpack.2.w_ref), custom_call_target="tpu_custom_call" | custom-call | flops 3121348608 | bytes 8388608 | tf_op jit(solution)/shard_map/spatial_0/pallas_call | solution.py:31
  106.5 6.2 all-to-all-start
  112.7 6.6 all-to-all-done.both_ref
  130.8 7.6 %collective-permute-done.3.last_ref = bf16[1176,128]{1,0:T(8,128)(2,1)S(1)} collective-permute-done((bf16[1176,128]{1,0:T(8,128)(2,1)S(1)}, bf16[1176,128]{1,0:T(8,128)(2,1)S(1)}, u32[]{:S(2)}, u32[]{:S(2)}) %collective-permute-start.3) | collective-permute-done | bytes 301088 | tf_op jit(solution)/shard_map/ppermute | solution.py:429
  145.0 32.7 %all-gather.1 = bf16[1,3456,128]{2,1,0:T(8,128)(2,1)S(1)} all-gather(bf16[1,432,128]{2,1,0:T(8,128)(2,1)S(1)} %get-tuple-element.196), channel_id=3, replica_groups=mesh['frames'=8,'rep'=4] {'frames'}, dimensions={1}, use_global_device_ids=true | all-gather | bytes 995328 | tf_op jit(solution)/shard_map/all_gather | solution.py:498
  185.6 11.1 %spatial_1.1 = (f32[1176,288]{1,0:T(8,128)S(1)}, f32[49,1,288]{2,1,0:T(1,128)S(1)}, f32[49,1,288]{2,1,0:T(1,128)S(1)}, f32[2,288]{1,0:T(2,128)S(1)}, bf16[1176,512]{1,0:T(8,128)(2,1)S(1)}) custom-call(s32[6]{0:T(128)S(1)} %stack.54.ids_ref, bf16[1176,128]{1,0:T(8,128)(2,1)S(1)} %get-tuple-element.78.t0.b0, ...), custom_call_target="tpu_custom_call" | custom-call | flops 3121348608 | bytes 8388608 | tf_op jit(solution)/shard_map/spatial_1/pallas_call | solution.py:31
  204.4 6.6 %all-to-all-start.3 = ((f32[8,2,288]{2,1,0:T(2,128)}), f32[8,2,288]{2,1,0:T(2,128)S(1)}, u32[]{:S(2)}, u32[]{:S(2)}) async-start(f32[8,2,288]{2,1,0:T(2,128)} %broadcast_in_dim.30), calls=%async_computation.3 | async-start | bytes 49152 | tf_op jit(solution)/shard_map/all_to_all | solution.py:419
  211.1 6.6 all-to-all-done.3.both_ref
  239.0 7.0 %all-to-all-done.6 = bf16[4,6,49,128]{3,2,1,0:T(8,128)(2,1)} async-done(((bf16[4,6,49,128]{3,2,1,0:T(8,128)(2,1)}), bf16[4,6,49,128]{3,2,1,0:T(8,128)(2,1)}, u32[]{:S(2)}, u32[]{:S(2)}) %all-to-all-start.6) | async-done | bytes 301088 | tf_op jit(solution)/shard_map/all_to_all | solution.py:419
  268.2 8.2 %collective-permute-done.11.g1.b1 = bf16[1176,128]{1,0:T(8,128)(2,1)} collective-permute-done((bf16[1176,128]{1,0:T(8,128)(2,1)S(1)}, bf16[1176,128]{1,0:T(8,128)(2,1)}, u32[]{:S(2)}, u32[]{:S(2)}) %collective-permute-start.11) | collective-permute-done | bytes 301088 | tf_op jit(solution)/shard_map/ppermute | solution.py:429
  288.2 5.2 collective-permute-start.17
  301.9 4.6 middle_1.1
  306.5 13.9 %all_to_all.101.sums_ref = f32[8,2,288]{2,1,0:T(2,128)S(1)} all-to-all(f32[8,2,288]{2,1,0:T(2,128)S(1)} %broadcast_in_dim.33), channel_id=1, replica_groups=mesh['frames'=8,'rep'=4] {'frames'}, dimensions={0} | all-to-all | bytes 36864 | tf_op jit(solution)/shard_map/all_to_all | solution.py:419
  320.4 8.8 %input_1.1 = (bf16[1176,288]{1,0:T(8,128)(2,1)S(1)}, bf16[2,1176,128]{2,1,0:T(8,128)(2,1)S(1)}, f32[2,1176,128]{2,1,0:T(8,128)S(1)}, f32[2,288]{1,0:T(2,128)S(1)}) custom-call(s32[6]{0:T(128)S(1)} %stack.54.ids_ref, f32[1176,288]{1,0:T(8,128)S(1)} %get-tuple-element.100.d_ref, f32[1176,288]{1,0:T(8,128)S(1)} %copy-done.20, f32[2,288]{1,0:T(2,128)S(1)} %copy-done.45, ...), custom_call_target="tpu_custom_call" | custom-call | flops 3121348608 | bytes 8388608 | tf_op jit(solution)/shard_map/input_1/pallas_call | solution.py:31
  332.9 7.7 %collective-permute-done.22.last_ref = bf16[1176,128]{1,0:T(8,128)(2,1)S(1)} collective-permute-done((bf16[1176,128]{1,0:T(8,128)(2,1)S(1)}, bf16[1176,128]{1,0:T(8,128)(2,1)S(1)}, u32[]{:S(2)}, u32[]{:S(2)}) %collective-permute-start.22) | collective-permute-done | bytes 301088 | tf_op jit(solution)/shard_map/ppermute | solution.py:429
  343.2 6.9 %collective-permute-done.23.g1.b1 = bf16[1176,128]{1,0:T(8,128)(2,1)S(1)} collective-permute-done((bf16[1176,128]{1,0:T(8,128)(2,1)S(1)}, bf16[1176,128]{1,0:T(8,128)(2,1)S(1)}, u32[]{:S(2)}, u32[]{:S(2)}) %collective-permute-start.23) | collective-permute-done | bytes 301088 | tf_op jit(solution)/shard_map/ppermute | solution.py:429
  356.0 4.6 all-to-all-done.10
  369.7 4.6 collective-permute-start.26
  377.5 4.5 dt_0.1
  387.9 12.3 %all_to_all.102.sums_ref = f32[8,2,288]{2,1,0:T(2,128)S(1)} all-to-all(f32[8,2,288]{2,1,0:T(2,128)S(1)} %broadcast_in_dim.35), channel_id=1, replica_groups=mesh['frames'=8,'rep'=4] {'frames'}, dimensions={0} | all-to-all | bytes 36864 | tf_op jit(solution)/shard_map/all_to_all | solution.py:419
  407.5 8.5 %input_0.1 = (bf16[1176,288]{1,0:T(8,128)(2,1)S(1)}, bf16[1176,512]{1,0:T(8,128)(2,1)S(1)}, f32[2,288]{1,0:T(2,128)S(1)}) custom-call(s32[6]{0:T(128)S(1)} %stack.54.ids_ref, f32[1176,288]{1,0:T(8,128)S(1)} %copy-done.53, f32[1176,288]{1,0:T(8,128)S(1)} %copy-done.17, f32[2,288]{1,0:T(2,128)S(1)} %copy-done.43, f32[2,288]{1,0:T(2,128)S(1)} %get-tuple-element.199.norm_ref, ...), custom_call_target="tpu_custom_call" | custom-call | flops 3121348608 | bytes 8388608 | tf_op jit(solution)/shard_map/input_0/pallas_call | solution.py:31
  426.5 26.1 %all_to_all.103 = bf16[8,432,128]{2,1,0:T(8,128)(2,1)} all-to-all(bf16[8,432,128]{2,1,0:T(8,128)(2,1)S(1)} %bitcast.127), channel_id=1, replica_groups=mesh['frames'=8,'rep'=4] {'frames'}, dimensions={0} | all-to-all | bytes 1769472 | tf_op jit(solution)/shard_map/all_to_all | solution.py:419
  459.1 10.6 %all-to-all-done.15 = bf16[4,864,128]{2,1,0:T(8,128)(2,1)} async-done(((bf16[4,864,128]{2,1,0:T(8,128)(2,1)}), bf16[4,864,128]{2,1,0:T(8,128)(2,1)}, u32[]{:S(2)}, u32[]{:S(2)}) %all-to-all-start.15) | async-done | bytes 884768 | tf_op jit(solution)/shard_map/all_to_all | solution.py:419
  475.5 15.6 %all-to-all-done.12 = bf16[4,6,49,512]{3,2,1,0:T(8,128)(2,1)S(1)} async-done(((bf16[4,6,49,512]{3,2,1,0:T(8,128)(2,1)}), bf16[4,6,49,512]{3,2,1,0:T(8,128)(2,1)S(1)}, u32[]{:S(2)}, u32[]{:S(2)}) %all-to-all-start.12) | async-done | bytes 1204256 | tf_op jit(solution)/shard_map/all_to_all | solution.py:419
  495.4 7.6 %weight_1.1 = bf16[8,144,1152]{2,1,0:T(8,128)(2,1)} custom-call(bf16[1176,512]{1,0:T(8,128)(2,1)S(1)} %copy-done.63, bf16[1176,288]{1,0:T(8,128)(2,1)S(1)} %copy-done.61), custom_call_target="tpu_custom_call" | custom-call | flops 3121348608 | bytes 8388608 | tf_op jit(solution)/shard_map/weight_1/pallas_call | solution.py:31
  503.1 14.7 %all-to-all-done.16 = bf16[8,432,128]{2,1,0:T(8,128)(2,1)} async-done(((bf16[8,432,128]{2,1,0:T(8,128)(2,1)}), bf16[8,432,128]{2,1,0:T(8,128)(2,1)}, u32[]{:S(2)}, u32[]{:S(2)}) %all-to-all-start.16) | async-done | bytes 884768 | tf_op jit(solution)/shard_map/all_to_all | solution.py:419
  517.8 4.6 all-to-all-start.14
  522.4 7.6 %weight_0.1 = bf16[8,144,1152]{2,1,0:T(8,128)(2,1)} custom-call(bf16[1176,512]{1,0:T(8,128)(2,1)S(1)} %bitcast.114, bf16[1176,288]{1,0:T(8,128)(2,1)S(1)} %copy-done.59), custom_call_target="tpu_custom_call" | custom-call | flops 3121348608 | bytes 8388608 | tf_op jit(solution)/shard_map/weight_0/pallas_call | solution.py:31
  530.0 52.0 %all-to-all-done.14 = bf16[8,144,1152]{2,1,0:T(8,128)(2,1)} async-done(((bf16[8,144,1152]{2,1,0:T(8,128)(2,1)}), bf16[8,144,1152]{2,1,0:T(8,128)(2,1)}, u32[]{:S(2)}, u32[]{:S(2)}) %all-to-all-start.14) | async-done | bytes 2654240 | tf_op jit(solution)/shard_map/all_to_all | solution.py:419
  611.2 34.8 %all-to-all-done.13 = bf16[8,144,1152]{2,1,0:T(8,128)(2,1)S(1)} async-done(((bf16[8,144,1152]{2,1,0:T(8,128)(2,1)}), bf16[8,144,1152]{2,1,0:T(8,128)(2,1)S(1)}, u32[]{:S(2)}, u32[]{:S(2)}) %all-to-all-start.13) | async-done | bytes 2654240 | tf_op jit(solution)/shard_map/all_to_all | solution.py:419
  (323 shorter events, 216.8 us)
Async XLA Ops:
  7.2 44.8 %all-gather.6.cloned.1.call-start = ((), (), s32[]{:S(2)}) async-start(), calls=%async_computation.20 | async-start | bytes 1720320 | tf_op jit(solution)/shard_map/all_gather | solution.py:510
  7.9 80.9 %all-gather.8.cloned.1.call-start = ((), (), s32[]{:S(2)}) async-start(), calls=%async_computation.21 | async-start | bytes 2985984 | tf_op jit(solution)/shard_map/all_gather | solution.py:492
  10.5 172.7 %all-gather.10.cloned.1.call-start = ((), (), s32[]{:S(2)}) async-start(), calls=%async_computation.22 | async-start | bytes 2985984 | tf_op jit(solution)/shard_map/all_gather | solution.py:492
  46.5 59.4 %all-to-all-start.1 = ((bf16[4,3,288,128]{3,2,1,0:T(8,128)(2,1)}), bf16[4,3,288,128]{3,2,1,0:T(8,128)(2,1)S(1)}, u32[]{:S(2)}, u32[]{:S(2)}) async-start(bf16[4,3,288,128]{3,2,1,0:T(8,128)(2,1)} %copy.104), calls=%async_computation.1 | async-start | bytes 1769472 | tf_op jit(solution)/shard_map/all_to_all | solution.py:419
  102.1 17.2 %collective-permute-start = (f32[49,1,288]{2,1,0:T(1,128)S(1)}, f32[49,1,288]{2,1,0:T(1,128)S(1)}, u32[]{:S(2)}, u32[]{:S(2)}) collective-permute-start(f32[49,1,288]{2,1,0:T(1,128)S(1)} %get-tuple-element.74), channel_id=1, source_target_pairs={{0,4},{4,8},{8,12},{12,16},{16,20},{20,24},{24,28},{1,5},{5,9},{9,... | collective-permute-start | bytes 169352 | tf_op jit(solution)/shard_map/ppermute | solution.py:440
  104.6 14.7 %collective-permute-start.1 = (f32[49,1,288]{2,1,0:T(1,128)S(1)}, f32[49,1,288]{2,1,0:T(1,128)S(1)}, u32[]{:S(2)}, u32[]{:S(2)}) collective-permute-start(f32[49,1,288]{2,1,0:T(1,128)S(1)} %get-tuple-element.75), channel_id=1, source_target_pairs={{4,0},{8,4},{12,8},{16,12},{20,16},{24,20},{28,24},{5,1},{9,5},{13... | collective-permute-start | bytes 169352 | tf_op jit(solution)/shard_map/ppermute | solution.py:441
  106.5 12.8 %all-to-all-start = ((f32[8,2,288]{2,1,0:T(2,128)}), f32[8,2,288]{2,1,0:T(2,128)S(1)}, u32[]{:S(2)}, u32[]{:S(2)}) async-start(f32[8,2,288]{2,1,0:T(2,128)} %broadcast_in_dim.26), calls=%async_computation | async-start | bytes 49152 | tf_op jit(solution)/shard_map/all_to_all | solution.py:419
  140.2 42.8 %collective-permute-start.4 = (bf16[1176,128]{1,0:T(8,128)(2,1)S(1)}, bf16[1176,128]{1,0:T(8,128)(2,1)S(1)}, u32[]{:S(2)}, u32[]{:S(2)}) collective-permute-start(bf16[1176,128]{1,0:T(8,128)(2,1)S(1)} %get-tuple-element.78.t0.b0), channel_id=1, source_target_pairs={{0,2},{1,3},{2,0},{3,1},{4,6},{5,7},{6,4},{7,5},{8,10},{9,11},{10,... | collective-permute-start | bytes 903176 | tf_op jit(solution)/shard_map/ppermute | solution.py:429
  142.4 36.3 %all-to-all-start.2 = ((f32[32,2,128]{2,1,0:T(2,128)}), f32[32,2,128]{2,1,0:T(2,128)S(1)}, u32[]{:S(2)}, u32[]{:S(2)}) async-start(f32[32,2,128]{2,1,0:T(2,128)} %broadcast_in_dim.29), calls=%async_computation.2 | async-start | bytes 65536 | tf_op jit(solution)/shard_map/all_to_all | solution.py:419
  178.7 25.1 %all-to-all-start.4 = ((bf16[4,3,288,128]{3,2,1,0:T(8,128)(2,1)}), bf16[4,3,288,128]{3,2,1,0:T(8,128)(2,1)S(1)}, u32[]{:S(2)}, u32[]{:S(2)}) async-start(bf16[4,3,288,128]{3,2,1,0:T(8,128)(2,1)} %copy.106), calls=%async_computation.4 | async-start | bytes 1769472 | tf_op jit(solution)/shard_map/all_to_all | solution.py:419
  199.0 18.7 %collective-permute-start.7 = (f32[49,1,288]{2,1,0:T(1,128)S(1)}, f32[49,1,288]{2,1,0:T(1,128)S(1)}, u32[]{:S(2)}, u32[]{:S(2)}) collective-permute-start(f32[49,1,288]{2,1,0:T(1,128)S(1)} %get-tuple-element.82), channel_id=1, source_target_pairs={{0,4},{4,8},{8,12},{12,16},{16,20},{20,24},{24,28},{1,5},{5,9},{9,... | collective-permute-start | bytes 169352 | tf_op jit(solution)/shard_map/ppermute | solution.py:440
  202.5 15.2 %collective-permute-start.8 = (f32[49,1,288]{2,1,0:T(1,128)S(1)}, f32[49,1,288]{2,1,0:T(1,128)S(1)}, u32[]{:S(2)}, u32[]{:S(2)}) collective-permute-start(f32[49,1,288]{2,1,0:T(1,128)S(1)} %get-tuple-element.83), channel_id=1, source_target_pairs={{4,0},{8,4},{12,8},{16,12},{20,16},{24,20},{28,24},{5,1},{9,5},{13... | collective-permute-start | bytes 169352 | tf_op jit(solution)/shard_map/ppermute | solution.py:441
  204.4 13.2 %all-to-all-start.3 = ((f32[8,2,288]{2,1,0:T(2,128)}), f32[8,2,288]{2,1,0:T(2,128)S(1)}, u32[]{:S(2)}, u32[]{:S(2)}) async-start(f32[8,2,288]{2,1,0:T(2,128)} %broadcast_in_dim.30), calls=%async_computation.3 | async-start | bytes 49152 | tf_op jit(solution)/shard_map/all_to_all | solution.py:419
  229.4 18.3 %collective-permute-start.10 = (bf16[1176,128]{1,0:T(8,128)(2,1)}, bf16[1176,128]{1,0:T(8,128)(2,1)}, u32[]{:S(2)}, u32[]{:S(2)}) collective-permute-start(bf16[1176,128]{1,0:T(8,128)(2,1)} %fusion.3), channel_id=1, source_target_pairs={{0,2},{1,3},{2,0},{3,1},{4,6},{5,7},{6,4},{7,5},{8,10},{9,11},{10,... | collective-permute-start | bytes 903176 | tf_op jit(solution)/shard_map/ppermute | solution.py:429
  267.6 12.0 %collective-permute-start.16 = (bf16[1176,128]{1,0:T(8,128)(2,1)S(1)}, bf16[1176,128]{1,0:T(8,128)(2,1)}, u32[]{:S(2)}, u32[]{:S(2)}) collective-permute-start(bf16[1176,128]{1,0:T(8,128)(2,1)S(1)} %collective-permute-done.14.t1.b1), channel_id=1, source_target_pairs={{0,1},{1,0},{2,3},{3,2},{4,5},{5,4},{6,7},{7,6},{8,9},{9,8},{10,11... | collective-permute-start | bytes 903176 | tf_op jit(solution)/shard_map/ppermute | solution.py:429
  268.1 18.2 %collective-permute-start.12 = (bf16[1176,128]{1,0:T(8,128)(2,1)S(1)}, bf16[1176,128]{1,0:T(8,128)(2,1)}, u32[]{:S(2)}, u32[]{:S(2)}) collective-permute-start(bf16[1176,128]{1,0:T(8,128)(2,1)S(1)} %get-tuple-element.89.g0.b0), channel_id=1, source_target_pairs={{0,1},{1,0},{2,3},{3,2},{4,5},{5,4},{6,7},{7,6},{8,9},{9,8},{10,11... | collective-permute-start | bytes 903176 | tf_op jit(solution)/shard_map/ppermute | solution.py:429
  277.0 18.2 %all-to-all-start.8 = ((f32[32,2,128]{2,1,0:T(2,128)}), f32[32,2,128]{2,1,0:T(2,128)S(1)}, u32[]{:S(2)}, u32[]{:S(2)}) async-start(f32[32,2,128]{2,1,0:T(2,128)} %broadcast_in_dim.32), calls=%async_computation.8 | async-start | bytes 65536 | tf_op jit(solution)/shard_map/all_to_all | solution.py:419
  281.4 20.4 %collective-permute-start.19 = (f32[4,49,1,128]{3,2,1,0:T(1,128)}, f32[4,49,1,128]{3,2,1,0:T(1,128)S(1)}, u32[]{:S(2)}, u32[]{:S(2)}) collective-permute-start(f32[4,49,1,128]{3,2,1,0:T(1,128)} %get-tuple-element.97), channel_id=1, source_target_pairs={{0,4},{4,8},{8,12},{12,16},{16,20},{20,24},{24,28},{1,5},{5,9},{9,... | collective-permute-start | bytes 301064 | tf_op jit(solution)/shard_map/ppermute | solution.py:440
  285.0 16.8 %collective-permute-start.20 = (f32[4,49,1,128]{3,2,1,0:T(1,128)}, f32[4,49,1,128]{3,2,1,0:T(1,128)}, u32[]{:S(2)}, u32[]{:S(2)}) collective-permute-start(f32[4,49,1,128]{3,2,1,0:T(1,128)} %get-tuple-element.98), channel_id=1, source_target_pairs={{4,0},{8,4},{12,8},{16,12},{20,16},{24,20},{28,24},{5,1},{9,5},{13... | collective-permute-start | bytes 301064 | tf_op jit(solution)/shard_map/ppermute | solution.py:441
  288.2 13.6 %collective-permute-start.17 = (f32[4,49,1,128]{3,2,1,0:T(1,128)}, f32[4,49,1,128]{3,2,1,0:T(1,128)}, u32[]{:S(2)}, u32[]{:S(2)}) collective-permute-start(f32[4,49,1,128]{3,2,1,0:T(1,128)} %get-tuple-element.95), channel_id=1, source_target_pairs={{0,4},{4,8},{8,12},{12,16},{16,20},{20,24},{24,28},{1,5},{5,9},{9,... | collective-permute-start | bytes 301064 | tf_op jit(solution)/shard_map/ppermute | solution.py:440
  343.2 25.4 %collective-permute-start.24 = (bf16[1176,128]{1,0:T(8,128)(2,1)S(1)}, bf16[1176,128]{1,0:T(8,128)(2,1)S(1)}, u32[]{:S(2)}, u32[]{:S(2)}) collective-permute-start(bf16[1176,128]{1,0:T(8,128)(2,1)S(1)} %get-tuple-element.105.g0.b0), channel_id=1, source_target_pairs={{0,1},{1,0},{2,3},{3,2},{4,5},{5,4},{6,7},{7,6},{8,9},{9,8},{10,11... | collective-permute-start | bytes 903176 | tf_op jit(solution)/shard_map/ppermute | solution.py:429
  350.1 18.5 %collective-permute-start.25 = (bf16[1176,128]{1,0:T(8,128)(2,1)S(1)}, bf16[1176,128]{1,0:T(8,128)(2,1)}, u32[]{:S(2)}, u32[]{:S(2)}) collective-permute-start(bf16[1176,128]{1,0:T(8,128)(2,1)S(1)} %collective-permute-done.23.g1.b1), channel_id=1, source_target_pairs={{0,1},{1,0},{2,3},{3,2},{4,5},{5,4},{6,7},{7,6},{8,9},{9,8},{10,11... | collective-permute-start | bytes 903176 | tf_op jit(solution)/shard_map/ppermute | solution.py:429
  360.6 27.3 %all-to-all-start.7 = ((bf16[4,6,49,128]{3,2,1,0:T(8,128)(2,1)}), bf16[4,6,49,128]{3,2,1,0:T(8,128)(2,1)}, u32[]{:S(2)}, u32[]{:S(2)}) async-start(bf16[4,6,49,128]{3,2,1,0:T(8,128)(2,1)} %copy.110), calls=%async_computation.7 | async-start | bytes 688128 | tf_op jit(solution)/shard_map/all_to_all | solution.py:419
  364.8 17.2 %collective-permute-start.28 = (f32[4,49,1,128]{3,2,1,0:T(1,128)S(1)}, f32[4,49,1,128]{3,2,1,0:T(1,128)S(1)}, u32[]{:S(2)}, u32[]{:S(2)}) collective-permute-start(f32[4,49,1,128]{3,2,1,0:T(1,128)S(1)} %get-tuple-element.112), channel_id=1, source_target_pairs={{0,4},{4,8},{8,12},{12,16},{16,20},{20,24},{24,28},{1,5},{5,9},{9,... | collective-permute-start | bytes 301064 | tf_op jit(solution)/shard_map/ppermute | solution.py:440
  367.3 14.7 %collective-permute-start.29 = (f32[4,49,1,128]{3,2,1,0:T(1,128)S(1)}, f32[4,49,1,128]{3,2,1,0:T(1,128)S(1)}, u32[]{:S(2)}, u32[]{:S(2)}) collective-permute-start(f32[4,49,1,128]{3,2,1,0:T(1,128)S(1)} %get-tuple-element.113), channel_id=1, source_target_pairs={{4,0},{8,4},{12,8},{16,12},{20,16},{24,20},{28,24},{5,1},{9,5},{13... | collective-permute-start | bytes 301064 | tf_op jit(solution)/shard_map/ppermute | solution.py:441
  369.7 12.3 %collective-permute-start.26 = (f32[4,49,1,128]{3,2,1,0:T(1,128)S(1)}, f32[4,49,1,128]{3,2,1,0:T(1,128)S(1)}, u32[]{:S(2)}, u32[]{:S(2)}) collective-permute-start(f32[4,49,1,128]{3,2,1,0:T(1,128)S(1)} %get-tuple-element.110), channel_id=1, source_target_pairs={{0,4},{4,8},{8,12},{12,16},{16,20},{20,24},{24,28},{1,5},{5,9},{9,... | collective-permute-start | bytes 301064 | tf_op jit(solution)/shard_map/ppermute | solution.py:440
  400.2 17.9 %all-to-all-start.17 = ((bf16[4,864,128]{2,1,0:T(8,128)(2,1)}), bf16[4,864,128]{2,1,0:T(8,128)(2,1)}, u32[]{:S(2)}, u32[]{:S(2)}) async-start(bf16[4,864,128]{2,1,0:T(8,128)(2,1)} %copy-done.35), calls=%async_computation.17 | async-start | bytes 1769472 | tf_op jit(solution)/shard_map/all_to_all | solution.py:419
  452.7 17.0 %all-to-all-start.15 = ((bf16[4,864,128]{2,1,0:T(8,128)(2,1)}), bf16[4,864,128]{2,1,0:T(8,128)(2,1)}, u32[]{:S(2)}, u32[]{:S(2)}) async-start(bf16[4,864,128]{2,1,0:T(8,128)(2,1)} %get-tuple-element.122), calls=%async_computation.15 | async-start | bytes 1769472 | tf_op jit(solution)/shard_map/all_to_all | solution.py:419
  469.7 21.5 %all-to-all-start.12 = ((bf16[4,6,49,512]{3,2,1,0:T(8,128)(2,1)}), bf16[4,6,49,512]{3,2,1,0:T(8,128)(2,1)S(1)}, u32[]{:S(2)}, u32[]{:S(2)}) async-start(bf16[4,6,49,512]{3,2,1,0:T(8,128)(2,1)} %copy.112), calls=%async_computation.12 | async-start | bytes 2752512 | tf_op jit(solution)/shard_map/all_to_all | solution.py:419
  491.2 26.6 %all-to-all-start.16 = ((bf16[8,432,128]{2,1,0:T(8,128)(2,1)}), bf16[8,432,128]{2,1,0:T(8,128)(2,1)}, u32[]{:S(2)}, u32[]{:S(2)}) async-start(bf16[8,432,128]{2,1,0:T(8,128)(2,1)} %bitcast.126), calls=%async_computation.16 | async-start | bytes 1769472 | tf_op jit(solution)/shard_map/all_to_all | solution.py:419
  517.8 64.2 %all-to-all-start.14 = ((bf16[8,144,1152]{2,1,0:T(8,128)(2,1)}), bf16[8,144,1152]{2,1,0:T(8,128)(2,1)}, u32[]{:S(2)}, u32[]{:S(2)}) async-start(bf16[8,144,1152]{2,1,0:T(8,128)(2,1)} %weight_1.1), calls=%async_computation.14 | async-start | bytes 5308416 | tf_op jit(solution)/shard_map/all_to_all | solution.py:419
  582.0 64.0 %all-to-all-start.13 = ((bf16[8,144,1152]{2,1,0:T(8,128)(2,1)}), bf16[8,144,1152]{2,1,0:T(8,128)(2,1)S(1)}, u32[]{:S(2)}, u32[]{:S(2)}) async-start(bf16[8,144,1152]{2,1,0:T(8,128)(2,1)} %weight_0.1), calls=%async_computation.13 | async-start | bytes 5308416 | tf_op jit(solution)/shard_map/all_to_all | solution.py:419
  (94 other events, 951.7 us)
Sparse Core Ops, SparseCore 0:
  9.6 21.2 all-gather.5
  33.6 55.1 all-gather.7
  91.6 54.6 all-gather.9

commit v3 on v2

v3 whole, which is shorter than its diff:
```python
import functools

import jax
import jax.numpy as jnp
from jax import lax
from jax.experimental import pallas as pl
from jax.experimental.pallas import tpu as pltpu
from jax.sharding import PartitionSpec as P

STEP = 5
NORM_EPS = 1e-05
ADAM_EPS = 1e-08
BETA_ONE = 0.5
BETA_TWO = 0.5
RATE_WEIGHT = 0.015
RATE_NORM = 0.2
DECAY = 0.05
BF = jnp.bfloat16
F32 = jnp.float32
MIB = 1 << 20
VMEM = pl.BlockSpec(memory_space=pltpu.VMEM)
SMEM = pl.BlockSpec(memory_space=pltpu.SMEM)
LANES = 128


def shape(dims, dtype):
    return jax.ShapeDtypeStruct(tuple(dims), dtype)


def run(body, outs, args, name, scratch=(), limit=24, scalars=0, flops=0, moved=0, after=()):
    def kernel(*refs):
        body(*refs[len(after) :])

    return pl.pallas_call(
        kernel,
        out_shape=tuple(outs),
        in_specs=[pl.BlockSpec(memory_space=pl.ANY)] * len(after) + [SMEM] * scalars + [VMEM] * (len(args) - scalars),
        out_specs=tuple(VMEM for _ in outs),
        scratch_shapes=list(scratch),
        compiler_params=pltpu.CompilerParams(vmem_limit_bytes=limit * MIB),
        cost_estimate=pl.CostEstimate(flops=30 * flops, bytes_accessed=30 * moved, transcendentals=0),
        name=name,
    )(*after, *args)


def sigmoid(v):
    return 1.0 / (1.0 + jnp.exp(-v))


def silu(v):
    return v / (1.0 + jnp.exp(-v))


def silu_slope(v):
    s = sigmoid(v)
    return s * (1.0 + v * (1.0 - s))


def mm(a, b, dims):
    return lax.dot_general(a, b, (dims, ((), ())), preferred_element_type=F32)


def put_moments(values, out_ref):
    rows = values.shape[0]
    mean = jnp.sum(values, axis=0, keepdims=True) * (1.0 / rows)
    off = values - mean
    out_ref[0:1, :] = mean
    out_ref[1:2, :] = jnp.sum(off * off, axis=0, keepdims=True)


def joined_moments(both, rows):
    count = both.shape[0]
    mean = jnp.sum(both[:, 0:1], axis=0) * (1.0 / count)
    off = both[:, 0:1] - mean[None]
    total = jnp.sum(both[:, 1:2] + rows * (off * off), axis=0)
    return mean, lax.rsqrt(total * (1.0 / (rows * count)) + NORM_EPS)


def put_sums(upstream, normed, out_ref):
    out_ref[0:1, :] = jnp.sum(upstream * normed, axis=0, keepdims=True)
    out_ref[1:2, :] = jnp.sum(upstream, axis=0, keepdims=True)


def convolve(pad, w_ref, acc_ref, dims):
    height, width, frames, depth = dims
    rows = height * width * frames

    for k in range(9):
        i, j = k // 3, k % 3
        piece = pad[i : i + height, j : j + width].reshape(rows, depth).astype(BF)
        part = mm(piece, w_ref[:, k * depth : (k + 1) * depth], ((1,), (1,)))
        if k == 0:
            acc_ref[...] = part
        else:
            acc_ref[...] += part


def widened(scr, values, before, after):
    frames = values.shape[1]
    scr[:, 8 : 8 + frames, :] = values
    scr[:, 7:8, :] = before
    scr[:, 8 + frames : 9 + frames, :] = after


RING = (0, 2, 4, 6, 7, 5, 3, 1)


def can_ring(mid, k, k_t, count):
    return count == len(RING) and mid == 288 and k == 576 and k_t == 432


def ring_place(frame):
    return jnp.where(frame % 2 == 0, frame // 2, 7 - frame // 2)


def ring_device(place):
    place = place % 8
    return jnp.where(place < 4, 2 * place, 15 - 2 * place)


def low_half(shape_):
    return lax.broadcasted_iota(jnp.int32, shape_, 1) < LANES // 2


def fold(top, bottom, out_ref, k):
    edge = k - LANES // 2
    out_ref[:, 0:edge] = top[:, 0:edge].astype(out_ref.dtype)
    mixed = jnp.where(low_half((top.shape[0], LANES)), top[:, edge : edge + LANES], bottom[:, 0:LANES])
    out_ref[:, edge : edge + LANES] = mixed.astype(out_ref.dtype)
    out_ref[:, edge + LANES : 2 * k] = bottom[:, LANES : k + LANES // 2].astype(out_ref.dtype)


def pack_body(w_ref, t_ref, *refs):
    outs, scr = refs[:-1], refs[-1]
    units, mid, k = w_ref.shape
    half = mid // 2
    for u in range(units):
        scr[:, 0:k] = w_ref[u]
        fold(scr[0:half, :], pltpu.roll(scr[half:mid, :], LANES // 2, 1), outs[u].at[0:half], k)
        rows = outs[u].shape[0] - half
        for i in range(2 * k // LANES):
            at = slice(i * LANES, (i + 1) * LANES)
            outs[u][half:, at] = t_ref[u, rows * i : rows * (i + 1), :].astype(BF)


def unpack_temporal(f, slot, t_ref):
    rows = slot.shape[0]
    per = t_ref.shape[3] // rows
    for j in range(slot.shape[1] // LANES):
        block = 3 * f + j // per
        piece = slot[:, j * LANES : (j + 1) * LANES]
        t_ref[(block % 8) // 2, block // 8, block % 2, (j % per) * rows : (j % per + 1) * rows, :] = piece


def unpack_body(ids_ref, *refs):
    slots, outs = refs[:8], refs[-2:] if len(refs) == 10 else refs[9:]
    w_ref, t_ref = outs[:2]
    if len(outs) > 2:
        outs[2][...] = refs[8][...]
    half, k = w_ref.shape[0] // 2, w_ref.shape[1] // 8
    edge, wide = k - LANES // 2, k + LANES // 2
    for i, slot in enumerate(slots):
        f = ids_ref[6 + i]
        base = (f // 2) * (2 * k)
        values = slot[0:half, :].astype(F32)
        low = low_half((half, LANES))

        def at(start, size):
            return pl.ds(pl.multiple_of(base + start, LANES), size)

        @pl.when(f % 2 == 0)
        def _():
            for start, part in ((0, values[:, 0:wide]), (half, pltpu.roll(values[:, edge:], k, 1))):
                rows = slice(start, start + half)
                w_ref[rows, at(0, edge)] = part[:, 0:edge].astype(BF)
                old = w_ref[rows, at(edge, LANES)].astype(F32)
                w_ref[rows, at(edge, LANES)] = jnp.where(low, part[:, edge:wide], old).astype(BF)

        @pl.when(f % 2 == 1)
        def _():
            for start, part in ((0, pltpu.roll(values[:, 0:wide], LANES // 2, 1)), (half, values[:, edge:])):
                rows = slice(start, start + half)
                old = w_ref[rows, at(edge, LANES)].astype(F32)
                w_ref[rows, at(edge, LANES)] = jnp.where(low, old, part[:, 0:LANES]).astype(BF)
                w_ref[rows, at(edge + LANES, edge)] = part[:, LANES:wide].astype(BF)

        unpack_temporal(f, slot.at[half:], t_ref)


def spatial_body(act_ref, w_ref, s_ref, pad, *, dims):
    height, width, frames, depth = dims
    pad[...] = jnp.zeros(pad.shape, F32)
    pad[1 : height + 1, 1 : width + 1] = act_ref[...].astype(F32).reshape(dims)
    convolve(pad, w_ref, s_ref, dims)


def moments_body(s_ref, first_ref, last_ref, mom_ref, *, dims):
    put_spatial(s_ref, first_ref, last_ref, mom_ref, dims)


def put_spatial(s_ref, first_ref, last_ref, mom_ref, dims):
    height, width, frames, depth = dims
    values = s_ref[...]
    put_moments(values, mom_ref)
    grid = values.reshape(height * width, frames, values.shape[-1])
    first_ref[...] = grid[:, 0:1, :]
    last_ref[...] = grid[:, frames - 1 : frames, :]


def next_body(
    ids_ref, t0, t1, t2, t3, both_ref, norm_ref, w_ref,
    s_ref, first_ref, last_ref, mom_ref, act_ref, pad, *, dims
):
    height, width, frames, depth = dims
    rows = height * width * frames
    pad[...] = jnp.zeros(pad.shape, F32)
    for j, t_ref in enumerate((t0, t1, t2, t3)):
        b = ids_ref[j]
        mean, inverse = joined_moments(both_ref[:, b], rows)
        norm = norm_ref[b]
        y = (t_ref[...].astype(F32) - mean) * (inverse * norm[0:1]) + norm[1:2]
        a = silu(y)
        at = pl.ds(pl.multiple_of(b * LANES, LANES), LANES)
        act_ref[:, at] = a.astype(BF)
        pad[1 : height + 1, 1 : width + 1, :, at] = a.reshape(height, width, frames, LANES)
    convolve(pad, w_ref, s_ref, dims)
    put_spatial(s_ref, first_ref, last_ref, mom_ref, dims)


def temporal_body(
    ids_ref, s_ref, both_ref, before_ref, after_ref, norm_ref, keep_ref, w_ref,
    send_ref, kept_ref, win_ref, stat_ref, row_ref, scr, part, *, dims
):
    height, width, frames, depth = dims
    pixels = height * width
    rows = pixels * frames
    mid = s_ref.shape[-1]
    mean, inverse = joined_moments(both_ref[...], rows)
    stat_ref[0:1, :] = mean
    stat_ref[1:2, :] = inverse
    scale, bias = inverse * norm_ref[0:1], norm_ref[1:2]

    def active(v):
        return silu((v - mean) * scale + bias)

    middle = active(s_ref[...])
    widened(
        scr, middle.reshape(pixels, frames, mid),
        active(before_ref[...].reshape(pixels, mid)).reshape(pixels, 1, mid),
        active(after_ref[...].reshape(pixels, mid)).reshape(pixels, 1, mid),
    )
    win_ref[0] = (scr[:, 7 : 7 + frames, :] * keep_ref[0][None]).reshape(rows, mid).astype(BF)
    win_ref[1] = middle.astype(BF)
    win_ref[2] = (scr[:, 9 : 9 + frames, :] * keep_ref[1][None]).reshape(rows, mid).astype(BF)
    for r in range(w_ref.shape[0]):
        row_ref[:, :, r * LANES : (r + 1) * LANES] = w_ref[r]
    part[...] = mm(win_ref[0], row_ref[0], ((1,), (0,)))
    part[...] += mm(win_ref[1], row_ref[1], ((1,), (0,)))
    part[...] += mm(win_ref[2], row_ref[2], ((1,), (0,)))
    put_halves(ids_ref, part, send_ref, kept_ref)


def put_halves(ids_ref, part, send_ref, kept_ref):
    core = ids_ref[4]
    for i in range(2):
        other = pl.multiple_of((2 * i + 1 - core) * LANES, LANES)
        own = pl.multiple_of((2 * i + core) * LANES, LANES)
        send_ref[i] = part[:, pl.ds(other, LANES)].astype(BF)
        kept_ref[i] = part[:, pl.ds(own, LANES)]


def total_body(ids_ref, got_ref, kept_ref, last_ref, t_ref, low_ref, mom_ref):
    x = ids_ref[5]
    t = got_ref[x].astype(F32) + kept_ref[x] + last_ref[...].astype(F32)
    t_ref[...] = t
    low_ref[...] = t.astype(BF)
    put_moments(t, mom_ref)


def edges_body(*refs, dims):
    height, width, frames, depth = dims
    blocks, (first_ref, last_ref) = refs[:-2], refs[-2:]
    for j, ref in enumerate(blocks):
        grid = ref[...].astype(F32).reshape(height * width, frames, LANES)
        first_ref[j] = grid[:, 0:1, :]
        last_ref[j] = grid[:, frames - 1 : frames, :]


def top_body(ids_ref, t_ref, both_ref, norm_ref, x_ref, cot_ref, block_ref, g_ref, low_ref, sums_ref):
    rows = t_ref.shape[0]
    b = ids_ref[0]
    mean, inverse = joined_moments(both_ref[:, b], rows)
    norm = norm_ref[b]
    normed = (t_ref[...] - mean) * inverse
    own = pl.ds(pl.multiple_of(b * LANES, LANES), LANES)
    summed = normed * norm[0:1] + norm[1:2] + x_ref[:, own].astype(F32)
    block_ref[...] = silu(summed).astype(BF)
    g = cot_ref[...].astype(F32) * silu_slope(summed)
    g_ref[...] = g
    low_ref[...] = g.astype(BF)
    put_sums(g, normed, sums_ref)


def below_body(ids_ref, got_ref, kept_ref, last_ref, t_ref, both_ref, norm_ref, low_ref, sums_ref):
    rows = t_ref.shape[0]
    b, x = ids_ref[0], ids_ref[5]
    d_act = got_ref[x].astype(F32) + kept_ref[x] + last_ref[...].astype(F32)
    mean, inverse = joined_moments(both_ref[:, b], rows)
    norm = norm_ref[b]
    normed = (t_ref[...] - mean) * inverse
    g = d_act * silu_slope(normed * norm[0:1] + norm[1:2])
    low_ref[...] = g.astype(BF)
    put_sums(g, normed, sums_ref)


def dt_body(
    ids_ref, g0, g1, g2, g3, t0, t1, t2, t3, both_ref, sums_ref, norm_ref, win_ref,
    dt_ref, coef_ref, grad_ref, sum_ref, *, total
):
    rows = g0.shape[0]
    mid = win_ref.shape[-1]
    n_r = norm_ref.shape[0]
    for j, (g_ref, t_ref) in enumerate(((g0, t0), (g1, t1), (g2, t2), (g3, t3))):
        b = ids_ref[j]
        mean, inverse = joined_moments(both_ref[:, b], rows)
        sums = jnp.sum(sums_ref[:, b], axis=0)
        if j == 0:
            sum_ref[...] = sums
        c1 = norm_ref[b][0:1] * inverse
        c2 = c1 * sums[1:2] * (1.0 / total)
        c3 = c1 * inverse * sums[0:1] * (1.0 / total)
        coef_ref[j] = jnp.concatenate([c1, c2, c3, mean], axis=0)
        d = c1 * g_ref[...].astype(F32) - c2 - c3 * (t_ref[...].astype(F32) - mean)
        dt_ref[:, pl.ds(pl.multiple_of(b * LANES, LANES), LANES)] = d.astype(BF)
    dt = dt_ref[...]
    for k in range(3):
        term = mm(win_ref[k], dt, ((0,), (0,)))
        for r in range(n_r):
            grad_ref[r, k * mid : (k + 1) * mid, :] = term[:, r * LANES : (r + 1) * LANES].astype(BF)


def middle_body(
    ids_ref, dt_ref, coef_ref, before_ref, after_ref, keep_ref, w_ref, s_ref, stat_ref, norm_ref,
    d_ref, sums_ref, scr, *, dims
):
    height, width, frames, depth = dims
    pixels = height * width
    rows = pixels * frames
    scr[:, 8 : 8 + frames, :] = dt_ref[...].astype(F32).reshape(pixels, frames, depth)
    for j in range(4):
        at = pl.ds(pl.multiple_of(ids_ref[j] * LANES, LANES), LANES)
        c = coef_ref[j]

        def halo(g, t):
            d = c[0:1] * g.reshape(pixels, LANES) - c[1:2] - c[2:3] * (t.reshape(pixels, LANES) - c[3:4])
            return d.astype(BF).astype(F32).reshape(pixels, 1, LANES)

        scr[:, 7:8, at] = halo(before_ref[j], before_ref[4 + j])
        scr[:, 8 + frames : 9 + frames, at] = halo(after_ref[j], after_ref[4 + j])
    later = (scr[:, 9 : 9 + frames, :] * keep_ref[1][None]).reshape(rows, depth).astype(BF)
    earlier = (scr[:, 7 : 7 + frames, :] * keep_ref[0][None]).reshape(rows, depth).astype(BF)
    d_ref[...] = mm(later, w_ref[0], ((1,), (1,)))
    d_ref[...] += mm(dt_ref[...], w_ref[1], ((1,), (1,)))
    d_ref[...] += mm(earlier, w_ref[2], ((1,), (1,)))
    normed = (s_ref[...] - stat_ref[0:1]) * stat_ref[1:2]
    d = d_ref[...] * silu_slope(normed * norm_ref[0:1] + norm_ref[1:2])
    d_ref[...] = d
    put_sums(d, normed, sums_ref)


def spatial_grad(d_ref, s_ref, stat_ref, norm_ref, sums_ref, ds_ref, sum_ref, total):
    sums = jnp.sum(sums_ref[...], axis=0)
    sum_ref[...] = sums
    inverse = stat_ref[1:2]
    normed = (s_ref[...] - stat_ref[0:1]) * inverse
    d = d_ref[...] - sums[1:2] * (1.0 / total) - normed * (sums[0:1] * (1.0 / total))
    ds_ref[...] = (norm_ref[0:1] * inverse * d).astype(BF)


def adjoint(ds_ref, w_ref, pad, dims):
    height, width, frames, depth = dims
    pad[...] = jnp.zeros(pad.shape, F32)

    for k in range(9):
        part = mm(ds_ref[...], w_ref[:, k * depth : (k + 1) * depth], ((1,), (0,)))
        at = (slice(k // 3, k // 3 + height), slice(k % 3, k % 3 + width))
        pad[at] = pad[at] + part.reshape(dims)


def input_body(
    ids_ref, d_ref, s_ref, stat_ref, norm_ref, sums_ref, w_ref,
    ds_ref, send_ref, kept_ref, sum_ref, pad, part, *, dims, total
):
    height, width, frames, depth = dims
    spatial_grad(d_ref, s_ref, stat_ref, norm_ref, sums_ref, ds_ref, sum_ref, total)
    adjoint(ds_ref, w_ref, pad, dims)
    part[...] = pad[1 : height + 1, 1 : width + 1].reshape(part.shape)
    put_halves(ids_ref, part, send_ref, kept_ref)


def by_frame(source, out_ref, dims):
    height, width, frames, depth = dims
    pixels, own = height * width, out_ref.shape[1]
    for r in range(source.shape[0]):
        for f in range(frames):
            values = source[r, pl.ds(f, pixels, stride=frames), :]
            out_ref[f // own, f % own, :, r * LANES : (r + 1) * LANES] = values.astype(out_ref.dtype)


def last_body(ids_ref, ds_ref, w_ref, g_ref, block_ref, out_ref, block_out_ref, pad, part, block, *, dims):
    height, width, frames, depth = dims
    block[0] = block_ref[...].astype(F32)
    by_frame(block, block_out_ref, dims)
    adjoint(ds_ref, w_ref, pad, dims)
    own = ids_ref[0]
    for r in range(part.shape[0]):
        columns = pad[1 : height + 1, 1 : width + 1, :, r * LANES : (r + 1) * LANES]
        part[r] = columns.reshape(part.shape[1:])
    part[own] = part[own] + g_ref[...]
    by_frame(part, out_ref, dims)


def finish_body(*refs):
    block_ref, grad_ref, out_ref, grad_out_ref = refs
    own, height, width, depth = out_ref.shape
    for f in range(own):
        block = jnp.concatenate([block_ref[r, f].astype(F32) for r in range(4)], axis=1)
        grad = sum(grad_ref[r, f].astype(F32) for r in range(4))
        for h in range(height):
            at = slice(h * width, (h + 1) * width)
            out_ref[f, h] = block[at].astype(BF)
            grad_out_ref[f, h] = grad[at]


def weight_terms(act_ref, ds_ref, pad, acc, dims):
    height, width, frames, depth = dims
    rows = height * width * frames
    pad[...] = jnp.zeros(pad.shape, F32)
    pad[1 : height + 1, 1 : width + 1] = act_ref[...].astype(F32).reshape(dims)
    flipped = ds_ref[...].astype(F32).T.astype(BF)

    for k in range(9):
        i, j = k // 3, k % 3
        piece = pad[i : i + height, j : j + width].reshape(rows, depth).astype(BF)
        acc[:, k * depth : (k + 1) * depth] = mm(flipped, piece, ((1,), (0,)))


def put_shards(acc, places, out_ref, k):
    mid = acc.shape[0]
    half = mid // 2
    wide = k + LANES // 2
    for f in range(8):
        if f % 2 == 0:
            top = acc[0:half, k * f : k * f + wide]
            bottom = pltpu.roll(acc[half:mid, k * f : k * f + wide], LANES // 2, 1)
        else:
            start = k * f - LANES // 2
            top = pltpu.roll(acc[0:half, start : start + wide], k, 1)
            bottom = acc[half:mid, start : start + wide]
        fold(top, bottom, out_ref.at[places[f], 0:half], k)


def weight_plain_body(act_ref, ds_ref, out_ref, pad, acc, *, dims):
    weight_terms(act_ref, ds_ref, pad, acc, dims)
    out_ref[...] = acc[...].astype(BF)


def put_temporal(t_ref, places, out_ref, half):
    rows = out_ref.shape[1] - half
    per = half // rows
    for block in range(24):
        tap, r, part = block // 8, (block % 8) // 2, block % 2
        for j in range(per):
            start = tap * 2 * half + part * half + j * rows
            at = (block % 3) * per + j
            out_ref[places[block // 3], half:, at * LANES : (at + 1) * LANES] = t_ref[r, start : start + rows, :]


def weight_body(ids_ref, act_ref, ds_ref, t_ref, out_ref, ahead_ref, back_ref, pad, acc, *, dims):
    weight_terms(act_ref, ds_ref, pad, acc, dims)
    places = [ids_ref[14 + f] for f in range(8)]
    put_shards(acc, places, out_ref, acc.shape[1] // 8)
    put_temporal(t_ref, places, out_ref, acc.shape[0] // 2)
    ahead_ref[...] = out_ref[4]
    back_ref[...] = out_ref[5]


def weight_first_body(
    ids_ref, act_ref, d_ref, s_ref, stat_ref, norm_ref, sums_ref, t_ref, mid_ref, out_1_ref, out_0_ref,
    ds_ref, flat_ref, out_ref, ahead_ref, back_ref, sum_ref, pad, acc, *, dims, total
):
    spatial_grad(d_ref, s_ref, stat_ref, norm_ref, sums_ref, ds_ref, sum_ref, total)
    for r in range(flat_ref.shape[0]):
        flat_ref[r] = jnp.zeros(flat_ref.shape[1:], F32)
        for i, ref in enumerate((sum_ref, mid_ref, out_0_ref, out_1_ref)):
            flat_ref[r, 2 * i : 2 * i + 2, 0 : ref.shape[1]] = ref[...]
    weight_body(ids_ref, act_ref, ds_ref, t_ref, out_ref, ahead_ref, back_ref, pad, acc, dims=dims)


def norm_body(flat_ref, *refs):
    count = flat_ref.shape[0]
    for which in range(2):
        old, new = refs[3 * which : 3 * which + 3], refs[6 + 3 * which : 9 + 3 * which]
        width = old[0].shape[-1] // count
        for u in range(2):
            row = 4 * which + 2 * u
            grad = jnp.concatenate([flat_ref[r, row : row + 2, 0:width] for r in range(count)], axis=1)
            values = adam_step(old[0][u], grad, old[1][u], old[2][u], RATE_NORM, 0.0)
            for ref, value in zip(new, values):
                ref[u] = value


def adam_step(param, gradient, moment_one, moment_two, rate, decay):
    first_new = BETA_ONE * moment_one + (1.0 - BETA_ONE) * gradient
    second_new = BETA_TWO * moment_two + (1.0 - BETA_TWO) * gradient * gradient
    fix_one = 1.0 - BETA_ONE**STEP
    fix_two = 1.0 - BETA_TWO**STEP
    update = first_new / fix_one / (jnp.sqrt(second_new / fix_two) + ADAM_EPS)
    return (param - rate * (update + decay * param), first_new, second_new)


def adam_into(grad, refs, outs, rows):
    new, first, second = adam_step(refs[0][0, rows], grad, refs[1][0, rows], refs[2][0, rows], RATE_WEIGHT, DECAY)
    outs[0][0, rows] = new
    outs[1][0, rows] = first
    outs[2][0, rows] = second
    outs[3][0, rows] = new.astype(BF)


def adam_body(*refs, grads):
    sources, refs = refs[:grads], refs[grads:]
    refs, outs = refs[:6], refs[-8:]
    summed = sum(r[...].astype(F32) for r in sources)
    half = refs[0].shape[1] // 2
    spatial, temporal = summed[0:half], summed[half:]
    rows = temporal.shape[0]
    for i in range(temporal.shape[1] // LANES):
        piece = temporal[:, i * LANES : (i + 1) * LANES]
        adam_into(piece, refs[3:], outs[4:], slice(i * rows, (i + 1) * rows))
    half, double = spatial.shape
    k = double // 2
    edge = k - LANES // 2
    adam_into(spatial[:, 0:k], refs, outs, slice(0, half))
    adam_into(pltpu.roll(spatial[:, edge:], k, 1)[:, 0:k], refs, outs, slice(half, 2 * half))


def adam_unit(u, sources, state, before, name, after=()):
    unit = [pl.BlockSpec((1,) + a.shape[1:], lambda i: (u, 0, 0)) for a in state]
    types = [F32, F32, F32, BF]
    outs = [shape(state[0].shape, t) for t in types] + [shape(state[3].shape, t) for t in types]
    before = list(before or ())
    whole = [pl.BlockSpec(a.shape, lambda i, n=a.ndim: (0,) * n) for a in sources]

    def kernel(*refs):
        adam_body(*refs[len(after) :], grads=len(sources))

    return pl.pallas_call(
        kernel,
        grid=(1,),
        out_shape=tuple(outs),
        in_specs=[pl.BlockSpec(memory_space=pl.ANY)] * len(after) + whole + unit + [pl.BlockSpec(memory_space=pl.ANY)] * len(before),
        out_specs=tuple([unit[0]] * 4 + [unit[3]] * 4),
        input_output_aliases={len(after) + len(sources) + 6 + i: i for i in range(len(before))},
        compiler_params=pltpu.CompilerParams(vmem_limit_bytes=40 * MIB),
        name=name,
    )(*after, *sources, *state, *before)


def swap(parts, axis):
    return lax.all_to_all(parts, axis, 0, 0, tiled=True)


def from_all(value, axis):
    count = lax.axis_size(axis)
    return swap(jnp.broadcast_to(value[None], (count,) + value.shape), axis)


def across(value, bit):
    count = lax.axis_size("rep")
    return lax.ppermute(value, "rep", [(i, i ^ bit) for i in range(count)])


def from_group(value):
    far = across(value, 2)
    near = across(value, 1)
    return value, far, near, across(far, 1)


def neighbours(first, last):
    count = lax.axis_size("frames")
    before = lax.ppermute(last, "frames", [(i, i + 1) for i in range(count - 1)])
    after = lax.ppermute(first, "frames", [(i + 1, i) for i in range(count - 1)])
    return before, after


def along(step):
    return [(RING[i], RING[(i + step) % 8]) for i in range(8)]


def ring_gather(own):
    ahead, back = [own], [own]
    for step in range(4):
        ahead.append(lax.ppermute(ahead[-1], "frames", along(1)))
        if step < 3:
            back.append(lax.ppermute(back[-1], "frames", along(-1)))
    return ahead + back[1:], list(zip(ahead[1:4], back[1:]))


def ring_sums(parts, ahead, back):
    def plus(got, part):
        return (got.astype(F32) + part.astype(F32)).astype(BF)

    steps = []
    for i in (3, 2, 1):
        ahead = plus(lax.ppermute(ahead, "frames", along(1)), parts[i])
        if i > 1:
            back = plus(lax.ppermute(back, "frames", along(-1)), parts[9 - i])
        steps.append((ahead, back))
    ends = [parts[0], lax.ppermute(ahead, "frames", along(1)), lax.ppermute(back, "frames", along(-1))]
    return ends, steps


def reduced(send, kept, x):
    got = across(send, 1)
    away = lax.dynamic_index_in_dim(got, 1 - x, 0, False).astype(F32)
    away = away + lax.dynamic_index_in_dim(kept, 1 - x, 0, False)
    return got, kept, across(away.astype(BF), 2)


def ordered(t_grad, count):
    n_r, rows, cols = t_grad.shape
    return t_grad.reshape(n_r, 3, rows // 3, cols).transpose(1, 0, 2, 3).reshape(count, -1, cols)


def sum_over(parts, axis):
    return jnp.sum(swap(parts, axis).astype(F32), axis=0)


def on_device(
    frames_in, cotangent, lengths,
    spatial_weights, spatial_first, spatial_second,
    temporal_weights, temporal_first, temporal_second,
    mid_norm, mid_first, mid_second,
    out_norm, out_first, out_second,
):
    own_frames, height, width, depth = frames_in.shape
    n_f, n_r = lax.axis_size("frames"), lax.axis_size("rep")
    assert n_r == 4 and depth == n_r * LANES
    me = lax.axis_index("rep")
    frames = own_frames * n_r
    pixels = height * width
    rows = pixels * frames
    total = float(rows * n_f)
    dims = (height, width, frames, depth)
    units, k, mid = spatial_weights.shape
    cols = LANES
    everyone = ("frames", "rep")
    k_t = temporal_weights.shape[1]
    ring = can_ring(mid, k, k_t, n_f)
    spatial_flops = 2 * rows * 9 * depth * mid
    temporal_flops = 2 * rows * 3 * depth * mid
    pad = pltpu.VMEM((height + 2, width + 2, frames, depth), F32)
    flip = functools.partial(jnp.swapaxes, axis1=1, axis2=2)
    ids = [me, me ^ 2, me ^ 1, me ^ 3, me & 1, me >> 1]
    if ring:
        place = ring_place(lax.axis_index("frames"))
        ids += [ring_device(place + i) for i in (0, -1, -2, -3, -4, 1, 2, 3)]
        ids += [(ring_place(jnp.int32(f)) - place) % 8 for f in range(8)]
    ids = jnp.stack(ids).astype(jnp.int32)

    frame_ids = lax.axis_index("frames") * frames + jnp.arange(frames, dtype=jnp.int32)
    clip_ends = jnp.cumsum(lengths)
    starts = jnp.concatenate([jnp.zeros((1,), jnp.int32), clip_ends[:-1]])
    opening = jnp.any(frame_ids[:, None] == starts[None, :], axis=1)
    closing = jnp.any((frame_ids + 1)[:, None] == clip_ends[None, :], axis=1)
    keep = jnp.where(jnp.stack([opening, closing]), 0.0, 1.0).astype(F32)[:, :, None]

    act = lax.all_gather(frames_in, "rep", axis=0, tiled=True).transpose(1, 2, 0, 3).reshape(rows, depth)
    cot = cotangent.reshape(own_frames, pixels, n_r, cols).transpose(2, 0, 1, 3)
    cot = swap(cot, "rep").reshape(frames, pixels, cols).transpose(1, 0, 2).reshape(rows, cols)

    mid_own = lax.dynamic_slice_in_dim(mid_norm, me * mid, mid, axis=2)
    out_split = out_norm.reshape(units, 2, n_r, cols).transpose(0, 2, 1, 3)

    spatial_w, temporal_w, steps = [], [], [(), (), ()]
    if ring:
        wire = shape((mid // 2 + k_t * LANES // (2 * k), 2 * k), BF)
        w_shape, t_shape = shape((mid, n_f * k), BF), shape((n_r, 3, 2, mid // 2, cols), BF)
        wires = run(
            pack_body, [wire] * units, [flip(spatial_weights), temporal_weights], "pack",
            [pltpu.VMEM((mid, k + LANES // 2), F32)],
        )
        held, _ = ring_gather(wires[0])
        w, t, *waiting = run(
            unpack_body, [w_shape, t_shape] + [wire] * (units - 1), [ids, *held, *wires[1:]], "unpack_0", scalars=1,
            after=[act, cot, keep, mid_own, out_split],
        )
        spatial_w.append(w)
        temporal_w.append(swap(t, "rep").reshape(n_r, 3, mid, cols))
        for u in range(1, units):
            held, steps = ring_gather(waiting[u - 1])
            w, t = run(unpack_body, [w_shape, t_shape], [ids, *held], f"unpack_{u}", scalars=1)
            spatial_w.append(w)
            temporal_w.append(swap(t, "rep").reshape(n_r, 3, mid, cols))
    else:
        wire = flip(spatial_weights).astype(BF)
        temporal_low = temporal_weights.astype(BF)
        for u in range(units):
            held = lax.all_gather(wire[u], "frames", axis=0)
            spatial_w.append(held.transpose(1, 0, 2).reshape(mid, n_f * k))
            shard = lax.all_gather(temporal_low[u], "frames", axis=0, tiled=True)
            shard = shard.reshape(3, n_r, mid, cols).transpose(1, 0, 2, 3)
            temporal_w.append(swap(shard, "rep"))

    halo = shape((pixels, 1, mid), F32)
    column = shape((rows, cols), BF)
    saved = []
    for u in range(units):
        outs = [shape((rows, mid), F32), halo, halo, shape((2, mid), F32)]
        if u == 0:
            (spatial,) = run(
                functools.partial(spatial_body, dims=dims), outs[:1], [act, spatial_w[u]],
                f"spatial_{u}", [pad], flops=spatial_flops, moved=8 * MIB,
            )
            first, last, mom = run(
                functools.partial(moments_body, dims=dims), outs[1:], [spatial], f"moments_{u}", moved=MIB,
                after=[temporal_w[0]],
            )
        else:
            spatial, first, last, mom, act = run(
                functools.partial(next_body, dims=dims), outs + [shape((rows, depth), BF)],
                [ids, *t_group, both, out_split[u - 1], spatial_w[u]],
                f"spatial_{u}", [pad], scalars=1, flops=spatial_flops, moved=8 * MIB,
            )
        mid_both = from_all(mom, "frames")
        before, after = neighbours(first, last)
        send, kept, window, stat, row_w = run(
            functools.partial(temporal_body, dims=dims),
            [shape((2, rows, cols), BF), shape((2, rows, cols), F32), shape((3, rows, mid), BF), shape((2, mid), F32),
             shape((3, mid, depth), BF)],
            [ids, spatial, mid_both, before, after, mid_own[u], keep, temporal_w[u]],
            f"temporal_{u}", [pltpu.VMEM((pixels, frames + 16, mid), F32), pltpu.VMEM((rows, depth), F32)],
            scalars=1, flops=temporal_flops, moved=8 * MIB, after=steps[1] if u == 0 else (),
        )
        t, low, mom = run(
            total_body, [shape((rows, cols), F32), column, shape((2, cols), F32)],
            [ids, *reduced(send, kept, me >> 1)], f"total_{u}", scalars=1, moved=3 * MIB,
            after=steps[2] if u == 0 else (),
        )
        both = from_all(mom, everyone).reshape(n_f, n_r, 2, cols)
        t_group = from_group(low)
        saved.append((act, spatial, stat, window, row_w, t, t_group, both))

    d_norms = [None] * units
    weight_parts = [None] * units
    pending = [()] * 4
    held_back = ()
    for u in reversed(range(units)):
        act, spatial, stat, window, row_w, t, t_group, both = saved[u]
        if u == units - 1:
            block, summed_grad, low, sums = run(
                top_body, [column, shape((rows, cols), F32), column, shape((2, cols), F32)],
                [ids, t, both, out_split[u], saved[0][0], cot], "top", scalars=1, moved=3 * MIB,
            )
        else:
            low, sums = run(
                below_body, [column, shape((2, cols), F32)],
                [ids, *reduced(send, kept, me >> 1), t, both, out_split[u]], f"below_{u}", scalars=1, moved=3 * MIB,
                after=pending[0],
            )
        sums = from_all(sums, everyone).reshape(n_f, n_r, 2, cols)
        g_group = from_group(low)
        edge = [shape((2 * n_r, pixels, 1, cols), F32)] * 2
        edges = neighbours(*run(functools.partial(edges_body, dims=dims), edge, g_group + t_group, f"edges_{u}", after=[sums]))
        dt, coef, t_grad, out_sums = run(
            functools.partial(dt_body, total=total),
            [shape((rows, depth), BF), shape((n_r, 4, cols), F32), shape((n_r, 3 * mid, cols), BF), shape((2, cols), F32)],
            [ids, *g_group, *t_group, both, sums, out_split[u], window],
            f"dt_{u}", scalars=1, flops=temporal_flops, moved=8 * MIB, after=pending[1],
        )
        t_grad = swap(t_grad, "rep")
        d_mid, sums = run(
            functools.partial(middle_body, dims=dims), [shape((rows, mid), F32), shape((2, mid), F32)],
            [ids, dt, coef, *edges, keep, row_w, spatial, stat, mid_own[u]],
            f"middle_{u}", [pltpu.VMEM((pixels, frames + 16, depth), F32)],
            scalars=1, flops=temporal_flops, moved=8 * MIB, after=pending[2],
        )
        sums = from_all(sums, "frames")
        ds_shape, sum_shape = shape((rows, mid), BF), shape((2, mid), F32)
        acc = pltpu.VMEM((mid, n_f * k), F32)
        grad_args = [d_mid, spatial, stat, mid_own[u], sums]
        if u > 0 or not ring:
            ds, send, kept, mid_sums = run(
                functools.partial(input_body, dims=dims, total=total),
                [ds_shape, shape((2, rows, cols), BF), shape((2, rows, cols), F32), sum_shape],
                [ids, *grad_args, spatial_w[u]],
                f"input_{u}", [pad, pltpu.VMEM((rows, depth), F32)], scalars=1, flops=spatial_flops, moved=8 * MIB,
                after=[t_grad],
            )
        if ring:
            slab = shape(wires[u].shape, BF)
            slabs = [shape((n_f,) + slab.shape, BF), slab, slab]
        if ring and u > 0:
            s_grad, ahead, back = run(
                functools.partial(weight_body, dims=dims), slabs, [ids, act, ds, t_grad],
                f"weight_{u}", [pad, acc], scalars=1, flops=spatial_flops, moved=8 * MIB,
            )
            weight_parts[u], sent = ring_sums(s_grad, ahead, back)
            pending = [[s_grad], sent[0], sent[1], weight_parts[u][1:]]
        elif ring:
            ds, flat, s_grad, ahead, back = run(
                functools.partial(weight_first_body, dims=dims, total=total),
                [ds_shape, shape((n_r, 8, 512), F32)] + slabs,
                [ids, act, *grad_args, t_grad, *d_norms[1], out_sums],
                f"weight_{u}", [pltpu.VMEM((2, mid), F32), pad, acc], scalars=1, flops=spatial_flops, moved=8 * MIB,
                after=pending[3],
            )
            weight_parts[u], sent = ring_sums(s_grad, ahead, back)
            held_back = sent[0]
        else:
            (s_grad,) = run(
                functools.partial(weight_plain_body, dims=dims), [shape((mid, n_f * k), BF)], [act, ds],
                f"weight_{u}", [pad, acc], flops=spatial_flops, moved=8 * MIB,
            )
            s_grad = swap(s_grad.reshape(mid, n_f, k).transpose(1, 0, 2), "frames")
            weight_parts[u] = (s_grad, swap(ordered(t_grad, n_f), "frames"))
        if u == 0:
            d_input, block = run(
                functools.partial(last_body, dims=dims),
                [shape((n_r, own_frames, pixels, depth), BF), shape((n_r, own_frames, pixels, cols), BF)],
                [ids, ds, spatial_w[u], summed_grad, block], "last",
                [pad, pltpu.VMEM((n_r, rows, cols), F32), pltpu.VMEM((1, rows, cols), F32)], scalars=1,
                flops=spatial_flops, moved=8 * MIB, after=held_back,
            )
        d_norms[u] = (mid_sums, out_sums)

    block_out, input_grad = run(
        finish_body, [shape(frames_in.shape, BF), shape(frames_in.shape, F32)],
        [swap(block, "rep"), swap(d_input, "rep")], "finish", moved=3 * MIB,
    )
    if ring:
        flat = swap(flat, "rep")
        norms = [mid_norm, mid_first, mid_second, out_norm, out_first, out_second]
        norms = run(norm_body, [shape(a.shape, F32) for a in norms], [flat, *norms], "norms")
    else:
        flat = jnp.concatenate([jnp.concatenate([m.reshape(-1), o.reshape(-1)]) for m, o in d_norms])
        flat = from_all(flat, "rep").reshape(n_r, units, -1)
        mid_grad = flat[:, :, : 2 * mid].reshape(n_r, units, 2, mid).transpose(1, 2, 0, 3)
        mid_grad = mid_grad.reshape(units, 2, n_r * mid)
        out_grad = flat[:, :, 2 * mid :].reshape(n_r, units, 2, cols).transpose(1, 2, 0, 3)
        out_grad = out_grad.reshape(units, 2, depth)
        norms = [*adam_step(mid_norm, mid_grad, mid_first, mid_second, RATE_NORM, 0.0)]
        norms += adam_step(out_norm, out_grad, out_first, out_second, RATE_NORM, 0.0)

    if ring:
        state = [flip(a) for a in (spatial_weights, spatial_first, spatial_second)]
        state += [temporal_weights, temporal_first, temporal_second]
        weights = None
        for u in reversed(range(units)):
            weights = adam_unit(u, weight_parts[u], state, weights, f"adam_{u}", held_back if u > 0 else ())
        weights = [flip(a) for a in weights[:4]] + list(weights[4:])
    else:
        grads = [jnp.stack([jnp.sum(parts[i].astype(F32), axis=0) for parts in weight_parts]) for i in range(2)]
        news = adam_step(spatial_weights, flip(grads[0]), spatial_first, spatial_second, RATE_WEIGHT, DECAY)
        weights = [*news, news[0].astype(BF)]
        news = adam_step(temporal_weights, grads[1], temporal_first, temporal_second, RATE_WEIGHT, DECAY)
        weights += [*news, news[0].astype(BF)]
    return (block_out, input_grad, *weights, *norms)


def solution(mesh):
    by_frame = P(("frames", "rep"), None, None, None)
    by_block = P(None, "frames", "rep")
    placed = (by_frame, by_frame, P()) + (by_block,) * 6 + (P(),) * 6
    return jax.shard_map(
        on_device,
        mesh=mesh,
        in_specs=placed,
        out_specs=(by_frame, by_frame) + (by_block,) * 8 + (P(),) * 6,
        check_vma=False,
    )
```

time: 668 us -> 485 us (0.73)
  waiting for transfers between devices: 232 us -> 154 us
  blocking collectives: 119 us -> 60.9 us
  local copies, waits for them, and re-layouts: 78.4 us -> 57.1 us
  starting transfers between devices: 108 us -> 93.9 us
  other arithmetic: 16.3 us -> 9.04 us
    all_to_all x17 -> x11, waiting for transfers between devices: 159 us -> 23.9 us  [swap(): return lax.all_to_all(parts, axis, 0, 0, tiled=True)]
    ppermute x0 -> x28, waiting for transfers between devices: none -> 91.1 us  [the longest x6 36 us: ring_sums(): ahead = plus(lax.ppermute(ahead, 'frames', along(1)), parts[i])]
    all_gather x2 -> x0, blocking collectives: 66.9 us -> none  [on_device(): shard = lax.all_gather(temporal_low[u], 'frames', axis=0, tiled=True)]
    all_gather x2 -> x0, waiting for transfers between devices: 35 us -> none  [on_device(): held = lax.all_gather(wire[u], 'frames', axis=0)]
    ppermute x0 -> x28, starting transfers between devices: none -> 28.4 us  [the longest x8 10.4 us: ring_gather(): ahead.append(lax.ppermute(ahead[-1], 'frames', along(1)))]
    all_to_all x17 -> x11, starting transfers between devices: 66.3 us -> 39.6 us  [swap(): return lax.all_to_all(parts, axis, 0, 0, tiled=True)]
    reshape x14 -> x1, local copies, waits for them, and re-layouts: 12 us -> 0.1 us  [the longest x2 3.5 us: on_device(): swap(t_grad, 'rep').reshape(n_r, 3, mid, cols).transpose(1, 0, 2, 3)]
    ppermute x6 -> x4, starting transfers between devices: 21.7 us -> 11.9 us  [neighbours(): lax.ppermute(last, 'frames', [(i, i + 1) for i in range(count - 1)])]
  transfers between devices with their start and end apart: 50 -> 66, of which waited for: 19 -> 31; matrix products, arithmetic and copies ran while one was open for 8% -> 3% of each run, Pallas kernels for 11% -> 7%
where the time goes in v3:
time: 485 us; the launch traced here: 478 us
  waiting for transfers between devices  154 us (32%)
  starting transfers between devices  93.9 us (19%)
  Pallas kernels  87 us (18%)
  blocking collectives  60.9 us (13%)
  local copies, waits for them, and re-layouts  57.1 us (12%)
  between operations  15.7 us (3%)
  other arithmetic  9.04 us (2%)
    pallas_call x24, Pallas kernels, run(): pl.pallas_call(kernel, out_shape=tuple(outs), in_specs=[pl.BlockSpec(memo...  82.5 us
    all_to_all x5, blocking collectives, swap(): return lax.all_to_all(parts, axis, 0, 0, tiled=True)  60.9 us
    unnamed x208, local copies, waits for them, and re-layouts  48.9 us
    all_to_all x11, starting transfers between devices, swap(): return lax.all_to_all(parts, axis, 0, 0, tiled=True)  39.6 us
    ppermute x6, waiting for transfers between devices, ring_sums(): ahead = plus(lax.ppermute(ahead, 'frames', along(1)), parts[i])  36 us
    ppermute x18, waiting for transfers between devices, across(): return lax.ppermute(value, 'rep', [(i, i ^ bit) for i in range(count)])  29 us
    ppermute x8, waiting for transfers between devices, ring_gather(): ahead.append(lax.ppermute(ahead[-1], 'frames', along(1)))  26.2 us
    all_to_all x11, waiting for transfers between devices, swap(): return lax.all_to_all(parts, axis, 0, 0, tiled=True)  23.9 us
  transfers between devices with their start and end apart: 66, of which 31 were waited for; matrix products, arithmetic and copies ran while one was open for 3% of the time, Pallas kernels for 7%

profile of v3, /device:TPU:0, one launch (start us, length us, event | category | flops | bytes accessed | tf_op | source)
XLA Modules:
  0.0 477.9 jit_solution(18321500406088940727)
XLA Ops:
  13.7 10.1 %collective-permute-done.refs_7_ = bf16[192,1152]{1,0:T(8,128)(2,1)S(1)} collective-permute-done((bf16[192,1152]{1,0:T(8,128)(2,1)S(1)}, bf16[192,1152]{1,0:T(8,128)(2,1)S(1)}, u32[]{:S(2)}, u32[]{:S(2)}) %collective-permute-start) | collective-permute-done | bytes 442400 | tf_op jit(solution)/shard_map/ppermute | solution.py:603
  25.8 9.4 %collective-permute-done.1.refs_8_ = bf16[192,1152]{1,0:T(8,128)(2,1)S(1)} collective-permute-done((bf16[192,1152]{1,0:T(8,128)(2,1)S(1)}, bf16[192,1152]{1,0:T(8,128)(2,1)S(1)}, u32[]{:S(2)}, u32[]{:S(2)}) %collective-permute-start.1) | collective-permute-done | bytes 442400 | tf_op jit(solution)/shard_map/ppermute | solution.py:603
  50.0 4.5 collective-permute-done.6.refs_13_
  67.2 4.6 collective-permute-done.10.refs_6_
  75.8 5.8 %spatial_0.1.refs_1_.refs_3_.refs_9_.refs_5_ = f32[1176,288]{1,0:T(8,128)S(1)} custom-call(bf16[1176,512]{1,0:T(8,128)(2,1)S(1)} %bitcast.102, bf16[288,4608]{1,0:T(8,128)(2,1)S(1)} %copy-done.74), custom_call_target="tpu_custom_call" | custom-call | flops 93640458240 | bytes 251658240 | tf_op jit(solution)/shard_map/spatial_0/pallas_call | solution.py:34
  86.9 5.3 %all-to-all-start.2 = ((f32[8,2,288]{2,1,0:T(2,128)}), f32[8,2,288]{2,1,0:T(2,128)S(1)}, u32[]{:S(2)}, u32[]{:S(2)}) async-start(f32[8,2,288]{2,1,0:T(2,128)} %broadcast_in_dim.26), calls=%async_computation.2 | async-start | bytes 49152 | tf_op jit(solution)/shard_map/all_to_all | solution.py:570
  92.2 4.5 collective-permute-start.13
  98.8 4.5 collective-permute-done.14.refs_6_
  106.5 5.0 %temporal_0.1 = (bf16[2,1176,128]{2,1,0:T(8,128)(2,1)}, f32[2,1176,128]{2,1,0:T(8,128)S(1)}, bf16[3,1176,288]{2,1,0:T(8,128)(2,1)S(1)}, f32[2,288]{1,0:T(2,128)S(1)}, bf16[3,288,512]{2,1,0:T(8,128)(2,1)S(1)}) custom-call(bf16[192,1152]{1,0:T(8,128)(2,1)} %collective-permute-done.8.refs_0_.refs_3_, bf16[192,1152]{1,0:T(8,128)(2,1)S(1)} %copy-done.40, ...), custom_call_target="tpu_custom_call" | custom-call | flops 31213486080 | bytes 251658240 | tf_op jit(solution)/shard_map/temporal_0/pallas_call | solution.py:34
  119.5 7.8 %collective-permute-done.12.refs_1_.refs_8_ = bf16[192,1152]{1,0:T(8,128)(2,1)S(1)} collective-permute-done((bf16[192,1152]{1,0:T(8,128)(2,1)}, bf16[192,1152]{1,0:T(8,128)(2,1)S(1)}, u32[]{:S(2)}, u32[]{:S(2)}) %collective-permute-start.12) | collective-permute-done | bytes 442400 | tf_op jit(solution)/shard_map/ppermute | solution.py:605
  133.8 6.9 %collective-permute-done.17.refs_2_.refs_8_.refs_6_ = bf16[1176,128]{1,0:T(8,128)(2,1)S(1)} collective-permute-done((bf16[1176,128]{1,0:T(8,128)(2,1)}, bf16[1176,128]{1,0:T(8,128)(2,1)S(1)}, u32[]{:S(2)}, u32[]{:S(2)}) %collective-permute-start.17) | collective-permute-done | bytes 301088 | tf_op jit(solution)/shard_map/ppermute | solution.py:580
  157.3 8.6 %spatial_1.1 = (f32[1176,288]{1,0:T(8,128)S(1)}, f32[49,1,288]{2,1,0:T(1,128)S(1)}, f32[49,1,288]{2,1,0:T(1,128)S(1)}, f32[2,288]{1,0:T(2,128)S(1)}, bf16[1176,512]{1,0:T(8,128)(2,1)S(1)}) custom-call(s32[22]{0:T(128)S(1)} %stack.100.refs_5_.refs_2_.refs_0_.refs_1_, bf16[1176,128]{1,0:T(8,128)(2,1)} %get-tuple-element.117.refs_1_.refs_7_.refs_5_, ...), custom_call_target="tpu_custom_call" | custom-call | flops 93640458240 | bytes 251658240 | tf_op jit(solution)/shard_map/spatial_1/pallas_call | solution.py:34
  168.1 12.2 %all_to_all.80.refs_2_ = f32[8,2,288]{2,1,0:T(2,128)S(1)} all-to-all(f32[8,2,288]{2,1,0:T(2,128)S(1)} %broadcast_in_dim.28), channel_id=1, replica_groups=mesh['frames'=8,'rep'=4] {'frames'}, dimensions={0} | all-to-all | bytes 36864 | tf_op jit(solution)/shard_map/all_to_all | solution.py:570
  187.7 8.8 %all-to-all-done.5 = bf16[4,3,2,144,128]{4,3,2,1,0:T(8,128)(2,1)S(1)} async-done(((bf16[4,3,2,144,128]{4,3,2,1,0:T(8,128)(2,1)}), bf16[4,3,2,144,128]{4,3,2,1,0:T(8,128)(2,1)S(1)}, u32[]{:S(2)}, u32[]{:S(2)}) %all-to-all-start.5) | async-done | bytes 884768 | tf_op jit(solution)/shard_map/all_to_all | solution.py:570
  205.8 8.8 %collective-permute-done.24.refs_3_ = bf16[1176,128]{1,0:T(8,128)(2,1)S(1)} collective-permute-done((bf16[1176,128]{1,0:T(8,128)(2,1)S(1)}, bf16[1176,128]{1,0:T(8,128)(2,1)S(1)}, u32[]{:S(2)}, u32[]{:S(2)}) %collective-permute-start.24) | collective-permute-done | bytes 301088 | tf_op jit(solution)/shard_map/ppermute | solution.py:580
  220.6 5.6 %all-to-all-done.6 = f32[32,2,128]{2,1,0:T(2,128)S(1)} async-done(((f32[32,2,128]{2,1,0:T(2,128)}), f32[32,2,128]{2,1,0:T(2,128)S(1)}, u32[]{:S(2)}, u32[]{:S(2)}) %all-to-all-start.6) | async-done | bytes 32800 | tf_op jit(solution)/shard_map/all_to_all | solution.py:570
  228.4 8.0 %collective-permute-done.25.refs_2_ = bf16[1176,128]{1,0:T(8,128)(2,1)S(1)} collective-permute-done((bf16[1176,128]{1,0:T(8,128)(2,1)S(1)}, bf16[1176,128]{1,0:T(8,128)(2,1)S(1)}, u32[]{:S(2)}, u32[]{:S(2)}) %collective-permute-start.25) | collective-permute-done | bytes 301088 | tf_op jit(solution)/shard_map/ppermute | solution.py:580
  236.4 11.2 %all_to_all.81 = f32[32,2,128]{2,1,0:T(2,128)S(1)} all-to-all(f32[32,2,128]{2,1,0:T(2,128)S(1)} %broadcast_in_dim.30), channel_id=1, replica_groups=mesh['frames'=8,'rep'=4] {'frames','rep'}, dimensions={0} | all-to-all | bytes 65536 | tf_op jit(solution)/shard_map/all_to_all | solution.py:570
  254.7 4.5 collective-permute-done.31.refs_3_
  263.2 11.0 %all_to_all.82.refs_6_ = f32[8,2,288]{2,1,0:T(2,128)S(1)} all-to-all(f32[8,2,288]{2,1,0:T(2,128)S(1)} %broadcast_in_dim.31), channel_id=1, replica_groups=mesh['frames'=8,'rep'=4] {'frames'}, dimensions={0} | all-to-all | bytes 36864 | tf_op jit(solution)/shard_map/all_to_all | solution.py:570
  274.3 15.3 %all_to_all.83.refs_0_.refs_3_ = bf16[4,864,128]{2,1,0:T(8,128)(2,1)S(1)} all-to-all(bf16[4,864,128]{2,1,0:T(8,128)(2,1)S(1)} %get-tuple-element.134), channel_id=1, replica_groups=mesh['frames'=8,'rep'=4] {'rep'}, dimensions={0} | all-to-all | bytes 1769472 | tf_op jit(solution)/shard_map/all_to_all | solution.py:570
  289.6 6.7 %input_1.1 = (bf16[1176,288]{1,0:T(8,128)(2,1)S(1)}, bf16[2,1176,128]{2,1,0:T(8,128)(2,1)S(1)}, f32[2,1176,128]{2,1,0:T(8,128)S(1)}, f32[2,288]{1,0:T(2,128)S(1)}) custom-call(bf16[4,864,128]{2,1,0:T(8,128)(2,1)S(1)} %all_to_all.83.refs_0_.refs_3_, s32[22]{0:T(128)S(1)} %stack.100.refs_5_.refs_2_.refs_0_.refs_1_, ...), custom_call_target="tpu_custom_call" | custom-call | flops 93640458240 | bytes 251658240 | tf_op jit(solution)/shard_map/input_1/pallas_call | solution.py:34
  296.3 4.5 weight_1.1
  302.9 9.6 %collective-permute-done.33 = bf16[192,1152]{1,0:T(8,128)(2,1)S(1)} collective-permute-done((bf16[192,1152]{1,0:T(8,128)(2,1)S(1)}, bf16[192,1152]{1,0:T(8,128)(2,1)S(1)}, u32[]{:S(2)}, u32[]{:S(2)}) %collective-permute-start.33) | collective-permute-done | bytes 442400 | tf_op jit(solution)/shard_map/ppermute | solution.py:615
  314.0 9.4 %collective-permute-done.34 = bf16[192,1152]{1,0:T(8,128)(2,1)S(1)} collective-permute-done((bf16[192,1152]{1,0:T(8,128)(2,1)S(1)}, bf16[192,1152]{1,0:T(8,128)(2,1)S(1)}, u32[]{:S(2)}, u32[]{:S(2)}) %collective-permute-start.34) | collective-permute-done | bytes 442400 | tf_op jit(solution)/shard_map/ppermute | solution.py:615
  357.4 11.1 %all_to_all.84.refs_8_ = f32[8,2,288]{2,1,0:T(2,128)S(1)} all-to-all(f32[8,2,288]{2,1,0:T(2,128)S(1)} %broadcast_in_dim.33), channel_id=1, replica_groups=mesh['frames'=8,'rep'=4] {'frames'}, dimensions={0} | all-to-all | bytes 36864 | tf_op jit(solution)/shard_map/all_to_all | solution.py:570
  374.8 10.7 %collective-permute-done.36.refs_0_.refs_3_ = bf16[192,1152]{1,0:T(8,128)(2,1)S(1)} collective-permute-done((bf16[192,1152]{1,0:T(8,128)(2,1)}, bf16[192,1152]{1,0:T(8,128)(2,1)S(1)}, u32[]{:S(2)}, u32[]{:S(2)}) %collective-permute-start.36) | collective-permute-done | bytes 442400 | tf_op jit(solution)/shard_map/ppermute | solution.py:619
  390.6 6.3 %weight_0.1 = (bf16[1176,288]{1,0:T(8,128)(2,1)S(1)}, f32[4,8,512]{2,1,0:T(8,128)}, bf16[8,192,1152]{2,1,0:T(8,128)(2,1)S(1)}, bf16[192,1152]{1,0:T(8,128)(2,1)S(1)}, bf16[192,1152]{1,0:T(8,128)(2,1)}) custom-call(bf16[192,1152]{1,0:T(8,128)(2,1)S(1)} %copy-done.43, bf16[192,1152]{1,0:T(8,128)(2,1)S(1)} %copy-done.46, ...), custom_call_target="tpu_custom_call" | custom-call | flops 93640458240 | bytes 251658240 | tf_op jit(solution)/shard_map/weight_0/pallas_call | solution.py:34
  398.9 9.8 %collective-permute-done.47 = bf16[192,1152]{1,0:T(8,128)(2,1)S(1)} collective-permute-done((bf16[192,1152]{1,0:T(8,128)(2,1)S(1)}, bf16[192,1152]{1,0:T(8,128)(2,1)S(1)}, u32[]{:S(2)}, u32[]{:S(2)}) %collective-permute-start.47) | collective-permute-done | bytes 442400 | tf_op jit(solution)/shard_map/ppermute | solution.py:615
  412.8 7.3 %collective-permute-done.49 = bf16[192,1152]{1,0:T(8,128)(2,1)} collective-permute-done((bf16[192,1152]{1,0:T(8,128)(2,1)S(1)}, bf16[192,1152]{1,0:T(8,128)(2,1)}, u32[]{:S(2)}, u32[]{:S(2)}) %collective-permute-start.49) | collective-permute-done | bytes 442400 | tf_op jit(solution)/shard_map/ppermute | solution.py:615
  428.0 7.8 %last.1 = (bf16[4,6,49,512]{3,2,1,0:T(8,128)(2,1)S(1)}, bf16[4,6,49,128]{3,2,1,0:T(8,128)(2,1)}) custom-call(bf16[192,1152]{1,0:T(8,128)(2,1)S(1)} %fusion.4.refs_0_, bf16[192,1152]{1,0:T(8,128)(2,1)} %get-tuple-element.201.refs_1_, s32[22]{0:T(128)S(1)} %stack.100.refs_5_.refs_2_.refs_0_.refs_1_, bf16[1176,288]{1,0:T(8,128)(2,1)S(1)} %copy-done.101, ...), custom_call_target="tpu_custom_call" | custom-call | flops 93640458240 | bytes 251658240 | tf_op jit(solution)/shard_map/last/pallas_call | solution.py:34
  441.4 5.8 %all-to-all-done.13.refs_0_ = bf16[4,6,49,128]{3,2,1,0:T(8,128)(2,1)S(1)} async-done(((bf16[4,6,49,128]{3,2,1,0:T(8,128)(2,1)}), bf16[4,6,49,128]{3,2,1,0:T(8,128)(2,1)S(1)}, u32[]{:S(2)}, u32[]{:S(2)}) %all-to-all-start.13) | async-done | bytes 301088 | tf_op jit(solution)/shard_map/all_to_all | solution.py:570
  (378 shorter events, 210.8 us)
Async XLA Ops:
  7.2 40.9 %all-gather.2.cloned.1.call-start = ((), (), s32[]{:S(2)}) async-start(), calls=%async_computation.16 | async-start | bytes 1720320 | tf_op jit(solution)/shard_map/all_gather | solution.py:678
  10.6 13.2 %collective-permute-start = (bf16[192,1152]{1,0:T(8,128)(2,1)S(1)}, bf16[192,1152]{1,0:T(8,128)(2,1)S(1)}, u32[]{:S(2)}, u32[]{:S(2)}) collective-permute-start(bf16[192,1152]{1,0:T(8,128)(2,1)S(1)} %get-tuple-element.107.refs_6_), channel_id=1, source_target_pairs={{0,8},{8,16},{16,24},{24,28},{28,20},{20,12},{12,4},{4,0},{1,9},{9... | collective-permute-start | bytes 1327112 | tf_op jit(solution)/shard_map/ppermute | solution.py:603
  13.7 11.9 %collective-permute-start.4 = (bf16[192,1152]{1,0:T(8,128)(2,1)S(1)}, bf16[192,1152]{1,0:T(8,128)(2,1)S(1)}, u32[]{:S(2)}, u32[]{:S(2)}) collective-permute-start(bf16[192,1152]{1,0:T(8,128)(2,1)S(1)} %get-tuple-element.107.refs_6_), channel_id=1, source_target_pairs={{0,4},{8,0},{16,8},{24,16},{28,24},{20,28},{12,20},{4,12},{1,5},{9... | collective-permute-start | bytes 1327112 | tf_op jit(solution)/shard_map/ppermute | solution.py:605
  25.6 16.3 %collective-permute-start.5 = (bf16[192,1152]{1,0:T(8,128)(2,1)S(1)}, bf16[192,1152]{1,0:T(8,128)(2,1)}, u32[]{:S(2)}, u32[]{:S(2)}) collective-permute-start(bf16[192,1152]{1,0:T(8,128)(2,1)S(1)} %collective-permute-done.4.refs_11_), channel_id=1, source_target_pairs={{0,4},{8,0},{16,8},{24,16},{28,24},{20,28},{12,20},{4,12},{1,5},{9... | collective-permute-start | bytes 1327112 | tf_op jit(solution)/shard_map/ppermute | solution.py:605
  41.9 12.6 %collective-permute-start.6 = (bf16[192,1152]{1,0:T(8,128)(2,1)}, bf16[192,1152]{1,0:T(8,128)(2,1)}, u32[]{:S(2)}, u32[]{:S(2)}) collective-permute-start(bf16[192,1152]{1,0:T(8,128)(2,1)} %collective-permute-done.5.refs_12_), channel_id=1, source_target_pairs={{0,4},{8,0},{16,8},{24,16},{28,24},{20,28},{12,20},{4,12},{1,5},{9... | collective-permute-start | bytes 1327112 | tf_op jit(solution)/shard_map/ppermute | solution.py:605
  63.7 19.2 %all-to-all-start.1 = ((bf16[4,3,2,144,128]{4,3,2,1,0:T(8,128)(2,1)}), bf16[4,3,2,144,128]{4,3,2,1,0:T(8,128)(2,1)S(1)}, u32[]{:S(2)}, u32[]{:S(2)}) async-start(bf16[4,3,2,144,128]{4,3,2,1,0:T(8,128)(2,1)} %get-tuple-element.111), calls=%async_computation.1 | async-start | bytes 1769472 | tf_op jit(solution)/shard_map/all_to_all | solution.py:570
  71.8 31.5 %collective-permute-start.11 = (bf16[192,1152]{1,0:T(8,128)(2,1)S(1)}, bf16[192,1152]{1,0:T(8,128)(2,1)S(1)}, u32[]{:S(2)}, u32[]{:S(2)}) collective-permute-start(bf16[192,1152]{1,0:T(8,128)(2,1)S(1)} %collective-permute-done.10.refs_6_), channel_id=1, source_target_pairs={{0,4},{8,0},{16,8},{24,16},{28,24},{20,28},{12,20},{4,12},{1,5},{9... | collective-permute-start | bytes 1327112 | tf_op jit(solution)/shard_map/ppermute | solution.py:605
  73.0 31.0 %collective-permute-start.8 = (bf16[192,1152]{1,0:T(8,128)(2,1)S(1)}, bf16[192,1152]{1,0:T(8,128)(2,1)}, u32[]{:S(2)}, u32[]{:S(2)}) collective-permute-start(bf16[192,1152]{1,0:T(8,128)(2,1)S(1)} %collective-permute-done.7.refs_2_), channel_id=1, source_target_pairs={{0,8},{8,16},{16,24},{24,28},{28,20},{20,12},{12,4},{4,0},{1,9},{9... | collective-permute-start | bytes 1327112 | tf_op jit(solution)/shard_map/ppermute | solution.py:603
  86.9 11.9 %all-to-all-start.2 = ((f32[8,2,288]{2,1,0:T(2,128)}), f32[8,2,288]{2,1,0:T(2,128)S(1)}, u32[]{:S(2)}, u32[]{:S(2)}) async-start(f32[8,2,288]{2,1,0:T(2,128)} %broadcast_in_dim.26), calls=%async_computation.2 | async-start | bytes 49152 | tf_op jit(solution)/shard_map/all_to_all | solution.py:570
  114.6 12.8 %collective-permute-start.12 = (bf16[192,1152]{1,0:T(8,128)(2,1)}, bf16[192,1152]{1,0:T(8,128)(2,1)S(1)}, u32[]{:S(2)}, u32[]{:S(2)}) collective-permute-start(bf16[192,1152]{1,0:T(8,128)(2,1)} %copy-done.39), channel_id=1, source_target_pairs={{0,4},{8,0},{16,8},{24,16},{28,24},{20,28},{12,20},{4,12},{1,5},{9... | collective-permute-start | bytes 1327112 | tf_op jit(solution)/shard_map/ppermute | solution.py:605
  116.3 12.6 %collective-permute-start.9 = (bf16[192,1152]{1,0:T(8,128)(2,1)}, bf16[192,1152]{1,0:T(8,128)(2,1)}, u32[]{:S(2)}, u32[]{:S(2)}) collective-permute-start(bf16[192,1152]{1,0:T(8,128)(2,1)} %collective-permute-done.8.refs_0_.refs_3_), channel_id=1, source_target_pairs={{0,8},{8,16},{16,24},{24,28},{28,20},{20,12},{12,4},{4,0},{1,9},{9... | collective-permute-start | bytes 1327112 | tf_op jit(solution)/shard_map/ppermute | solution.py:603
  133.7 21.5 %collective-permute-start.18 = (bf16[1176,128]{1,0:T(8,128)(2,1)}, bf16[1176,128]{1,0:T(8,128)(2,1)S(1)}, u32[]{:S(2)}, u32[]{:S(2)}) collective-permute-start(bf16[1176,128]{1,0:T(8,128)(2,1)} %get-tuple-element.117.refs_1_.refs_7_.refs_5_), channel_id=1, source_target_pairs={{0,1},{1,0},{2,3},{3,2},{4,5},{5,4},{6,7},{7,6},{8,9},{9,8},{10,11... | collective-permute-start | bytes 903176 | tf_op jit(solution)/shard_map/ppermute | solution.py:580
  140.6 14.6 %collective-permute-start.19 = (bf16[1176,128]{1,0:T(8,128)(2,1)S(1)}, bf16[1176,128]{1,0:T(8,128)(2,1)S(1)}, u32[]{:S(2)}, u32[]{:S(2)}) collective-permute-start(bf16[1176,128]{1,0:T(8,128)(2,1)S(1)} %collective-permute-done.17.refs_2_.refs_8_.refs_6_), channel_id=1, source_target_pairs={{0,1},{1,0},{2,3},{3,2},{4,5},{5,4},{6,7},{7,6},{8,9},{9,8},{10,11... | collective-permute-start | bytes 903176 | tf_op jit(solution)/shard_map/ppermute | solution.py:580
  141.3 13.9 %all-to-all-start.3 = ((f32[32,2,128]{2,1,0:T(2,128)}), f32[32,2,128]{2,1,0:T(2,128)S(1)}, u32[]{:S(2)}, u32[]{:S(2)}) async-start(f32[32,2,128]{2,1,0:T(2,128)} %broadcast_in_dim.27), calls=%async_computation.3 | async-start | bytes 65536 | tf_op jit(solution)/shard_map/all_to_all | solution.py:570
  180.3 16.2 %all-to-all-start.5 = ((bf16[4,3,2,144,128]{4,3,2,1,0:T(8,128)(2,1)}), bf16[4,3,2,144,128]{4,3,2,1,0:T(8,128)(2,1)S(1)}, u32[]{:S(2)}, u32[]{:S(2)}) async-start(bf16[4,3,2,144,128]{4,3,2,1,0:T(8,128)(2,1)} %get-tuple-element.125), calls=%async_computation.5 | async-start | bytes 1769472 | tf_op jit(solution)/shard_map/all_to_all | solution.py:570
  183.9 12.7 %collective-permute-start.21 = (f32[49,1,288]{2,1,0:T(1,128)S(1)}, f32[49,1,288]{2,1,0:T(1,128)S(1)}, u32[]{:S(2)}, u32[]{:S(2)}) collective-permute-start(f32[49,1,288]{2,1,0:T(1,128)S(1)} %get-tuple-element.123), channel_id=1, source_target_pairs={{0,4},{4,8},{8,12},{12,16},{16,20},{20,24},{24,28},{1,5},{5,9},{9,... | collective-permute-start | bytes 169352 | tf_op jit(solution)/shard_map/ppermute | solution.py:591
  227.8 19.9 %collective-permute-start.29 = (bf16[1176,128]{1,0:T(8,128)(2,1)S(1)}, bf16[1176,128]{1,0:T(8,128)(2,1)S(1)}, u32[]{:S(2)}, u32[]{:S(2)}) collective-permute-start(bf16[1176,128]{1,0:T(8,128)(2,1)S(1)} %get-tuple-element.131.refs_5_), channel_id=1, source_target_pairs={{0,1},{1,0},{2,3},{3,2},{4,5},{5,4},{6,7},{7,6},{8,9},{9,8},{10,11... | collective-permute-start | bytes 903176 | tf_op jit(solution)/shard_map/ppermute | solution.py:580
  227.8 19.9 %collective-permute-start.26 = (bf16[1176,128]{1,0:T(8,128)(2,1)S(1)}, bf16[1176,128]{1,0:T(8,128)(2,1)S(1)}, u32[]{:S(2)}, u32[]{:S(2)}) collective-permute-start(bf16[1176,128]{1,0:T(8,128)(2,1)S(1)} %get-tuple-element.130.refs_1_), channel_id=1, source_target_pairs={{0,1},{1,0},{2,3},{3,2},{4,5},{5,4},{6,7},{7,6},{8,9},{9,8},{10,11... | collective-permute-start | bytes 903176 | tf_op jit(solution)/shard_map/ppermute | solution.py:580
  228.4 19.2 %collective-permute-start.30 = (bf16[1176,128]{1,0:T(8,128)(2,1)S(1)}, bf16[1176,128]{1,0:T(8,128)(2,1)S(1)}, u32[]{:S(2)}, u32[]{:S(2)}) collective-permute-start(bf16[1176,128]{1,0:T(8,128)(2,1)S(1)} %collective-permute-done.28.refs_6_), channel_id=1, source_target_pairs={{0,1},{1,0},{2,3},{3,2},{4,5},{5,4},{6,7},{7,6},{8,9},{9,8},{10,11... | collective-permute-start | bytes 903176 | tf_op jit(solution)/shard_map/ppermute | solution.py:580
  301.3 12.7 %collective-permute-start.37 = (bf16[192,1152]{1,0:T(8,128)(2,1)S(1)}, bf16[192,1152]{1,0:T(8,128)(2,1)S(1)}, u32[]{:S(2)}, u32[]{:S(2)}) collective-permute-start(bf16[192,1152]{1,0:T(8,128)(2,1)S(1)} %get-tuple-element.146), channel_id=1, source_target_pairs={{0,4},{8,0},{16,8},{24,16},{28,24},{20,28},{12,20},{4,12},{1,5},{9... | collective-permute-start | bytes 1327112 | tf_op jit(solution)/shard_map/ppermute | solution.py:617
  313.2 12.5 %collective-permute-start.41 = (bf16[1176,128]{1,0:T(8,128)(2,1)S(1)}, bf16[1176,128]{1,0:T(8,128)(2,1)S(1)}, u32[]{:S(2)}, u32[]{:S(2)}) collective-permute-start(bf16[1176,128]{1,0:T(8,128)(2,1)S(1)} %fusion.12), channel_id=1, source_target_pairs={{0,2},{1,3},{2,0},{3,1},{4,6},{5,7},{6,4},{7,5},{8,10},{9,11},{10,... | collective-permute-start | bytes 903176 | tf_op jit(solution)/shard_map/ppermute | solution.py:580
  368.5 18.5 %all-to-all-start.12 = ((bf16[4,864,128]{2,1,0:T(8,128)(2,1)}), bf16[4,864,128]{2,1,0:T(8,128)(2,1)}, u32[]{:S(2)}, u32[]{:S(2)}) async-start(bf16[4,864,128]{2,1,0:T(8,128)(2,1)} %copy-done.24), calls=%async_computation.12 | async-start | bytes 1769472 | tf_op jit(solution)/shard_map/all_to_all | solution.py:570
  372.8 12.8 %collective-permute-start.36 = (bf16[192,1152]{1,0:T(8,128)(2,1)}, bf16[192,1152]{1,0:T(8,128)(2,1)S(1)}, u32[]{:S(2)}, u32[]{:S(2)}) collective-permute-start(bf16[192,1152]{1,0:T(8,128)(2,1)} %get-tuple-element.203), channel_id=1, source_target_pairs={{0,8},{8,16},{16,24},{24,28},{28,20},{20,12},{12,4},{4,0},{1,9},{9... | collective-permute-start | bytes 1327112 | tf_op jit(solution)/shard_map/ppermute | solution.py:619
  373.3 13.0 %collective-permute-start.39 = (bf16[192,1152]{1,0:T(8,128)(2,1)S(1)}, bf16[192,1152]{1,0:T(8,128)(2,1)S(1)}, u32[]{:S(2)}, u32[]{:S(2)}) collective-permute-start(bf16[192,1152]{1,0:T(8,128)(2,1)S(1)} %copy-done.34), channel_id=1, source_target_pairs={{0,4},{8,0},{16,8},{24,16},{28,24},{20,28},{12,20},{4,12},{1,5},{9... | collective-permute-start | bytes 1327112 | tf_op jit(solution)/shard_map/ppermute | solution.py:619
  396.9 11.8 %collective-permute-start.47 = (bf16[192,1152]{1,0:T(8,128)(2,1)S(1)}, bf16[192,1152]{1,0:T(8,128)(2,1)S(1)}, u32[]{:S(2)}, u32[]{:S(2)}) collective-permute-start(bf16[192,1152]{1,0:T(8,128)(2,1)S(1)} %get-tuple-element.165), channel_id=1, source_target_pairs={{0,8},{8,16},{16,24},{24,28},{28,20},{20,12},{12,4},{4,0},{1,9},{9... | collective-permute-start | bytes 1327112 | tf_op jit(solution)/shard_map/ppermute | solution.py:615
  397.3 15.4 %collective-permute-start.48 = (bf16[192,1152]{1,0:T(8,128)(2,1)}, bf16[192,1152]{1,0:T(8,128)(2,1)}, u32[]{:S(2)}, u32[]{:S(2)}) collective-permute-start(bf16[192,1152]{1,0:T(8,128)(2,1)} %get-tuple-element.167), channel_id=1, source_target_pairs={{0,4},{8,0},{16,8},{24,16},{28,24},{20,28},{12,20},{4,12},{1,5},{9... | collective-permute-start | bytes 1327112 | tf_op jit(solution)/shard_map/ppermute | solution.py:617
  409.3 27.5 %all-to-all-start.15 = ((f32[4,8,512]{2,1,0:T(8,128)}), f32[4,8,512]{2,1,0:T(8,128)S(1)}, u32[]{:S(2)}, u32[]{:S(2)}) async-start(f32[4,8,512]{2,1,0:T(8,128)} %get-tuple-element.191), calls=%async_computation.15 | async-start | bytes 131072 | tf_op jit(solution)/shard_map/all_to_all | solution.py:570
  422.6 29.1 %collective-permute-start.50 = (bf16[192,1152]{1,0:T(8,128)(2,1)}, bf16[192,1152]{1,0:T(8,128)(2,1)}, u32[]{:S(2)}, u32[]{:S(2)}) collective-permute-start(bf16[192,1152]{1,0:T(8,128)(2,1)} %get-tuple-element.200), channel_id=1, source_target_pairs={{0,8},{8,16},{16,24},{24,28},{28,20},{20,12},{12,4},{4,0},{1,9},{9... | collective-permute-start | bytes 1327112 | tf_op jit(solution)/shard_map/ppermute | solution.py:615
  423.0 28.7 %collective-permute-start.52 = (bf16[192,1152]{1,0:T(8,128)(2,1)}, bf16[192,1152]{1,0:T(8,128)(2,1)}, u32[]{:S(2)}, u32[]{:S(2)}) collective-permute-start(bf16[192,1152]{1,0:T(8,128)(2,1)} %get-tuple-element.201.refs_1_), channel_id=1, source_target_pairs={{0,4},{8,0},{16,8},{24,16},{28,24},{20,28},{12,20},{4,12},{1,5},{9... | collective-permute-start | bytes 1327112 | tf_op jit(solution)/shard_map/ppermute | solution.py:617
  447.9 21.6 %all-to-all-start.14 = ((bf16[4,6,49,512]{3,2,1,0:T(8,128)(2,1)}), bf16[4,6,49,512]{3,2,1,0:T(8,128)(2,1)S(1)}, u32[]{:S(2)}, u32[]{:S(2)}) async-start(bf16[4,6,49,512]{3,2,1,0:T(8,128)(2,1)} %copy-done.21), calls=%async_computation.14 | async-start | bytes 2752512 | tf_op jit(solution)/shard_map/all_to_all | solution.py:570
  453.5 12.6 %collective-permute-start.53 = (bf16[192,1152]{1,0:T(8,128)(2,1)S(1)}, bf16[192,1152]{1,0:T(8,128)(2,1)S(1)}, u32[]{:S(2)}, u32[]{:S(2)}) collective-permute-start(bf16[192,1152]{1,0:T(8,128)(2,1)S(1)} %get-tuple-element.198), channel_id=1, source_target_pairs={{0,4},{8,0},{16,8},{24,16},{28,24},{20,28},{12,20},{4,12},{1,5},{9... | collective-permute-start | bytes 1327112 | tf_op jit(solution)/shard_map/ppermute | solution.py:619
  453.8 12.4 %collective-permute-start.51 = (bf16[192,1152]{1,0:T(8,128)(2,1)S(1)}, bf16[192,1152]{1,0:T(8,128)(2,1)S(1)}, u32[]{:S(2)}, u32[]{:S(2)}) collective-permute-start(bf16[192,1152]{1,0:T(8,128)(2,1)S(1)} %get-tuple-element.199), channel_id=1, source_target_pairs={{0,8},{8,16},{16,24},{24,28},{28,20},{20,12},{12,4},{4,0},{1,9},{9... | collective-permute-start | bytes 1327112 | tf_op jit(solution)/shard_map/ppermute | solution.py:619
  (138 other events, 1258.1 us)
Sparse Core Ops, SparseCore 0:
  9.6 21.2 all-gather.1

commit v4 on v3

v4 whole, which is shorter than its diff:
```python
import functools

import jax
import jax.numpy as jnp
from jax import lax
from jax.experimental import pallas as pl
from jax.experimental.pallas import tpu as pltpu
from jax.sharding import PartitionSpec as P

STEP = 5
NORM_EPS = 1e-05
ADAM_EPS = 1e-08
BETA_ONE = 0.5
BETA_TWO = 0.5
RATE_WEIGHT = 0.015
RATE_NORM = 0.2
DECAY = 0.05
BF = jnp.bfloat16
F32 = jnp.float32
MIB = 1 << 20
VMEM = pl.BlockSpec(memory_space=pltpu.VMEM)
SMEM = pl.BlockSpec(memory_space=pltpu.SMEM)
LANES = 128
SCALE = 30
ANY = pl.BlockSpec(memory_space=pl.ANY)
HBM = pl.BlockSpec(memory_space=pltpu.HBM)


def shape(dims, dtype):
    return jax.ShapeDtypeStruct(tuple(dims), dtype)


class Placed:
    def __init__(self, value, where):
        self.value, self.where = value, where


def far(value):
    return Placed(value, "hbm")


def loaded(value):
    return Placed(value, "loaded")


def near(value):
    return Placed(value, "vmem")


def all_loaded(values):
    return [loaded(v) for v in values]


def in_hbm(array):
    return pltpu.with_memory_space_constraint(array, pltpu.HBM)


def operand(a):
    if not isinstance(a, Placed):
        return a
    return pltpu.with_memory_space_constraint(a.value, pltpu.VMEM if a.where == "vmem" else pltpu.HBM)


def result(a):
    if not isinstance(a, Placed):
        return a
    return (pltpu.VMEM if a.where == "vmem" else pltpu.HBM)(a.value.shape, a.value.dtype)


def is_far(a):
    return isinstance(a, Placed) and a.where == "hbm"


def run(body, outs, args, name, scratch=(), limit=28, scalars=0, flops=0, moved=0, after=(), scale=SCALE):
    def kernel(*refs):
        body(*refs[len(after) :])

    return pl.pallas_call(
        kernel,
        out_shape=tuple(result(o) for o in outs),
        in_specs=[ANY] * len(after) + [SMEM] * scalars + [ANY if is_far(a) else VMEM for a in args[scalars:]],
        out_specs=tuple(HBM if is_far(o) else VMEM for o in outs),
        scratch_shapes=list(scratch),
        compiler_params=pltpu.CompilerParams(vmem_limit_bytes=limit * MIB),
        cost_estimate=pl.CostEstimate(flops=int(scale * flops), bytes_accessed=int(scale * moved), transcendentals=0),
        name=name,
    )(*after, *[operand(a) for a in args])


def gate(value, after, name):
    return pl.pallas_call(
        lambda *refs: None,
        out_shape=shape(value.shape, value.dtype),
        in_specs=[ANY] * (len(after) + 1),
        out_specs=ANY,
        input_output_aliases={len(after): 0},
        name=name,
    )(*after, value)


def started(source, target, sem):
    copy = pltpu.make_async_copy(source, target, sem)
    copy.start()
    return copy


def padded(values, rows):
    return jnp.concatenate([values, jnp.zeros((rows - values.shape[0], values.shape[1]), F32)], axis=0)


def sigmoid(v):
    return 1.0 / (1.0 + jnp.exp(-v))


def silu(v):
    return v / (1.0 + jnp.exp(-v))


def silu_slope(v):
    s = sigmoid(v)
    return s * (1.0 + v * (1.0 - s))


def mm(a, b, dims):
    return lax.dot_general(a, b, (dims, ((), ())), preferred_element_type=F32)


def put_moments(values, out_ref):
    rows = values.shape[0]
    mean = jnp.sum(values, axis=0, keepdims=True) * (1.0 / rows)
    off = values - mean
    out_ref[0:1, :] = mean
    out_ref[1:2, :] = jnp.sum(off * off, axis=0, keepdims=True)


def joined_moments(both, rows):
    count = both.shape[0]
    mean = jnp.sum(both[:, 0:1], axis=0) * (1.0 / count)
    off = both[:, 0:1] - mean[None]
    total = jnp.sum(both[:, 1:2] + rows * (off * off), axis=0)
    return mean, lax.rsqrt(total * (1.0 / (rows * count)) + NORM_EPS)


def put_sums(upstream, normed, out_ref):
    out_ref[0:1, :] = jnp.sum(upstream * normed, axis=0, keepdims=True)
    out_ref[1:2, :] = jnp.sum(upstream, axis=0, keepdims=True)


def convolve(pad, w_ref, acc_ref, dims):
    height, width, frames, depth = dims
    rows = height * width * frames

    for k in range(9):
        i, j = k // 3, k % 3
        piece = pad[i : i + height, j : j + width].reshape(rows, depth).astype(BF)
        part = mm(piece, w_ref[:, k * depth : (k + 1) * depth], ((1,), (1,)))
        if k == 0:
            acc_ref[...] = part
        else:
            acc_ref[...] += part


def widened(scr, values, before, after):
    frames = values.shape[1]
    scr[:, 8 : 8 + frames, :] = values
    scr[:, 7:8, :] = before
    scr[:, 8 + frames : 9 + frames, :] = after


RING = (0, 2, 4, 6, 7, 5, 3, 1)


def can_ring(mid, k, k_t, count):
    return count == len(RING) and mid == 288 and k == 576 and k_t == 432


def ring_place(frame):
    return jnp.where(frame % 2 == 0, frame // 2, 7 - frame // 2)


def ring_device(place):
    place = place % 8
    return jnp.where(place < 4, 2 * place, 15 - 2 * place)


def low_half(shape_):
    return lax.broadcasted_iota(jnp.int32, shape_, 1) < LANES // 2


def fold(top, bottom, out_ref, k):
    edge = k - LANES // 2
    out_ref[:, 0:edge] = top[:, 0:edge].astype(out_ref.dtype)
    mixed = jnp.where(low_half((top.shape[0], LANES)), top[:, edge : edge + LANES], bottom[:, 0:LANES])
    out_ref[:, edge : edge + LANES] = mixed.astype(out_ref.dtype)
    out_ref[:, edge + LANES : 2 * k] = bottom[:, LANES : k + LANES // 2].astype(out_ref.dtype)


def pack_body(w_ref, t_ref, *refs):
    outs, folded, scr = refs[:-2], refs[-2], refs[-1]
    units, mid, k = w_ref.shape
    half = mid // 2
    for u in range(units):
        scr[:, 0:k] = w_ref[u]
        fold(scr[0:half, :], pltpu.roll(scr[half:mid, :], LANES // 2, 1), folded.at[0:half], k)
        rows = folded.shape[0] - half
        for i in range(2 * k // LANES):
            at = slice(i * LANES, (i + 1) * LANES)
            folded[half:, at] = t_ref[u, rows * i : rows * (i + 1), :].astype(BF)
        start = 0
        for out in outs[:3] if u == 0 else outs[u + 2 : u + 3]:
            out[...] = folded[start : start + out.shape[0], :]
            start += out.shape[0]


def unpack_temporal(f, slot, t_ref):
    rows = slot.shape[0]
    per = t_ref.shape[3] // rows
    for j in range(slot.shape[1] // LANES):
        block = 3 * f + j // per
        piece = slot[:, j * LANES : (j + 1) * LANES]
        t_ref[(block % 8) // 2, block // 8, block % 2, (j % per) * rows : (j % per + 1) * rows, :] = piece


def slots_of(refs):
    if len(refs[0].shape) == 3:
        half = refs[0].shape[1] * 3 // 4
        return [([refs[0].at[i, 0:half]], refs[0].at[i, half:]) for i in range(8)], refs[1:]
    return [([refs[i], refs[8 + i]], refs[16 + i]) for i in range(8)], refs[24:]


def unpack_temporal_body(ids_ref, *refs):
    slots, refs = slots_of(refs)
    if len(refs) > 5:
        refs[5][...] = refs[0][...]
        refs = refs[1:5] + refs[6:]
    outs, scr = refs[:4], refs[4]
    half = scr.shape[3]
    for i, (_, slot) in enumerate(slots):
        unpack_temporal(ids_ref[6 + i], slot, scr)
    for j, out_ref in enumerate(outs):
        for k in range(3):
            for part in range(2):
                out_ref[k, part * half : (part + 1) * half, :] = scr[ids_ref[j], k, part]


def unpack_spatial(ids_ref, slots, w_ref):
    half, k = w_ref.shape[0] // 2, w_ref.shape[1] // 8
    edge, wide = k - LANES // 2, k + LANES // 2
    for i, (slot, _) in enumerate(slots):
        f = ids_ref[6 + i]
        base = (f // 2) * (2 * k)
        values = jnp.concatenate([part[...].astype(F32) for part in slot], axis=0)
        low = low_half((half, LANES))

        def at(start, size):
            return pl.ds(pl.multiple_of(base + start, LANES), size)

        @pl.when(f % 2 == 0)
        def _():
            for start, part in ((0, values[:, 0:wide]), (half, pltpu.roll(values[:, edge:], k, 1))):
                rows = slice(start, start + half)
                w_ref[rows, at(0, edge)] = part[:, 0:edge].astype(BF)
                old = w_ref[rows, at(edge, LANES)].astype(F32)
                w_ref[rows, at(edge, LANES)] = jnp.where(low, part[:, edge:wide], old).astype(BF)

        @pl.when(f % 2 == 1)
        def _():
            for start, part in ((0, pltpu.roll(values[:, 0:wide], LANES // 2, 1)), (half, values[:, edge:])):
                rows = slice(start, start + half)
                old = w_ref[rows, at(edge, LANES)].astype(F32)
                w_ref[rows, at(edge, LANES)] = jnp.where(low, old, part[:, 0:LANES]).astype(BF)
                w_ref[rows, at(edge + LANES, edge)] = part[:, LANES:wide].astype(BF)


def spatial_body(*refs, dims, ring, first):
    height, width, frames, depth = dims
    rows = height * width * frames
    ids_ref, refs = refs[0], refs[1:]
    if ring:
        slots, refs = slots_of(refs)
    else:
        w_ref, refs = refs[0], refs[1:]
    refs = iter(refs)

    def take(count):
        return [next(refs) for _ in range(count)]

    sources = take(1 if first else 6)
    s_ref, first_ref, last_ref, mom_ref, s_far = take(5)
    w_far, act_far = take(int(ring)), take(int(not first))
    pad, sems = take(2)
    w_scr, act_scr = take(int(ring)), take(int(not first))

    copies = []
    if ring:
        w_ref = w_scr[0]
        unpack_spatial(ids_ref, slots, w_ref)
        copies.append(started(w_ref, w_far[0], sems.at[0]))
    pad[...] = jnp.zeros(pad.shape, F32)
    if first:
        pad[1 : height + 1, 1 : width + 1] = sources[0][...].astype(F32).reshape(dims)
    else:
        both_ref, norm_ref = sources[4:]
        for j, t_ref in enumerate(sources[:4]):
            b = ids_ref[j]
            mean, inverse = joined_moments(both_ref[:, b], rows)
            norm = norm_ref[b]
            y = (t_ref[...].astype(F32) - mean) * (inverse * norm[0:1]) + norm[1:2]
            a = silu(y)
            at = pl.ds(pl.multiple_of(b * LANES, LANES), LANES)
            act_scr[0][:, at] = padded(a, act_scr[0].shape[0]).astype(BF)
            pad[1 : height + 1, 1 : width + 1, :, at] = a.reshape(height, width, frames, LANES)
        copies.append(started(act_scr[0], act_far[0], sems.at[1]))
    convolve(pad, w_ref, s_ref, dims)
    copies.append(started(s_ref, s_far, sems.at[2]))
    values = s_ref[...]
    put_moments(values, mom_ref)
    grid = values.reshape(height * width, frames, values.shape[-1])
    first_ref[...] = grid[:, 0:1, :]
    last_ref[...] = grid[:, frames - 1 : frames, :]
    for copy in copies:
        copy.wait()


def temporal_body(
    ids_ref, s_ref, both_ref, before_ref, after_ref, norm_ref, keep_ref, w0, w1, w2, w3,
    send_ref, kept_ref, stat_ref, win_far, row_far, scr, part, win_ref, row_ref, sems, *, dims
):
    height, width, frames, depth = dims
    pixels = height * width
    rows = pixels * frames
    mid = s_ref.shape[-1]
    for j, w_ref in enumerate((w0, w1, w2, w3)):
        row_ref[:, :, pl.ds(pl.multiple_of(ids_ref[j] * LANES, LANES), LANES)] = w_ref[...]
    copies = [started(row_ref, row_far, sems.at[0])]
    mean, inverse = joined_moments(both_ref[...], rows)
    stat_ref[0:1, :] = mean
    stat_ref[1:2, :] = inverse
    scale, bias = inverse * norm_ref[0:1], norm_ref[1:2]

    def active(v):
        return silu((v - mean) * scale + bias)

    middle = active(s_ref[...])
    widened(
        scr, middle.reshape(pixels, frames, mid),
        active(before_ref[...].reshape(pixels, mid)).reshape(pixels, 1, mid),
        active(after_ref[...].reshape(pixels, mid)).reshape(pixels, 1, mid),
    )
    whole = win_ref.shape[1]
    earlier = (scr[:, 7 : 7 + frames, :] * keep_ref[0][None]).reshape(rows, mid)
    later = (scr[:, 9 : 9 + frames, :] * keep_ref[1][None]).reshape(rows, mid)
    for i, values in enumerate((earlier, middle, later)):
        win_ref[i] = padded(values, whole).astype(BF)
    copies.append(started(win_ref, win_far, sems.at[1]))
    part[...] = mm(win_ref[0], row_ref[0], ((1,), (0,)))
    part[...] += mm(win_ref[1], row_ref[1], ((1,), (0,)))
    part[...] += mm(win_ref[2], row_ref[2], ((1,), (0,)))
    put_halves(ids_ref, part, send_ref, kept_ref)
    for copy in copies:
        copy.wait()


def put_halves(ids_ref, part, send_ref, kept_ref):
    core = ids_ref[4]
    rows = send_ref.shape[1]
    for i in range(2):
        other = pl.multiple_of((2 * i + 1 - core) * LANES, LANES)
        own = pl.multiple_of((2 * i + core) * LANES, LANES)
        send_ref[i] = part[0:rows, pl.ds(other, LANES)].astype(BF)
        kept_ref[i] = part[0:rows, pl.ds(own, LANES)]


def total_body(ids_ref, got_ref, kept_ref, last_ref, t_ref, low_ref, mom_ref):
    x = ids_ref[5]
    t = got_ref[x].astype(F32) + kept_ref[x] + last_ref[...].astype(F32)
    t_ref[...] = t
    low_ref[...] = t.astype(BF)
    put_moments(t, mom_ref)


def edges_body(*refs, dims):
    height, width, frames, depth = dims
    blocks, (first_ref, last_ref) = refs[:-2], refs[-2:]
    for j, ref in enumerate(blocks):
        grid = ref[...].astype(F32).reshape(height * width, frames, LANES)
        first_ref[j] = grid[:, 0:1, :]
        last_ref[j] = grid[:, frames - 1 : frames, :]


def top_body(ids_ref, t_ref, both_ref, norm_ref, x_ref, cot_ref, block_ref, g_ref, low_ref, sums_ref):
    rows = t_ref.shape[0]
    b = ids_ref[0]
    mean, inverse = joined_moments(both_ref[:, b], rows)
    norm = norm_ref[b]
    normed = (t_ref[...] - mean) * inverse
    own = pl.ds(pl.multiple_of(b * LANES, LANES), LANES)
    summed = normed * norm[0:1] + norm[1:2] + x_ref[:, own].astype(F32)
    block_ref[...] = silu(summed).astype(BF)
    g = cot_ref[...].astype(F32) * silu_slope(summed)
    g_ref[...] = g
    low_ref[...] = g.astype(BF)
    put_sums(g, normed, sums_ref)


def below_body(ids_ref, got_ref, kept_ref, last_ref, t_ref, both_ref, norm_ref, low_ref, sums_ref):
    rows = t_ref.shape[0]
    b, x = ids_ref[0], ids_ref[5]
    d_act = got_ref[x].astype(F32) + kept_ref[x] + last_ref[...].astype(F32)
    mean, inverse = joined_moments(both_ref[:, b], rows)
    norm = norm_ref[b]
    normed = (t_ref[...] - mean) * inverse
    g = d_act * silu_slope(normed * norm[0:1] + norm[1:2])
    low_ref[...] = g.astype(BF)
    put_sums(g, normed, sums_ref)


def dt_body(
    ids_ref, g0, g1, g2, g3, t0, t1, t2, t3, both_ref, sums_ref, norm_ref, dt_ref, coef_ref, sum_ref, *, total
):
    rows, whole = g0.shape[0], dt_ref.shape[0]
    for j, (g_ref, t_ref) in enumerate(((g0, t0), (g1, t1), (g2, t2), (g3, t3))):
        b = ids_ref[j]
        mean, inverse = joined_moments(both_ref[:, b], rows)
        sums = jnp.sum(sums_ref[:, b], axis=0)
        if j == 0:
            sum_ref[...] = sums
        c1 = norm_ref[b][0:1] * inverse
        c2 = c1 * sums[1:2] * (1.0 / total)
        c3 = c1 * inverse * sums[0:1] * (1.0 / total)
        coef_ref[j] = jnp.concatenate([c1, c2, c3, mean], axis=0)
        d = c1 * g_ref[...].astype(F32) - c2 - c3 * (t_ref[...].astype(F32) - mean)
        dt_ref[:, pl.ds(pl.multiple_of(b * LANES, LANES), LANES)] = padded(d, whole).astype(BF)


def temporal_grad_body(ids_ref, win_ref, dt_ref, *refs):
    outs, term = refs[:-1], refs[-1]
    mid = win_ref.shape[-1]
    dt = dt_ref[...]
    for k in range(3):
        term[...] = mm(win_ref[k], dt, ((0,), (0,)))
        for j, out_ref in enumerate(outs):
            at = pl.ds(pl.multiple_of(ids_ref[j] * LANES, LANES), LANES)
            out_ref[k * mid : (k + 1) * mid, :] = term[:, at].astype(BF)


def middle_body(
    ids_ref, dt_ref, coef_ref, before_ref, after_ref, keep_ref, stat_ref, norm_ref, row_far, s_far,
    d_ref, sums_ref, scr, row_ref, s_ref, sems, *, dims
):
    height, width, frames, depth = dims
    pixels = height * width
    rows = pixels * frames
    copies = [started(row_far, row_ref, sems.at[0]), started(s_far, s_ref, sems.at[1])]
    dt = dt_ref[...]
    scr[:, 8 : 8 + frames, :] = dt.astype(F32)[0:rows].reshape(pixels, frames, depth)
    for j in range(4):
        at = pl.ds(pl.multiple_of(ids_ref[j] * LANES, LANES), LANES)
        c = coef_ref[j]

        def halo(g, t):
            d = c[0:1] * g.reshape(pixels, LANES) - c[1:2] - c[2:3] * (t.reshape(pixels, LANES) - c[3:4])
            return d.astype(BF).astype(F32).reshape(pixels, 1, LANES)

        scr[:, 7:8, at] = halo(before_ref[j], before_ref[4 + j])
        scr[:, 8 + frames : 9 + frames, at] = halo(after_ref[j], after_ref[4 + j])
    later = (scr[:, 9 : 9 + frames, :] * keep_ref[1][None]).reshape(rows, depth).astype(BF)
    earlier = (scr[:, 7 : 7 + frames, :] * keep_ref[0][None]).reshape(rows, depth).astype(BF)
    copies[0].wait()
    d_ref[...] = mm(later, row_ref[0], ((1,), (1,)))
    d_ref[...] += mm(dt, row_ref[1], ((1,), (1,)))[0:rows]
    d_ref[...] += mm(earlier, row_ref[2], ((1,), (1,)))
    copies[1].wait()
    normed = (s_ref[...] - stat_ref[0:1]) * stat_ref[1:2]
    d = d_ref[...] * silu_slope(normed * norm_ref[0:1] + norm_ref[1:2])
    d_ref[...] = d
    put_sums(d, normed, sums_ref)


def spatial_grad(d_ref, s_ref, stat_ref, norm_ref, sums_ref, ds_ref, sum_ref, total):
    sums = jnp.sum(sums_ref[...], axis=0)
    sum_ref[...] = sums
    inverse = stat_ref[1:2]
    normed = (s_ref[...] - stat_ref[0:1]) * inverse
    d = d_ref[...] - sums[1:2] * (1.0 / total) - normed * (sums[0:1] * (1.0 / total))
    ds_ref[...] = (norm_ref[0:1] * inverse * d).astype(BF)


def adjoint(ds_ref, w_ref, pad, dims):
    height, width, frames, depth = dims
    pad[...] = jnp.zeros(pad.shape, F32)

    for k in range(9):
        part = mm(ds_ref[...], w_ref[:, k * depth : (k + 1) * depth], ((1,), (0,)))
        at = (slice(k // 3, k // 3 + height), slice(k % 3, k % 3 + width))
        pad[at] = pad[at] + part.reshape(dims)


def input_body(
    ids_ref, d_ref, stat_ref, norm_ref, sums_ref, s_far, w_far,
    ds_ref, send_ref, kept_ref, sum_ref, pad, part, s_ref, w_ref, sems, *, dims, total
):
    height, width, frames, depth = dims
    copies = [started(s_far, s_ref, sems.at[0]), started(w_far, w_ref, sems.at[1])]
    copies[0].wait()
    spatial_grad(d_ref, s_ref, stat_ref, norm_ref, sums_ref, ds_ref, sum_ref, total)
    copies[1].wait()
    adjoint(ds_ref, w_ref, pad, dims)
    part[...] = pad[1 : height + 1, 1 : width + 1].reshape(part.shape)
    put_halves(ids_ref, part, send_ref, kept_ref)


def by_frame(source, out_ref, dims):
    height, width, frames, depth = dims
    pixels, own = height * width, out_ref.shape[1]
    for r in range(source.shape[0]):
        for f in range(frames):
            values = source[r, pl.ds(f, pixels, stride=frames), :]
            out_ref[f // own, f % own, :, r * LANES : (r + 1) * LANES] = values.astype(out_ref.dtype)


def last_body(ids_ref, ds_ref, g_ref, block_ref, w_far, *refs, dims):
    grads, blocks, (pad, part, block, grad_scr, block_scr, w_ref, sem) = refs[:4], refs[4:8], refs[8:]
    height, width, frames, depth = dims
    copy = started(w_far, w_ref, sem)
    block[0] = block_ref[...].astype(F32)
    by_frame(block, block_scr, dims)
    copy.wait()
    adjoint(ds_ref, w_ref, pad, dims)
    own = ids_ref[0]
    for r in range(part.shape[0]):
        columns = pad[1 : height + 1, 1 : width + 1, :, r * LANES : (r + 1) * LANES]
        part[r] = columns.reshape(part.shape[1:])
    part[own] = part[own] + g_ref[...]
    by_frame(part, grad_scr, dims)
    for j in range(4):
        grads[j][...] = grad_scr[ids_ref[j]]
        blocks[j][...] = block_scr[ids_ref[j]]


def finish_body(ids_ref, *refs):
    blocks, grads, (out_ref, grad_out_ref, block) = refs[:4], refs[4:8], refs[8:]
    own, height, width, depth = out_ref.shape
    for j, ref in enumerate(blocks):
        block[:, :, pl.ds(pl.multiple_of(ids_ref[j] * LANES, LANES), LANES)] = ref[...].astype(F32)
    for f in range(own):
        grad = sum(ref[f].astype(F32) for ref in grads)
        for h in range(height):
            at = slice(h * width, (h + 1) * width)
            out_ref[f, h] = block[f, at].astype(BF)
            grad_out_ref[f, h] = grad[at]


def weight_terms(act_ref, ds_ref, pad, acc, dims):
    height, width, frames, depth = dims
    rows = height * width * frames
    pad[...] = jnp.zeros(pad.shape, F32)
    pad[1 : height + 1, 1 : width + 1] = act_ref[...].astype(F32)[0:rows].reshape(dims)
    flipped = ds_ref[...].astype(F32).T.astype(BF)

    for k in range(9):
        i, j = k // 3, k % 3
        piece = pad[i : i + height, j : j + width].reshape(rows, depth).astype(BF)
        acc[:, k * depth : (k + 1) * depth] = mm(flipped, piece, ((1,), (0,)))


def put_shards(acc, places, out_ref, k):
    mid = acc.shape[0]
    half = mid // 2
    wide = k + LANES // 2
    for f in range(8):
        if f % 2 == 0:
            top = acc[0:half, k * f : k * f + wide]
            bottom = pltpu.roll(acc[half:mid, k * f : k * f + wide], LANES // 2, 1)
        else:
            start = k * f - LANES // 2
            top = pltpu.roll(acc[0:half, start : start + wide], k, 1)
            bottom = acc[half:mid, start : start + wide]
        fold(top, bottom, out_ref.at[places[f], 0:half], k)


def weight_plain_body(act_ref, ds_ref, out_ref, pad, acc, *, dims):
    weight_terms(act_ref, ds_ref, pad, acc, dims)
    out_ref[...] = acc[...].astype(BF)


def put_temporal(ids_ref, sources, out_ref, half):
    rows = out_ref.shape[1] - half
    per = half // rows
    for i, source in enumerate(sources):
        for tap in range(3):
            for part in range(2):
                block = tap * 8 + ids_ref[i] * 2 + part
                place = ids_ref[14 + block // 3]
                for j in range(per):
                    start = tap * 2 * half + part * half + j * rows
                    at = pl.multiple_of(((block % 3) * per + j) * LANES, LANES)
                    out_ref[place, half:, pl.ds(at, LANES)] = source[start : start + rows, :]


def weight_body(ids_ref, act_ref, ds_ref, t0, t1, t2, t3, out_ref, token_ref, pad, acc, *, dims):
    weight_terms(act_ref, ds_ref, pad, acc, dims)
    put_shards(acc, [ids_ref[14 + f] for f in range(8)], out_ref, acc.shape[1] // 8)
    put_temporal(ids_ref, (t0, t1, t2, t3), out_ref, acc.shape[0] // 2)
    token_ref[...] = jnp.zeros(token_ref.shape, F32)


def weight_first_body(
    ids_ref, act_ref, d_ref, stat_ref, norm_ref, sums_ref, mid_ref, out_1_ref, out_0_ref, t0, t1, t2, t3, s_far,
    ds_ref, flat_ref, out_ref, own_ref, ahead_ref, back_ref, sum_ref, s_ref, sem, pad, acc, *, dims, total
):
    started(s_far, s_ref, sem).wait()
    spatial_grad(d_ref, s_ref, stat_ref, norm_ref, sums_ref, ds_ref, sum_ref, total)
    flat_ref[...] = jnp.zeros(flat_ref.shape, F32)
    for i, ref in enumerate((sum_ref, mid_ref, out_0_ref, out_1_ref)):
        flat_ref[2 * i : 2 * i + 2, 0 : ref.shape[1]] = ref[...]
    weight_body(ids_ref, act_ref, ds_ref, t0, t1, t2, t3, out_ref, sum_ref, pad, acc, dims=dims)
    own_ref[...] = out_ref[0]
    ahead_ref[...] = out_ref[4]
    back_ref[...] = out_ref[5]


def norm_body(ids_ref, f0, f1, f2, f3, *refs):
    refs, flat_ref = refs[:-1], refs[-1]
    for j, ref in enumerate((f0, f1, f2, f3)):
        flat_ref[ids_ref[j]] = ref[...]
    count = flat_ref.shape[0]
    for which in range(2):
        old, new = refs[3 * which : 3 * which + 3], refs[6 + 3 * which : 9 + 3 * which]
        width = old[0].shape[-1] // count
        for u in range(2):
            row = 4 * which + 2 * u
            grad = jnp.concatenate([flat_ref[r, row : row + 2, 0:width] for r in range(count)], axis=1)
            values = adam_step(old[0][u], grad, old[1][u], old[2][u], RATE_NORM, 0.0)
            for ref, value in zip(new, values):
                ref[u] = value


def adam_step(param, gradient, moment_one, moment_two, rate, decay):
    first_new = BETA_ONE * moment_one + (1.0 - BETA_ONE) * gradient
    second_new = BETA_TWO * moment_two + (1.0 - BETA_TWO) * gradient * gradient
    fix_one = 1.0 - BETA_ONE**STEP
    fix_two = 1.0 - BETA_TWO**STEP
    update = first_new / fix_one / (jnp.sqrt(second_new / fix_two) + ADAM_EPS)
    return (param - rate * (update + decay * param), first_new, second_new)


def adam_into(grad, refs, outs, rows):
    new, first, second = adam_step(refs[0][0, rows], grad, refs[1][0, rows], refs[2][0, rows], RATE_WEIGHT, DECAY)
    outs[0][0, rows] = new
    outs[1][0, rows] = first
    outs[2][0, rows] = second
    outs[3][0, rows] = new.astype(BF)


def adam_body(*refs, grads):
    sources, refs = refs[:grads], refs[grads:]
    refs, outs = refs[:6], refs[-8:]
    half = refs[0].shape[1] // 2
    summed = sum(r[...].astype(F32) for r in sources)
    temporal = summed[half:]
    rows = temporal.shape[0]
    for i in range(temporal.shape[1] // LANES):
        piece = temporal[:, i * LANES : (i + 1) * LANES]
        adam_into(piece, refs[3:], outs[4:], slice(i * rows, (i + 1) * rows))
    spatial = summed[0:half]
    k = spatial.shape[1] // 2
    edge = k - LANES // 2
    adam_into(spatial[:, 0:k], refs, outs, slice(0, half))
    adam_into(pltpu.roll(spatial[:, edge:], k, 1)[:, 0:k], refs, outs, slice(half, 2 * half))


def adam_unit(u, sources, state, before, name, after=()):
    unit = [pl.BlockSpec((1,) + a.shape[1:], lambda i: (u, 0, 0)) for a in state]
    types = [F32, F32, F32, BF]
    outs = [shape(state[0].shape, t) for t in types] + [shape(state[3].shape, t) for t in types]
    before = list(before or ())
    whole = [pl.BlockSpec(a.shape, lambda i, n=a.ndim: (0,) * n) for a in sources]

    def kernel(*refs):
        adam_body(*refs[len(after) :], grads=len(sources))

    return pl.pallas_call(
        kernel,
        grid=(1,),
        out_shape=tuple(outs),
        in_specs=[pl.BlockSpec(memory_space=pl.ANY)] * len(after) + whole + unit + [pl.BlockSpec(memory_space=pl.ANY)] * len(before),
        out_specs=tuple([unit[0]] * 4 + [unit[3]] * 4),
        input_output_aliases={len(after) + len(sources) + 6 + i: i for i in range(len(before))},
        compiler_params=pltpu.CompilerParams(vmem_limit_bytes=40 * MIB),
        name=name,
    )(*after, *[in_hbm(a) for a in [*sources, *state]], *before)


def swap(parts, axis):
    return lax.all_to_all(parts, axis, 0, 0, tiled=True)


def from_all(value, axis):
    count = lax.axis_size(axis)
    return swap(jnp.broadcast_to(value[None], (count,) + value.shape), axis)


def across(value, bit):
    count = lax.axis_size("rep")
    return lax.ppermute(value, "rep", [(i, i ^ bit) for i in range(count)])


MASKS = (0, 2, 1, 3)


def traded(parts):
    return [part if mask == 0 else across(part, mask) for part, mask in zip(parts, MASKS)]


def from_group(value, after=None):
    distant = across(value, 2)
    beside = across(value, 1)
    if after is not None:
        distant = gate(distant, [after], "then")
    return value, distant, beside, across(distant, 1)


def neighbours(first, last):
    count = lax.axis_size("frames")
    before = lax.ppermute(last, "frames", [(i, i + 1) for i in range(count - 1)])
    after = lax.ppermute(first, "frames", [(i + 1, i) for i in range(count - 1)])
    return before, after


def along(step):
    return [(RING[i], RING[(i + step) % 8]) for i in range(8)]


def ring_gather(chunks):
    ahead, back = [[c] for c in chunks], [[c] for c in chunks]
    for step in range(4):
        for a, b in zip(ahead, back):
            a.append(lax.ppermute(a[-1], "frames", along(1)))
            if step < 3:
                b.append(lax.ppermute(b[-1], "frames", along(-1)))
    return [piece for a, b in zip(ahead, back) for piece in a + b[1:]]


def added(gots, parts, places, after, name):
    count = len(gots)

    def body(*refs):
        refs = refs[len(after) :]
        for got_ref, part_ref, out_ref in zip(refs[:count], refs[count : 2 * count], refs[2 * count :]):
            out_ref[...] = (got_ref[...].astype(F32) + part_ref[0].astype(F32)).astype(BF)

    flat = pl.BlockSpec(gots[0].shape, lambda g: (0, 0))
    part_specs = [pl.BlockSpec((1,) + gots[0].shape, lambda g, i=i: (i, 0, 0)) for i in places]
    return pl.pallas_call(
        body,
        grid=(1,),
        out_shape=[shape(g.shape, BF) for g in gots],
        in_specs=[ANY] * len(after) + [flat] * count + part_specs,
        out_specs=[flat] * count,
        name=name,
    )(*after, *[in_hbm(g) for g in gots], *[in_hbm(parts)] * count)


def ring_step(ahead, back):
    return lax.ppermute(ahead, "frames", along(1)), lax.ppermute(back, "frames", along(-1))


class RingSums:
    def __init__(self, parts, own, ahead, back, name):
        self.parts, self.own, self.ahead, self.back, self.name = parts, own, ahead, back, name
        self.step = 0

    def add(self, after=()):
        self.step += 1
        step, after, name = self.step, list(after), f"{self.name}_{self.step}"
        if step < 3:
            gots = ring_step(self.ahead, self.back)
            self.ahead, self.back = added(gots, self.parts, (4 - step, 5 + step), after, name)
        else:
            gots = [lax.ppermute(self.ahead, "frames", along(1))]
            (self.ahead,) = added(gots, self.parts, (4 - step,), after, name)
        return [self.ahead, self.back]

    def end(self):
        return [self.own, *ring_step(self.ahead, self.back)]


def reduced(send, kept, x):
    got = across(send, 1)
    away = lax.dynamic_index_in_dim(got, 1 - x, 0, False).astype(F32)
    away = away + lax.dynamic_index_in_dim(kept, 1 - x, 0, False)
    return got, kept, across(away.astype(BF), 2)


def ordered(t_grad, count):
    n_r, rows, cols = t_grad.shape
    return t_grad.reshape(n_r, 3, rows // 3, cols).transpose(1, 0, 2, 3).reshape(count, -1, cols)


def sum_over(parts, axis):
    return jnp.sum(swap(parts, axis).astype(F32), axis=0)


def on_device(
    frames_in, cotangent, lengths,
    spatial_weights, spatial_first, spatial_second,
    temporal_weights, temporal_first, temporal_second,
    mid_norm, mid_first, mid_second,
    out_norm, out_first, out_second,
):
    own_frames, height, width, depth = frames_in.shape
    n_f, n_r = lax.axis_size("frames"), lax.axis_size("rep")
    assert n_r == 4 and depth == n_r * LANES
    me = lax.axis_index("rep")
    frames = own_frames * n_r
    pixels = height * width
    rows = pixels * frames
    total = float(rows * n_f)
    dims = (height, width, frames, depth)
    units, k, mid = spatial_weights.shape
    cols = LANES
    everyone = ("frames", "rep")
    k_t = temporal_weights.shape[1]
    ring = can_ring(mid, k, k_t, n_f)
    spatial_flops = 2 * rows * 9 * depth * mid
    temporal_flops = 2 * rows * 3 * depth * mid
    pad = pltpu.VMEM((height + 2, width + 2, frames, depth), F32)
    flip = functools.partial(jnp.swapaxes, axis1=1, axis2=2)
    ids = [me, me ^ 2, me ^ 1, me ^ 3, me & 1, me >> 1]
    if ring:
        place = ring_place(lax.axis_index("frames"))
        in_order = jnp.stack(ids + [jnp.int32(f) for f in (*range(8), *range(8))]).astype(jnp.int32)
        ids += [ring_device(place + i) for i in (0, -1, -2, -3, -4, 1, 2, 3)]
        ids += [(ring_place(jnp.int32(f)) - place) % 8 for f in range(8)]
    ids = jnp.stack(ids).astype(jnp.int32)

    frame_ids = lax.axis_index("frames") * frames + jnp.arange(frames, dtype=jnp.int32)
    clip_ends = jnp.cumsum(lengths)
    starts = jnp.concatenate([jnp.zeros((1,), jnp.int32), clip_ends[:-1]])
    opening = jnp.any(frame_ids[:, None] == starts[None, :], axis=1)
    closing = jnp.any((frame_ids + 1)[:, None] == clip_ends[None, :], axis=1)
    keep = jnp.where(jnp.stack([opening, closing]), 0.0, 1.0).astype(F32)[:, :, None]

    act = lax.all_gather(frames_in, "rep", axis=0, tiled=True).transpose(1, 2, 0, 3).reshape(rows, depth)
    cot = cotangent.reshape(own_frames, pixels, n_r, cols).transpose(2, 0, 1, 3)
    cot = swap(cot, "rep").reshape(frames, pixels, cols).transpose(1, 0, 2).reshape(rows, cols)

    mid_own = lax.dynamic_slice_in_dim(mid_norm, me * mid, mid, axis=2)
    out_split = out_norm.reshape(units, 2, n_r, cols).transpose(0, 2, 1, 3)

    slots, temporal_w = [], []
    waiting = []

    def row_slices(order, held, after, handing):
        u = len(temporal_w)
        parts = [shape((3, mid, cols), BF)] * (n_r - 1)
        parts = run(
            unpack_temporal_body, [loaded(shape((3, mid, cols), BF)), *parts] + [shape(a.shape, BF) for a in handing],
            [order, *all_loaded(held), *all_loaded(handing)], f"unpack_{u}",
            [pltpu.VMEM((n_r, 3, 2, mid // 2, cols), BF)], scalars=1, after=after,
        )
        temporal_w.append(traded(parts[:n_r]))
        return parts[n_r:]

    if ring:
        wire = shape((mid // 2 + k_t * LANES // (2 * k), 2 * k), BF)
        chunks = [shape((n, 2 * k), BF) for n in (80, mid // 2 - 80, wire.shape[0] - mid // 2)]
        *chunks, wire_1 = run(
            pack_body, [*chunks, wire], [flip(spatial_weights), temporal_weights], "pack",
            [pltpu.VMEM(wire.shape, BF), pltpu.VMEM((mid, k + LANES // 2), F32)],
        )
        held = ring_gather(chunks)
        slots.append((ids, held))
        waiting = row_slices(ids, held, [act, cot], [wire_1])
    else:
        wire = flip(spatial_weights).astype(BF)
        temporal_low = temporal_weights.astype(BF)
        for u in range(units):
            held = lax.all_gather(wire[u], "frames", axis=0)
            slots.append((ids, [held.transpose(1, 0, 2).reshape(mid, n_f * k)]))
            shard = lax.all_gather(temporal_low[u], "frames", axis=0, tiled=True)
            shard = shard.reshape(3, n_r, mid, cols).transpose(1, 0, 2, 3)
            temporal_w.append(traded([lax.dynamic_index_in_dim(shard, ids[j], 0, False) for j in range(n_r)]))

    rows_16 = -(-rows // 16) * 16
    halo = shape((pixels, 1, mid), F32)
    column = shape((rows, cols), BF)
    s_shape, w_shape = shape((rows, mid), F32), shape((mid, n_f * k), BF)
    act_shape = shape((rows_16, depth), BF)
    win_shape, row_shape = shape((3, rows_16, mid), BF), shape((3, mid, depth), BF)
    s_scr, w_scr = pltpu.VMEM(s_shape.shape, F32), pltpu.VMEM(w_shape.shape, BF)
    sems = pltpu.SemaphoreType.DMA
    saved, spatial_w = [], []
    for u in range(units):
        order, held = slots[u]
        sources = [loaded(act)] if u == 0 else [*t_group, both, out_split[u - 1]]
        outs = [s_shape, halo, halo, shape((2, mid), F32), far(s_shape)]
        outs += [far(w_shape)] * ring + [far(act_shape)] * (u > 0)
        spatial, first, last, mom, s_far, *more = run(
            functools.partial(spatial_body, dims=dims, ring=ring, first=u == 0), outs,
            [order, *all_loaded(held), *sources], f"spatial_{u}",
            [pad, sems((3,))] + [w_scr] * ring + [pltpu.VMEM(act_shape.shape, BF)] * (u > 0),
            scalars=1, flops=spatial_flops, moved=8 * MIB,
            after=[temporal_w[0][0], cot, keep, mid_own, out_split] if u == 0 else (),
        )
        spatial_w.append(more.pop(0) if ring else held[0])
        if u > 0:
            act = more.pop(0)
        if ring and u + 1 < units:
            slots.append((in_order, [lax.all_gather(waiting[u], "frames", axis=0)]))
        if ring and u > 0:
            row_slices(*slots[u], [mom], ())
        mid_both = from_all(mom, "frames")
        before, after = neighbours(first, last)
        send, kept, stat, window, row_w = run(
            functools.partial(temporal_body, dims=dims),
            [shape((2, rows, cols), BF), shape((2, rows, cols), F32), shape((2, mid), F32), far(win_shape), far(row_shape)],
            [ids, spatial, mid_both, before, after, mid_own[u], keep, *temporal_w[u]], f"temporal_{u}",
            [pltpu.VMEM((pixels, frames + 16, mid), F32), pltpu.VMEM((rows_16, depth), F32),
             pltpu.VMEM(win_shape.shape, BF), pltpu.VMEM(row_shape.shape, BF), sems((2,))],
            scalars=1, flops=temporal_flops, moved=8 * MIB,
        )
        t, low, mom = run(
            total_body, [loaded(shape((rows, cols), F32)), column, shape((2, cols), F32)],
            [ids, *reduced(send, kept, me >> 1)], f"total_{u}", scalars=1, moved=3 * MIB,
        )
        both = from_all(mom, everyone).reshape(n_f, n_r, 2, cols)
        t_group = from_group(low, both if u + 1 < units else None)
        saved.append((act, s_far, stat, window, row_w, t, t_group, both))

    d_norms = [None] * units
    weight_parts = [None] * units
    token = None
    for u in reversed(range(units)):
        act, s_far, stat, window, row_w, t, t_group, both = saved[u]
        if u == units - 1:
            block, summed_grad, low, sums = run(
                top_body, [loaded(column), loaded(shape((rows, cols), F32)), column, shape((2, cols), F32)],
                [ids, loaded(t), both, out_split[u], loaded(saved[0][0]), loaded(cot)], "top", scalars=1, moved=3 * MIB,
            )
        else:
            low, sums = run(
                below_body, [column, shape((2, cols), F32)],
                [ids, *reduced(send, kept, me >> 1), loaded(t), both, out_split[u]], f"below_{u}", scalars=1, moved=3 * MIB,
                after=[token] if ring else (),
            )
        sums = from_all(sums, everyone).reshape(n_f, n_r, 2, cols)
        g_group = from_group(low, sums)
        edge = [shape((2 * n_r, pixels, 1, cols), F32)] * 2
        edges = neighbours(*run(functools.partial(edges_body, dims=dims), edge, [*g_group, *all_loaded(t_group)], f"edges_{u}"))
        dt, coef, out_sums = run(
            functools.partial(dt_body, total=total),
            [shape((rows_16, depth), BF), shape((n_r, 4, cols), F32), shape((2, cols), F32)],
            [ids, *g_group, *all_loaded(t_group), both, sums, out_split[u]], f"dt_{u}", scalars=1, moved=4 * MIB,
        )
        t_terms = run(
            temporal_grad_body, [loaded(shape((3 * mid, cols), BF))] + [shape((3 * mid, cols), BF)] * (n_r - 1), [ids, loaded(window), dt], f"temporal_grad_{u}",
            [pltpu.VMEM((mid, depth), F32)], scalars=1, flops=temporal_flops, moved=4 * MIB,
        )
        t_grad = traded(t_terms)
        d_mid, sums = run(
            functools.partial(middle_body, dims=dims), [shape((rows, mid), F32), shape((2, mid), F32)],
            [ids, dt, coef, *edges, keep, stat, mid_own[u], far(row_w), far(s_far)], f"middle_{u}",
            [pltpu.VMEM((pixels, frames + 16, depth), F32), pltpu.VMEM(row_shape.shape, BF), s_scr, sems((2,))],
            scalars=1, flops=temporal_flops, moved=8 * MIB, after=t_terms[:1],
        )
        sums = from_all(sums, "frames")
        ds_shape, sum_shape = shape((rows, mid), BF), shape((2, mid), F32)
        acc = pltpu.VMEM((mid, n_f * k), F32)
        grad_args = [d_mid, stat, mid_own[u], sums]
        if u > 0 or not ring:
            ds, send, kept, mid_sums = run(
                functools.partial(input_body, dims=dims, total=total),
                [ds_shape, shape((2, rows, cols), BF), shape((2, rows, cols), F32), sum_shape],
                [ids, *grad_args, far(s_far), far(spatial_w[u])], f"input_{u}",
                [pad, pltpu.VMEM((rows, depth), F32), s_scr, w_scr, sems((2,))],
                scalars=1, flops=spatial_flops, moved=8 * MIB, after=t_grad[1:],
            )
        if ring and u > 0:
            terms, token = run(
                functools.partial(weight_body, dims=dims), [loaded(shape((n_f,) + wire.shape, BF)), shape((8, LANES), F32)],
                [in_order, loaded(act), ds, *all_loaded(t_grad)], f"weight_{u}", [pad, acc],
                scalars=1, flops=spatial_flops, moved=8 * MIB,
            )
            weight_parts[u] = [lax.psum_scatter(terms, "frames", scatter_dimension=0, tiled=False)]
        elif ring:
            slab = wire
            ds, flat, *terms = run(
                functools.partial(weight_first_body, dims=dims, total=total),
                [ds_shape, shape((8, 512), F32), loaded(shape((n_f,) + slab.shape, BF)), loaded(slab), slab, slab],
                [ids, loaded(act), *grad_args, *d_norms[1], out_sums, *all_loaded(t_grad), far(s_far)], f"weight_{u}",
                [pltpu.VMEM((2, mid), F32), s_scr, sems(()), pad, acc],
                scalars=1, flops=spatial_flops, moved=8 * MIB, scale=1,
            )
            sums_0 = RingSums(*terms, f"sum_{u}")
        else:
            (s_grad,) = run(
                functools.partial(weight_plain_body, dims=dims), [w_shape], [loaded(act), ds],
                f"weight_{u}", [pad, acc], flops=spatial_flops, moved=8 * MIB,
            )
            s_grad = swap(s_grad.reshape(mid, n_f, k).transpose(1, 0, 2), "frames")
            t_rows = jnp.zeros((n_r,) + t_grad[0].shape, BF)
            for j in range(n_r):
                t_rows = lax.dynamic_update_index_in_dim(t_rows, t_grad[j], ids[j], 0)
            weight_parts[u] = (s_grad, swap(ordered(t_rows, n_f), "frames"))
        d_norms[u] = (mid_sums, out_sums) if u > 0 or not ring else None

    grad_part, block_part = (own_frames, pixels, depth), (own_frames, pixels, cols)
    ends = run(
        functools.partial(last_body, dims=dims), [loaded(shape(grad_part, BF))] + [shape(grad_part, BF)] * (n_r - 1) + [shape(block_part, BF)] * n_r,
        [ids, ds, loaded(summed_grad), loaded(block), far(spatial_w[0])], "last",
        [pad, pltpu.VMEM((n_r, rows, cols), F32), pltpu.VMEM((1, rows, cols), F32), pltpu.VMEM((n_r,) + grad_part, BF),
         pltpu.VMEM((n_r,) + block_part, BF), w_scr, sems(())],
        scalars=1, flops=spatial_flops, moved=8 * MIB, scale=1,
    )
    sent = ()
    if not ring:
        blocks, grads = traded(ends[n_r:]), traded(ends[:n_r])
    if ring:
        flats = from_group(flat)
        sums_0.add([ends[0], *flats[1:]])
        blocks, grads = traded(ends[n_r:]), traded(ends[:n_r])
        sums_0.add([*blocks[1:], *grads[1:]])
        sent = sums_0.add()
        weight_parts[0] = sums_0.end()
    block_out, input_grad = run(
        finish_body, [shape(frames_in.shape, BF), shape(frames_in.shape, F32)],
        [ids, *all_loaded(blocks + grads)], "finish", [pltpu.VMEM((own_frames, pixels, depth), F32)],
        scalars=1, moved=3 * MIB, after=sent,
    )
    if ring:
        norms = [mid_norm, mid_first, mid_second, out_norm, out_first, out_second]
        norms = run(
            norm_body, [shape(a.shape, F32) for a in norms], [ids, *flats, *norms], "norms",
            [pltpu.VMEM((n_r, 8, 512), F32)], scalars=1,
        )
    else:
        flat = jnp.concatenate([jnp.concatenate([m.reshape(-1), o.reshape(-1)]) for m, o in d_norms])
        flat = from_all(flat, "rep").reshape(n_r, units, -1)
        mid_grad = flat[:, :, : 2 * mid].reshape(n_r, units, 2, mid).transpose(1, 2, 0, 3)
        mid_grad = mid_grad.reshape(units, 2, n_r * mid)
        out_grad = flat[:, :, 2 * mid :].reshape(n_r, units, 2, cols).transpose(1, 2, 0, 3)
        out_grad = out_grad.reshape(units, 2, depth)
        norms = [*adam_step(mid_norm, mid_grad, mid_first, mid_second, RATE_NORM, 0.0)]
        norms += adam_step(out_norm, out_grad, out_first, out_second, RATE_NORM, 0.0)

    if ring:
        state = [flip(a) for a in (spatial_weights, spatial_first, spatial_second)]
        state += [temporal_weights, temporal_first, temporal_second]
        weights = None
        for u in reversed(range(units)):
            weights = adam_unit(u, weight_parts[u], state, weights, f"adam_{u}", sent if u > 0 else ())
        weights = [flip(a) for a in weights[:4]] + list(weights[4:])
    else:
        grads = [jnp.stack([jnp.sum(parts[i].astype(F32), axis=0) for parts in weight_parts]) for i in range(2)]
        news = adam_step(spatial_weights, flip(grads[0]), spatial_first, spatial_second, RATE_WEIGHT, DECAY)
        weights = [*news, news[0].astype(BF)]
        news = adam_step(temporal_weights, grads[1], temporal_first, temporal_second, RATE_WEIGHT, DECAY)
        weights += [*news, news[0].astype(BF)]
    return (block_out, input_grad, *weights, *norms)


def solution(mesh):
    by_frame = P(("frames", "rep"), None, None, None)
    by_block = P(None, "frames", "rep")
    placed = (by_frame, by_frame, P()) + (by_block,) * 6 + (P(),) * 6
    return jax.shard_map(
        on_device,
        mesh=mesh,
        in_specs=placed,
        out_specs=(by_frame, by_frame) + (by_block,) * 8 + (P(),) * 6,
        check_vma=False,
    )
```

time: 485 us -> 425 us (0.88)
  blocking collectives: 60.9 us -> 12 us
  Pallas kernels: 87 us -> 129 us
  waiting for transfers between devices: 154 us -> 120 us
  local copies, waits for them, and re-layouts: 57.1 us -> 34.9 us
  starting transfers between devices: 93.9 us -> 106 us
  other arithmetic: 9.04 us -> 0.81 us
    ppermute x28, waiting for transfers between devices: 91.1 us -> 26.3 us  [the longest x1 10.3 us: add(): gots = [lax.ppermute(self.ahead, 'frames', along(1))]]
    all_to_all x5 -> x1, blocking collectives: 60.9 us -> 12 us  [swap(): return lax.all_to_all(parts, axis, 0, 0, tiled=True)]
    pallas_call x24 -> x31, Pallas kernels: 82.5 us -> 120 us  [the longest x25 113 us: run(): pl.pallas_call(kernel, out_shape=tuple((result(o) for o in outs)), in_spe...]
    unnamed x208 -> x200, local copies, waits for them, and re-layouts: 48.9 us -> 26.9 us
    all_to_all x11 -> x8, waiting for transfers between devices: 23.9 us -> 41.6 us  [swap(): return lax.all_to_all(parts, axis, 0, 0, tiled=True)]
    ppermute x18 -> x39, waiting for transfers between devices: 29 us -> 45.6 us  [across(): return lax.ppermute(value, 'rep', [(i, i ^ bit) for i in range(count)])]
    ppermute x18 -> x39, starting transfers between devices: 8.22 us -> 23.5 us  [across(): return lax.ppermute(value, 'rep', [(i, i ^ bit) for i in range(count)])]
    all_to_all x11 -> x8, starting transfers between devices: 39.6 us -> 32.2 us  [swap(): return lax.all_to_all(parts, axis, 0, 0, tiled=True)]
  transfers between devices with their start and end apart: 66 -> 86, of which waited for: 31 -> 29; matrix products, arithmetic and copies ran while one was open for 3% -> 2% of each run, Pallas kernels for 7% -> 21%
where the time goes in v4:
time: 425 us; the launch traced here: 418 us
  Pallas kernels  129 us (30%)
  waiting for transfers between devices  120 us (28%)
  starting transfers between devices  106 us (25%)
  local copies, waits for them, and re-layouts  34.9 us (8%)
  between operations  15.5 us (4%)
  blocking collectives  12 us (3%)
    pallas_call x25, Pallas kernels, run(): pl.pallas_call(kernel, out_shape=tuple((result(o) for o in outs)), in_spe...  113 us
    ppermute x39, waiting for transfers between devices, across(): return lax.ppermute(value, 'rep', [(i, i ^ bit) for i in range(count)])  45.6 us
    all_to_all x8, waiting for transfers between devices, swap(): return lax.all_to_all(parts, axis, 0, 0, tiled=True)  41.6 us
    all_to_all x8, starting transfers between devices, swap(): return lax.all_to_all(parts, axis, 0, 0, tiled=True)  32.2 us
    unnamed x200, local copies, waits for them, and re-layouts  26.9 us
    ppermute x39, starting transfers between devices, across(): return lax.ppermute(value, 'rep', [(i, i ^ bit) for i in range(count)])  23.5 us
    ppermute x12, starting transfers between devices, ring_gather(): a.append(lax.ppermute(a[-1], 'frames', along(1)))  18.6 us
    all_to_all x1, blocking collectives, swap(): return lax.all_to_all(parts, axis, 0, 0, tiled=True)  12 us
  transfers between devices with their start and end apart: 86, of which 29 were waited for; matrix products, arithmetic and copies ran while one was open for 2% of the time, Pallas kernels for 21%

profile of v4, /device:TPU:0, one launch (start us, length us, event | category | flops | bytes accessed | tf_op | source)
XLA Modules:
  0.0 417.7 jit_solution(7030544792271861454)
XLA Ops:
  50.4 4.5 %collective-permute-done.17.refs_23_.refs_26_ = bf16[48,1152]{1,0:T(8,128)(2,1)} collective-permute-done((bf16[48,1152]{1,0:T(8,128)(2,1)}, bf16[48,1152]{1,0:T(8,128)(2,1)}, u32[]{:S(2)}, u32[]{:S(2)}) %collective-permute-start.17) | collective-permute-done | bytes 110624 | tf_op jit(solution)/shard_map/ppermute | solution.py:739
  62.3 11.4 %spatial_0.1 = (f32[1176,288]{1,0:T(8,128)S(1)}, f32[49,1,288]{2,1,0:T(1,128)S(1)}, f32[49,1,288]{2,1,0:T(1,128)S(1)}, f32[2,288]{1,0:T(2,128)S(1)}, f32[1176,288]{1,0:T(8,128)}, /*index=5*/bf16[288,4608]{1,0:T(8,128)(2,1)}) custom-call(bf16[3,288,128]{2,1,0:T(8,128)(2,1)S(1)} %copy-done.47, bf16[1176,128]{1,0:T(8,128)(2,1)S(1)} %bitcast.72, ...), custom_call_target="tpu_custom_call" | custom-call | flops 93640458240 | bytes 251658240 | tf_op jit(solution)/shard_map/spatial_0/pallas_call | solution.py:78
  75.7 5.9 %all-to-all-start.1 = ((f32[8,2,288]{2,1,0:T(2,128)}), f32[8,2,288]{2,1,0:T(2,128)S(1)}, u32[]{:S(2)}, u32[]{:S(2)}) async-start(f32[8,2,288]{2,1,0:T(2,128)} %broadcast_in_dim.26), calls=%async_computation.1 | async-start | bytes 49152 | tf_op jit(solution)/shard_map/all_to_all | solution.py:696
  81.6 3.9 collective-permute-start.21
  93.6 4.2 temporal_0.1
  101.7 7.5 %collective-permute-done.27.refs_3_ = bf16[1176,128]{1,0:T(8,128)(2,1)S(1)} collective-permute-done((bf16[1176,128]{1,0:T(8,128)(2,1)S(1)}, bf16[1176,128]{1,0:T(8,128)(2,1)S(1)}, u32[]{:S(2)}, u32[]{:S(2)}) %collective-permute-start.27) | collective-permute-done | bytes 301088 | tf_op jit(solution)/shard_map/ppermute | solution.py:706
  113.3 4.2 %all-to-all-start.2 = ((f32[32,2,128]{2,1,0:T(2,128)}), f32[32,2,128]{2,1,0:T(2,128)S(1)}, u32[]{:S(2)}, u32[]{:S(2)}) async-start(f32[32,2,128]{2,1,0:T(2,128)} %broadcast_in_dim.27), calls=%async_computation.2 | async-start | bytes 65536 | tf_op jit(solution)/shard_map/all_to_all | solution.py:696
  117.8 7.3 %all-to-all-done.2 = f32[32,2,128]{2,1,0:T(2,128)S(1)} async-done(((f32[32,2,128]{2,1,0:T(2,128)}), f32[32,2,128]{2,1,0:T(2,128)S(1)}, u32[]{:S(2)}, u32[]{:S(2)}) %all-to-all-start.2) | async-done | bytes 32800 | tf_op jit(solution)/shard_map/all_to_all | solution.py:696
  129.5 13.0 %spatial_1.1 = (f32[1176,288]{1,0:T(8,128)S(1)}, f32[49,1,288]{2,1,0:T(1,128)S(1)}, f32[49,1,288]{2,1,0:T(1,128)S(1)}, f32[2,288]{1,0:T(2,128)S(1)}, f32[1176,28...) custom-call(s32[22]{0:T(128)S(1)} %stack.113.refs_0_.refs_1_, bf16[8,192,1152]{2,1,0:T(8,128)(2,1)} %bitcast.90, ...), custom_call_target="tpu_custom_call" | custom-call | flops 93640458240 | bytes 251658240 | tf_op jit(solution)/shard_map/spatial_1/pallas_call | solution.py:78
  152.4 12.0 %all_to_all.45.refs_2_ = f32[8,2,288]{2,1,0:T(2,128)S(1)} all-to-all(f32[8,2,288]{2,1,0:T(2,128)S(1)} %broadcast_in_dim.28), channel_id=1, replica_groups=mesh['frames'=8,'rep'=4] {'frames'}, dimensions={0} | all-to-all | bytes 36864 | tf_op jit(solution)/shard_map/all_to_all | solution.py:696
  165.3 4.2 temporal_1.1
  173.2 7.7 %collective-permute-done.37.refs_3_ = bf16[1176,128]{1,0:T(8,128)(2,1)S(1)} collective-permute-done((bf16[1176,128]{1,0:T(8,128)(2,1)S(1)}, bf16[1176,128]{1,0:T(8,128)(2,1)S(1)}, u32[]{:S(2)}, u32[]{:S(2)}) %collective-permute-start.37) | collective-permute-done | bytes 301088 | tf_op jit(solution)/shard_map/ppermute | solution.py:706
  187.6 5.6 %all-to-all-done.4 = f32[32,2,128]{2,1,0:T(2,128)S(1)} async-done(((f32[32,2,128]{2,1,0:T(2,128)}), f32[32,2,128]{2,1,0:T(2,128)S(1)}, u32[]{:S(2)}, u32[]{:S(2)}) %all-to-all-start.4) | async-done | bytes 32800 | tf_op jit(solution)/shard_map/all_to_all | solution.py:696
  200.4 6.6 %all-to-all-done.5 = f32[32,2,128]{2,1,0:T(2,128)S(1)} async-done(((f32[32,2,128]{2,1,0:T(2,128)}), f32[32,2,128]{2,1,0:T(2,128)S(1)}, u32[]{:S(2)}, u32[]{:S(2)}) %all-to-all-start.5) | async-done | bytes 32800 | tf_op jit(solution)/shard_map/all_to_all | solution.py:696
  218.2 4.0 temporal_grad_1.1
  225.3 5.3 %middle_1.1 = (f32[1176,288]{1,0:T(8,128)S(1)}, f32[2,288]{1,0:T(2,128)S(1)}) custom-call(bf16[864,128]{1,0:T(8,128)(2,1)S(1)} %copy-done.60, s32[22]{0:T(128)S(1)} %stack.109.refs_2_.refs_5_.refs_0_.refs_1_.refs_3_, bf16[1184,512]{1,0:T(8,128)(2,1)S(1)} %get-tuple-element.169.refs_2_, f32[4,4,128]{2,1,0:T(4,128)S(1)} %get-tuple-element.174.refs_3_, ...), custom_call_target="tpu_custom_call" | custom-call | flops 31213486080 | bytes 251658240 | tf_op jit(solution)/shard_map/middle_1/pallas_call | solution.py:78
  232.5 5.1 %all-to-all-start.6 = ((f32[8,2,288]{2,1,0:T(2,128)}), f32[8,2,288]{2,1,0:T(2,128)S(1)}, u32[]{:S(2)}, u32[]{:S(2)}) async-start(f32[8,2,288]{2,1,0:T(2,128)} %broadcast_in_dim.31), calls=%async_computation.6 | async-start | bytes 49152 | tf_op jit(solution)/shard_map/all_to_all | solution.py:696
  237.6 6.5 %all-to-all-done.6.refs_7_ = f32[8,2,288]{2,1,0:T(2,128)S(1)} async-done(((f32[8,2,288]{2,1,0:T(2,128)}), f32[8,2,288]{2,1,0:T(2,128)S(1)}, u32[]{:S(2)}, u32[]{:S(2)}) %all-to-all-start.6) | async-done | bytes 18464 | tf_op jit(solution)/shard_map/all_to_all | solution.py:696
  245.6 9.0 %input_1.1 = (bf16[1176,288]{1,0:T(8,128)(2,1)S(1)}, bf16[2,1176,128]{2,1,0:T(8,128)(2,1)S(1)}, f32[2,1176,128]{2,1,0:T(8,128)S(1)}, f32[2,288]{1,0:T(2,128)S(1)}) custom-call(bf16[864,128]{1,0:T(8,128)(2,1)S(1)} %collective-permute-done.44.refs_0_.refs_4_, bf16[864,128]{1,0:T(8,128)(2,1)S(1)} %collective-permute-done.45.refs_1_.refs_5_, ...), custom_call_target="tpu_custom_call" | custom-call | flops 93640458240 | bytes 251658240 | tf_op jit(solution)/shard_map/input_1/pallas_call | solution.py:78
  257.4 7.3 %weight_1.1 = (bf16[8,192,1152]{2,1,0:T(8,128)(2,1)}, f32[8,128]{1,0:T(8,128)S(1)}) custom-call(s32[22]{0:T(128)S(1)} %stack.113.refs_0_.refs_1_, bf16[1184,512]{1,0:T(8,128)(2,1)} %get-tuple-element.152.refs_1_, bf16[1176,288]{1,0:T(8,128)(2,1)S(1)} %get-tuple-element.183.refs_2_, bf16[864,128]{1,0:T(8,128)(2,1)} %get-tuple-element.173.refs_0_.refs_3_, ...), custom_call_target="tpu_custom_call" | custom-call | flops 93640458240 | bytes 251658240 | tf_op jit(solution)/shard_map/weight_1/pallas_call | solution.py:78
  271.6 7.0 %all-to-all-done.7 = f32[32,2,128]{2,1,0:T(2,128)S(1)} async-done(((f32[32,2,128]{2,1,0:T(2,128)}), f32[32,2,128]{2,1,0:T(2,128)S(1)}, u32[]{:S(2)}, u32[]{:S(2)}) %all-to-all-start.7) | async-done | bytes 32800 | tf_op jit(solution)/shard_map/all_to_all | solution.py:696
  288.6 4.0 temporal_grad_0.1
  298.4 5.3 %middle_0.1 = (f32[1176,288]{1,0:T(8,128)S(1)}, f32[2,288]{1,0:T(2,128)S(1)}) custom-call(bf16[864,128]{1,0:T(8,128)(2,1)S(1)} %copy-done.55, s32[22]{0:T(128)S(1)} %stack.109.refs_2_.refs_5_.refs_0_.refs_1_.refs_3_, bf16[1184,512]{1,0:T(8,128)(2,1)S(1)} %get-tuple-element.190.refs_2_, f32[4,4,128]{2,1,0:T(4,128)S(1)} %get-tuple-element.192.refs_3_, ...), custom_call_target="tpu_custom_call" | custom-call | flops 31213486080 | bytes 251658240 | tf_op jit(solution)/shard_map/middle_0/pallas_call | solution.py:78
  305.6 5.9 %all-to-all-start.8 = ((f32[8,2,288]{2,1,0:T(2,128)}), f32[8,2,288]{2,1,0:T(2,128)S(1)}, u32[]{:S(2)}, u32[]{:S(2)}) async-start(f32[8,2,288]{2,1,0:T(2,128)} %broadcast_in_dim.33), calls=%async_computation.8 | async-start | bytes 49152 | tf_op jit(solution)/shard_map/all_to_all | solution.py:696
  311.5 7.1 %all-to-all-done.8.refs_5_ = f32[8,2,288]{2,1,0:T(2,128)S(1)} async-done(((f32[8,2,288]{2,1,0:T(2,128)}), f32[8,2,288]{2,1,0:T(2,128)S(1)}, u32[]{:S(2)}, u32[]{:S(2)}) %all-to-all-start.8) | async-done | bytes 18464 | tf_op jit(solution)/shard_map/all_to_all | solution.py:696
  320.1 9.4 %weight_0.1 = (bf16[1176,288]{1,0:T(8,128)(2,1)S(1)}, f32[8,512]{1,0:T(8,128)S(1)}, bf16[8,192,1152]{2,1,0:T(8,128)(2,1)}, bf16[192,1152]{1,0:T(8,128)(2,1)}, bf...) custom-call(s32[22]{0:T(128)S(1)} %stack.109.refs_2_.refs_5_.refs_0_.refs_1_.refs_3_, ...), custom_call_target="tpu_custom_call" | custom-call | flops 3121348608 | bytes 8388608 | tf_op jit(solution)/shard_map/weight_0/pallas_call | solution.py:78
  335.6 10.3 %last.1 = (bf16[6,49,512]{2,1,0:T(8,128)(2,1)}, bf16[6,49,512]{2,1,0:T(8,128)(2,1)S(1)}, bf16[6,49,512]{2,1,0:T(8,128)(2,1)S(1)}, bf16[6,49,512]{2,1,0:T(8,128)(...) custom-call(s32[22]{0:T(128)S(1)} %stack.109.refs_2_.refs_5_.refs_0_, ...), custom_call_target="tpu_custom_call" | custom-call | flops 3121348608 | bytes 8388608 | tf_op jit(solution)/shard_map/last/pallas_call | solution.py:78
  359.4 8.8 %collective-permute-done.62.refs_3_.refs_8_ = bf16[6,49,512]{2,1,0:T(8,128)(2,1)S(1)} collective-permute-done((bf16[6,49,512]{2,1,0:T(8,128)(2,1)S(1)}, bf16[6,49,512]{2,1,0:T(8,128)(2,1)S(1)}, u32[]{:S(2)}, u32[]{:S(2)}) %collective-permute-start.62) | collective-permute-done | bytes 301088 | tf_op jit(solution)/shard_map/ppermute | solution.py:706
  371.0 4.5 %collective-permute-done.71.refs_7_ = bf16[192,1152]{1,0:T(8,128)(2,1)S(1)} collective-permute-done((bf16[192,1152]{1,0:T(8,128)(2,1)}, bf16[192,1152]{1,0:T(8,128)(2,1)S(1)}, u32[]{:S(2)}, u32[]{:S(2)}) %collective-permute-start.71) | collective-permute-done | bytes 442400 | tf_op jit(solution)/shard_map/ppermute | solution.py:766
  380.9 10.3 %collective-permute-done.72.refs_0_ = bf16[192,1152]{1,0:T(8,128)(2,1)S(1)} collective-permute-done((bf16[192,1152]{1,0:T(8,128)(2,1)}, bf16[192,1152]{1,0:T(8,128)(2,1)S(1)}, u32[]{:S(2)}, u32[]{:S(2)}) %collective-permute-start.72) | collective-permute-done | bytes 442400 | tf_op jit(solution)/shard_map/ppermute | solution.py:781
  400.7 4.5 %adam_1.1 = (f32[2,288,576]{2,1,0:T(8,128)}, f32[2,288,576]{2,1,0:T(8,128)}, f32[2,288,576]{2,1,0:T(8,128)}, bf16[2,288,576]{2,1,0:T(8,128)(2,1)}, f32[2,432,128...) custom-call(bf16[192,1152]{1,0:T(8,128)(2,1)S(1)} %copy-done.3, ...), custom_call_target="tpu_custom_call" | custom-call | tf_op jit(solution)/shard_map/adam_1/pallas_call | solution.py:683
  406.3 4.4 %adam_0.1 = (f32[2,288,576]{2,1,0:T(8,128)}, f32[2,288,576]{2,1,0:T(8,128)}, f32[2,288,576]{2,1,0:T(8,128)}, bf16[2,288,576]{2,1,0:T(8,128)(2,1)}, f32[2,432,128...) custom-call(bf16[192,1152]{1,0:T(8,128)(2,1)} %get-tuple-element.228, ...), custom_call_target="tpu_custom_call", output_to_operand_aliasing={{0}: (9, {}), {1}: (10, {}), {2}: (11, {}), {3}: (12, {}), ... | custom-call | tf_op jit(solution)/shard_map/adam_0/pallas_call | solution.py:683
  (408 shorter events, 185.6 us)
Async XLA Ops:
  7.2 41.2 %all-gather.4.cloned.1.call-start = ((), (), s32[]{:S(2)}) async-start(), calls=%async_computation.10 | async-start | bytes 1720320 | tf_op jit(solution)/shard_map/all_gather | solution.py:845
  11.4 14.0 %collective-permute-start = (bf16[80,1152]{1,0:T(8,128)(2,1)S(1)}, bf16[80,1152]{1,0:T(8,128)(2,1)S(1)}, u32[]{:S(2)}, u32[]{:S(2)}) collective-permute-start(bf16[80,1152]{1,0:T(8,128)(2,1)S(1)} %get-tuple-element.134.refs_3_.refs_6_), channel_id=1, source_target_pairs={{0,8},{8,16},{16,24},{24,28},{28,20},{20,12},{12,4},{4,0},{1,9},{9... | collective-permute-start | bytes 552968 | tf_op jit(solution)/shard_map/ppermute | solution.py:739
  19.4 28.9 %all-to-all-start = ((bf16[4,6,49,128]{3,2,1,0:T(8,128)(2,1)}), bf16[4,6,49,128]{3,2,1,0:T(8,128)(2,1)S(1)}, u32[]{:S(2)}, u32[]{:S(2)}) async-start(bf16[4,6,49,128]{3,2,1,0:T(8,128)(2,1)} %bitcast.63), calls=%async_computation | async-start | bytes 688128 | tf_op jit(solution)/shard_map/all_to_all | solution.py:696
  22.9 104.8 %all-gather.6.cloned.1.call-start = ((), (), s32[]{:S(2)}) async-start(), calls=%async_computation.12 | async-start | bytes 3981312 | tf_op jit(solution)/shard_map/all_gather | solution.py:911
  42.2 12.7 %collective-permute-start.13 = (bf16[64,1152]{1,0:T(8,128)(2,1)S(1)}, bf16[64,1152]{1,0:T(8,128)(2,1)S(1)}, u32[]{:S(2)}, u32[]{:S(2)}) collective-permute-start(bf16[64,1152]{1,0:T(8,128)(2,1)S(1)} %collective-permute-done.12.refs_17_.refs_20_), channel_id=1, source_target_pairs={{0,4},{8,0},{16,8},{24,16},{28,24},{20,28},{12,20},{4,12},{1,5},{9... | collective-permute-start | bytes 442376 | tf_op jit(solution)/shard_map/ppermute | solution.py:741
  59.2 32.6 %collective-permute-start.23 = (bf16[3,288,128]{2,1,0:T(8,128)(2,1)S(1)}, bf16[3,288,128]{2,1,0:T(8,128)(2,1)S(1)}, u32[]{:S(2)}, u32[]{:S(2)}) collective-permute-start(bf16[3,288,128]{2,1,0:T(8,128)(2,1)S(1)} %get-tuple-element.143), channel_id=1, source_target_pairs={{0,2},{1,3},{2,0},{3,1},{4,6},{5,7},{6,4},{7,5},{8,10},{9,11},{10,... | collective-permute-start | bytes 663560 | tf_op jit(solution)/shard_map/ppermute | solution.py:706
  60.9 30.9 %collective-permute-start.24 = (bf16[3,288,128]{2,1,0:T(8,128)(2,1)S(1)}, bf16[3,288,128]{2,1,0:T(8,128)(2,1)S(1)}, u32[]{:S(2)}, u32[]{:S(2)}) collective-permute-start(bf16[3,288,128]{2,1,0:T(8,128)(2,1)S(1)} %get-tuple-element.144), channel_id=1, source_target_pairs={{0,1},{1,0},{2,3},{3,2},{4,5},{5,4},{6,7},{7,6},{8,9},{9,8},{10,11... | collective-permute-start | bytes 663560 | tf_op jit(solution)/shard_map/ppermute | solution.py:706
  60.9 30.9 %collective-permute-start.25 = (bf16[3,288,128]{2,1,0:T(8,128)(2,1)S(1)}, bf16[3,288,128]{2,1,0:T(8,128)(2,1)S(1)}, u32[]{:S(2)}, u32[]{:S(2)}) collective-permute-start(bf16[3,288,128]{2,1,0:T(8,128)(2,1)S(1)} %get-tuple-element.145), channel_id=1, source_target_pairs={{0,3},{1,2},{2,1},{3,0},{4,7},{5,6},{6,5},{7,4},{8,11},{9,10},{10,... | collective-permute-start | bytes 663560 | tf_op jit(solution)/shard_map/ppermute | solution.py:706
  75.7 12.8 %all-to-all-start.1 = ((f32[8,2,288]{2,1,0:T(2,128)}), f32[8,2,288]{2,1,0:T(2,128)S(1)}, u32[]{:S(2)}, u32[]{:S(2)}) async-start(f32[8,2,288]{2,1,0:T(2,128)} %broadcast_in_dim.26), calls=%async_computation.1 | async-start | bytes 49152 | tf_op jit(solution)/shard_map/all_to_all | solution.py:696
  110.9 14.2 %collective-permute-start.28 = (bf16[1176,128]{1,0:T(8,128)(2,1)S(1)}, bf16[1176,128]{1,0:T(8,128)(2,1)S(1)}, u32[]{:S(2)}, u32[]{:S(2)}) collective-permute-start(bf16[1176,128]{1,0:T(8,128)(2,1)S(1)} %get-tuple-element.150.refs_2_.refs_5_.refs_4_), channel_id=1, source_target_pairs={{0,2},{1,3},{2,0},{3,1},{4,6},{5,7},{6,4},{7,5},{8,10},{9,11},{10,... | collective-permute-start | bytes 903176 | tf_op jit(solution)/shard_map/ppermute | solution.py:706
  146.4 18.0 %collective-permute-start.33 = (bf16[3,288,128]{2,1,0:T(8,128)(2,1)S(1)}, bf16[3,288,128]{2,1,0:T(8,128)(2,1)S(1)}, u32[]{:S(2)}, u32[]{:S(2)}) collective-permute-start(bf16[3,288,128]{2,1,0:T(8,128)(2,1)S(1)} %get-tuple-element.158), channel_id=1, source_target_pairs={{0,2},{1,3},{2,0},{3,1},{4,6},{5,7},{6,4},{7,5},{8,10},{9,11},{10,... | collective-permute-start | bytes 663560 | tf_op jit(solution)/shard_map/ppermute | solution.py:706
  147.4 17.0 %collective-permute-start.34 = (bf16[3,288,128]{2,1,0:T(8,128)(2,1)S(1)}, bf16[3,288,128]{2,1,0:T(8,128)(2,1)S(1)}, u32[]{:S(2)}, u32[]{:S(2)}) collective-permute-start(bf16[3,288,128]{2,1,0:T(8,128)(2,1)S(1)} %get-tuple-element.159), channel_id=1, source_target_pairs={{0,1},{1,0},{2,3},{3,2},{4,5},{5,4},{6,7},{7,6},{8,9},{9,8},{10,11... | collective-permute-start | bytes 663560 | tf_op jit(solution)/shard_map/ppermute | solution.py:706
  147.4 17.0 %collective-permute-start.35 = (bf16[3,288,128]{2,1,0:T(8,128)(2,1)S(1)}, bf16[3,288,128]{2,1,0:T(8,128)(2,1)S(1)}, u32[]{:S(2)}, u32[]{:S(2)}) collective-permute-start(bf16[3,288,128]{2,1,0:T(8,128)(2,1)S(1)} %get-tuple-element.160), channel_id=1, source_target_pairs={{0,3},{1,2},{2,1},{3,0},{4,7},{5,6},{6,5},{7,4},{8,11},{9,10},{10,... | collective-permute-start | bytes 663560 | tf_op jit(solution)/shard_map/ppermute | solution.py:706
  148.5 15.8 %collective-permute-start.31 = (f32[49,1,288]{2,1,0:T(1,128)S(1)}, f32[49,1,288]{2,1,0:T(1,128)S(1)}, u32[]{:S(2)}, u32[]{:S(2)}) collective-permute-start(f32[49,1,288]{2,1,0:T(1,128)S(1)} %get-tuple-element.155), channel_id=1, source_target_pairs={{0,4},{4,8},{8,12},{12,16},{16,20},{20,24},{24,28},{1,5},{5,9},{9,... | collective-permute-start | bytes 169352 | tf_op jit(solution)/shard_map/ppermute | solution.py:726
  151.1 13.3 %collective-permute-start.32 = (f32[49,1,288]{2,1,0:T(1,128)S(1)}, f32[49,1,288]{2,1,0:T(1,128)S(1)}, u32[]{:S(2)}, u32[]{:S(2)}) collective-permute-start(f32[49,1,288]{2,1,0:T(1,128)S(1)} %get-tuple-element.156), channel_id=1, source_target_pairs={{4,0},{8,4},{12,8},{16,12},{20,16},{24,20},{28,24},{5,1},{9,5},{13... | collective-permute-start | bytes 169352 | tf_op jit(solution)/shard_map/ppermute | solution.py:727
  185.9 14.4 %collective-permute-start.41 = (bf16[1176,128]{1,0:T(8,128)(2,1)S(1)}, bf16[1176,128]{1,0:T(8,128)(2,1)S(1)}, u32[]{:S(2)}, u32[]{:S(2)}) collective-permute-start(bf16[1176,128]{1,0:T(8,128)(2,1)S(1)} %get-tuple-element.168.refs_5_.refs_4_), channel_id=1, source_target_pairs={{0,2},{1,3},{2,0},{3,1},{4,6},{5,7},{6,4},{7,5},{8,10},{9,11},{10,... | collective-permute-start | bytes 903176 | tf_op jit(solution)/shard_map/ppermute | solution.py:706
  222.2 15.4 %collective-permute-start.44 = (bf16[864,128]{1,0:T(8,128)(2,1)S(1)}, bf16[864,128]{1,0:T(8,128)(2,1)S(1)}, u32[]{:S(2)}, u32[]{:S(2)}) collective-permute-start(bf16[864,128]{1,0:T(8,128)(2,1)S(1)} %get-tuple-element.170), channel_id=1, source_target_pairs={{0,2},{1,3},{2,0},{3,1},{4,6},{5,7},{6,4},{7,5},{8,10},{9,11},{10,... | collective-permute-start | bytes 663560 | tf_op jit(solution)/shard_map/ppermute | solution.py:706
  222.9 14.7 %collective-permute-start.45 = (bf16[864,128]{1,0:T(8,128)(2,1)S(1)}, bf16[864,128]{1,0:T(8,128)(2,1)S(1)}, u32[]{:S(2)}, u32[]{:S(2)}) collective-permute-start(bf16[864,128]{1,0:T(8,128)(2,1)S(1)} %get-tuple-element.171), channel_id=1, source_target_pairs={{0,1},{1,0},{2,3},{3,2},{4,5},{5,4},{6,7},{7,6},{8,9},{9,8},{10,11... | collective-permute-start | bytes 663560 | tf_op jit(solution)/shard_map/ppermute | solution.py:706
  222.9 14.8 %collective-permute-start.46 = (bf16[864,128]{1,0:T(8,128)(2,1)S(1)}, bf16[864,128]{1,0:T(8,128)(2,1)S(1)}, u32[]{:S(2)}, u32[]{:S(2)}) collective-permute-start(bf16[864,128]{1,0:T(8,128)(2,1)S(1)} %get-tuple-element.172), channel_id=1, source_target_pairs={{0,3},{1,2},{2,1},{3,0},{4,7},{5,6},{6,5},{7,4},{8,11},{9,10},{10,... | collective-permute-start | bytes 663560 | tf_op jit(solution)/shard_map/ppermute | solution.py:706
  271.4 129.3 %reduce-scatter.2.cloned.1.call-start = ((), (), s32[]{:S(2)}) async-start(), calls=%async_computation.11 | async-start | bytes 3981312 | tf_op jit(solution)/shard_map/reduce_scatter | solution.py:986
  282.6 14.8 %collective-permute-start.54 = (f32[8,49,1,128]{3,2,1,0:T(1,128)S(1)}, f32[8,49,1,128]{3,2,1,0:T(1,128)S(1)}, u32[]{:S(2)}, u32[]{:S(2)}) collective-permute-start(f32[8,49,1,128]{3,2,1,0:T(1,128)S(1)} %get-tuple-element.193), channel_id=1, source_target_pairs={{0,4},{4,8},{8,12},{12,16},{16,20},{20,24},{24,28},{1,5},{5,9},{9,... | collective-permute-start | bytes 602120 | tf_op jit(solution)/shard_map/ppermute | solution.py:726
  292.7 18.8 %collective-permute-start.56 = (bf16[864,128]{1,0:T(8,128)(2,1)S(1)}, bf16[864,128]{1,0:T(8,128)(2,1)S(1)}, u32[]{:S(2)}, u32[]{:S(2)}) collective-permute-start(bf16[864,128]{1,0:T(8,128)(2,1)S(1)} %get-tuple-element.203), channel_id=1, source_target_pairs={{0,2},{1,3},{2,0},{3,1},{4,6},{5,7},{6,4},{7,5},{8,10},{9,11},{10,... | collective-permute-start | bytes 663560 | tf_op jit(solution)/shard_map/ppermute | solution.py:706
  293.3 18.2 %collective-permute-start.57 = (bf16[864,128]{1,0:T(8,128)(2,1)S(1)}, bf16[864,128]{1,0:T(8,128)(2,1)S(1)}, u32[]{:S(2)}, u32[]{:S(2)}) collective-permute-start(bf16[864,128]{1,0:T(8,128)(2,1)S(1)} %get-tuple-element.204), channel_id=1, source_target_pairs={{0,1},{1,0},{2,3},{3,2},{4,5},{5,4},{6,7},{7,6},{8,9},{9,8},{10,11... | collective-permute-start | bytes 663560 | tf_op jit(solution)/shard_map/ppermute | solution.py:706
  293.3 18.2 %collective-permute-start.58 = (bf16[864,128]{1,0:T(8,128)(2,1)S(1)}, bf16[864,128]{1,0:T(8,128)(2,1)S(1)}, u32[]{:S(2)}, u32[]{:S(2)}) collective-permute-start(bf16[864,128]{1,0:T(8,128)(2,1)S(1)} %get-tuple-element.205), channel_id=1, source_target_pairs={{0,3},{1,2},{2,1},{3,0},{4,7},{5,6},{6,5},{7,4},{8,11},{9,10},{10,... | collective-permute-start | bytes 663560 | tf_op jit(solution)/shard_map/ppermute | solution.py:706
  305.6 13.0 %all-to-all-start.8 = ((f32[8,2,288]{2,1,0:T(2,128)}), f32[8,2,288]{2,1,0:T(2,128)S(1)}, u32[]{:S(2)}, u32[]{:S(2)}) async-start(f32[8,2,288]{2,1,0:T(2,128)} %broadcast_in_dim.33), calls=%async_computation.8 | async-start | bytes 49152 | tf_op jit(solution)/shard_map/all_to_all | solution.py:696
  329.5 17.0 %collective-permute-start.68 = (bf16[192,1152]{1,0:T(8,128)(2,1)S(1)}, bf16[192,1152]{1,0:T(8,128)(2,1)S(1)}, u32[]{:S(2)}, u32[]{:S(2)}) collective-permute-start(bf16[192,1152]{1,0:T(8,128)(2,1)S(1)} %get-tuple-element.218), channel_id=1, source_target_pairs={{0,8},{8,16},{16,24},{24,28},{28,20},{20,12},{12,4},{4,0},{1,9},{9... | collective-permute-start | bytes 1327112 | tf_op jit(solution)/shard_map/ppermute | solution.py:766
  329.8 16.8 %collective-permute-start.69 = (bf16[192,1152]{1,0:T(8,128)(2,1)S(1)}, bf16[192,1152]{1,0:T(8,128)(2,1)S(1)}, u32[]{:S(2)}, u32[]{:S(2)}) collective-permute-start(bf16[192,1152]{1,0:T(8,128)(2,1)S(1)} %get-tuple-element.219), channel_id=1, source_target_pairs={{0,4},{8,0},{16,8},{24,16},{28,24},{20,28},{12,20},{4,12},{1,5},{9... | collective-permute-start | bytes 1327112 | tf_op jit(solution)/shard_map/ppermute | solution.py:766
  332.3 14.2 %collective-permute-start.66 = (f32[8,512]{1,0:T(8,128)S(1)}, f32[8,512]{1,0:T(8,128)S(1)}, u32[]{:S(2)}, u32[]{:S(2)}) collective-permute-start(f32[8,512]{1,0:T(8,128)S(1)} %get-tuple-element.217.refs_1_), channel_id=1, source_target_pairs={{0,1},{1,0},{2,3},{3,2},{4,5},{5,4},{6,7},{7,6},{8,9},{9,8},{10,11... | collective-permute-start | bytes 49160 | tf_op jit(solution)/shard_map/ppermute | solution.py:706
  349.9 21.2 %collective-permute-start.70 = (bf16[192,1152]{1,0:T(8,128)(2,1)}, bf16[192,1152]{1,0:T(8,128)(2,1)S(1)}, u32[]{:S(2)}, u32[]{:S(2)}) collective-permute-start(bf16[192,1152]{1,0:T(8,128)(2,1)} %get-tuple-element.221), channel_id=1, source_target_pairs={{0,8},{8,16},{16,24},{24,28},{28,20},{20,12},{12,4},{4,0},{1,9},{9... | collective-permute-start | bytes 1327112 | tf_op jit(solution)/shard_map/ppermute | solution.py:766
  350.0 25.5 %collective-permute-start.71 = (bf16[192,1152]{1,0:T(8,128)(2,1)}, bf16[192,1152]{1,0:T(8,128)(2,1)S(1)}, u32[]{:S(2)}, u32[]{:S(2)}) collective-permute-start(bf16[192,1152]{1,0:T(8,128)(2,1)} %get-tuple-element.222), channel_id=1, source_target_pairs={{0,4},{8,0},{16,8},{24,16},{28,24},{20,28},{12,20},{4,12},{1,5},{9... | collective-permute-start | bytes 1327112 | tf_op jit(solution)/shard_map/ppermute | solution.py:766
  357.3 13.7 %collective-permute-start.64 = (bf16[6,49,512]{2,1,0:T(8,128)(2,1)S(1)}, bf16[6,49,512]{2,1,0:T(8,128)(2,1)S(1)}, u32[]{:S(2)}, u32[]{:S(2)}) collective-permute-start(bf16[6,49,512]{2,1,0:T(8,128)(2,1)S(1)} %get-tuple-element.215), channel_id=1, source_target_pairs={{0,3},{1,2},{2,1},{3,0},{4,7},{5,6},{6,5},{7,4},{8,11},{9,10},{10,... | collective-permute-start | bytes 903176 | tf_op jit(solution)/shard_map/ppermute | solution.py:706
  380.8 24.4 %collective-permute-start.74 = (bf16[192,1152]{1,0:T(8,128)(2,1)}, bf16[192,1152]{1,0:T(8,128)(2,1)S(1)}, u32[]{:S(2)}, u32[]{:S(2)}) collective-permute-start(bf16[192,1152]{1,0:T(8,128)(2,1)} %get-tuple-element.224.refs_1_), channel_id=1, source_target_pairs={{0,4},{8,0},{16,8},{24,16},{28,24},{20,28},{12,20},{4,12},{1,5},{9... | collective-permute-start | bytes 1327112 | tf_op jit(solution)/shard_map/ppermute | solution.py:766
  (154 other events, 1376.4 us)
Sparse Core Ops, SparseCore 0:
  9.6 24.5 all-gather.3
  59.3 67.9 all-gather.5
  279.7 98.2 reduce-scatter.1
